TPU v7x, 128 devices: a whole 4x4x4 slice. The times are simulated.
128 devices in a mesh: aux: 32 (over y, z, core), grp: 4 (over x).
Axes of the slice: x: 4, y: 4, z: 4, core: 2. Of those that a mesh axis runs over, the one named last changes fastest.
Arguments:
- ao_blocks: bfloat16 [1024, 32, 32, 384], P(('aux', 'grp')), may hold values from -6 to 6
- blocks: int32 [1024, 4], P(('aux', 'grp')), may hold values from 0 to 12288, as said below
- occ_coeff: bfloat16 [2, 4352], replicated, may hold values from -0.75 to 0.75
- vir_coeff: bfloat16 [4352, 4096], P('grp'), may hold values from -0.09375 to 0.09375
- occ_energy: float32 [2], replicated, may hold values from -1.5 to -0.3
- vir_energy: float32 [4096], replicated, may hold values from 0.1 to 6
- owner: int32 [128], replicated, may hold values from 0 to 127, each once
Outputs:
- density_half: bfloat16 [2, 4352, 12288], P(None, 'grp', 'aux')
Inputs may be any that keep to these rules, and one draw needn't show every extreme that they name: `blocks`: row k belongs to device k // 8 in mesh order (aux slowest): its nu shell block lies in that device's AO quarter (q * 34 to (q + 1) * 34 - 1), its range lo <= hi lies inside that device's aux slice s * 384 to (s + 1) * 384; slots with lo == hi are empty and follow the live ones; every device has 1 to 8 live slots, its first one covers the whole slice, and some device has 8. `owner`: each device index once.
All inputs are finite; a program needn't handle non-finite values.
Results may differ from a plain program's by a relative error of at most 0.015.
Values may be sent and summed in bfloat16 or wider, within the bound.
No kernel may reach another device: no remote copies, remote signals or barrier semaphores. Data moves between devices by JAX's collectives and lax.ppermute only.
A program may use at most 128 MiB of HBM per device.

v0:
```python
import jax
import jax.numpy as jnp
from jax import lax
from jax.sharding import PartitionSpec as P


def body(ao_blocks, blocks, occ_coeff, vir_coeff, occ_energy, vir_energy, owner):
    aux_place = lax.axis_index("aux")
    grp_place = lax.axis_index("grp")
    aux_count = lax.axis_size("aux")
    grp_count = lax.axis_size("grp")
    devices = aux_count * grp_count
    occ_count = occ_coeff.shape[0]
    virtuals = vir_coeff.shape[1]
    shell = ao_blocks.shape[1]
    width = ao_blocks.shape[3]
    quarter_shells = vir_coeff.shape[0] // shell
    block_rows = occ_count * virtuals // devices
    positions = aux_place * width + jnp.arange(width, dtype=jnp.int32)
    occ_shells = occ_coeff.reshape(occ_count, occ_coeff.shape[1] // shell, shell)
    occ_rows = jnp.take(occ_shells, blocks[:, 0], axis=1)
    vir_shells = vir_coeff.reshape(quarter_shells, shell, virtuals)
    vir_rows = jnp.take(vir_shells, blocks[:, 1] - grp_place * quarter_shells, axis=0)
    half_tiles = jnp.einsum(
        "ikm,kmnp->iknp", occ_rows, ao_blocks, preferred_element_type=jnp.float32
    )
    inside = (
        (positions[None, :] >= blocks[:, 2:3]) & (positions[None, :] < blocks[:, 3:4])
    ).astype(jnp.float32)
    half_tiles = (half_tiles * inside[None, :, None, :]).astype(jnp.bfloat16)
    partial_value = jnp.einsum(
        "kna,iknp->iap", vir_rows, half_tiles, preferred_element_type=jnp.float32
    )
    partial_blocks = partial_value.astype(jnp.bfloat16).reshape(devices, block_rows, width)
    device_ids = jnp.arange(devices, dtype=jnp.int32)
    matches = (owner[None, :] == device_ids[:, None]).astype(jnp.int32)
    slot_block = jnp.sum(matches * device_ids[None, :], axis=1)
    self_id = aux_place * grp_count + grp_place
    outgoing = jnp.take(partial_blocks, slot_block, axis=0).reshape(devices * block_rows, width)
    arrived = lax.all_to_all(outgoing, "aux", split_axis=0, concat_axis=1, tiled=True)
    own_rows = lax.psum_scatter(
        arrived.astype(jnp.float32).astype(jnp.bfloat16), "grp", scatter_dimension=0, tiled=True
    )
    pair_energy = (occ_energy[:, None] - vir_energy[None, :]).reshape(occ_count * virtuals)

    def block_energy(block_id):
        return lax.dynamic_slice_in_dim(pair_energy, block_id * block_rows, block_rows)

    own_energy = block_energy(slot_block[self_id])
    members = lax.dynamic_slice_in_dim(slot_block, aux_place * grp_count, grp_count)
    panel_energy = jax.vmap(block_energy)(members).reshape(grp_count * block_rows)
    piece = lax.all_gather(own_rows, "grp", axis=0, tiled=True)
    scores = lax.dot_general(
        own_rows, piece, (((1,), (1,)), ((), ())), preferred_element_type=jnp.float32
    )
    amplitude = (scores / (own_energy[:, None] + panel_energy[None, :])).astype(jnp.bfloat16)
    density_rows = jnp.dot(amplitude, piece, preferred_element_type=jnp.float32)
    density_rows = density_rows.astype(jnp.bfloat16)
    group_rows = lax.all_gather(density_rows, "grp", axis=0, tiled=True)
    returned = lax.all_to_all(group_rows, "aux", split_axis=1, concat_axis=0, tiled=True)
    density = jnp.take(returned.reshape(devices, block_rows, width), owner, axis=0)
    density = density.reshape(occ_count, virtuals, width)
    result = jnp.einsum("na,iap->inp", vir_coeff, density, preferred_element_type=jnp.float32)
    return result.astype(jnp.bfloat16)


def solution(mesh):
    return jax.shard_map(
        body,
        mesh=mesh,
        in_specs=(
            P(("aux", "grp"), None, None, None),
            P(("aux", "grp"), None),
            P(),
            P("grp", None),
            P(),
            P(),
            P(),
        ),
        out_specs=P(None, "grp", "aux"),
        check_vma=False,
    )
```

profile of v0, /device:TPU:0, one launch (start us, length us, event | category | flops | bytes accessed | tf_op | source)
XLA Modules:
  0.0 472.6 jit_solution(13761138246017448003)
XLA Ops:
  6.5 0.8 select_reduce_fusion
  7.3 0.8 fusion.34
  8.1 0.8 and_bitcast_fusion
  8.9 0.8 reshape.108
  9.8 4.2 gather_fusion.1
  14.7 4.8 %fusion.21 = bf16[2,8,32,384]{3,0,2,1:T(2,128)(2,1)S(1)} fusion(bf16[8,32,32,384]{3,2,1,0:T(8,128)(2,1)} %param.9, f32[8,384]{1,0:T(8,128)S(1)} %and_convert_fusion, bf16[8,2,32]{2,1,0:T(2,128)(2,1)S(1)} %gather_fusion, pred[8]{0:T(512)(128)(4,1)S(1)} %get-tuple-element.24), kind=kOutput, calls=%fused_computation.25 | convolution fusion | flops 12976640 | bytes 6697992 | tf_op jit(solution)/shard_map/ikm,kmnp->iknp/dot_general | solution.py:24
  19.5 4.5 fusion.4
  24.0 8.6 %copy.22 = bf16[2,4096,384]{2,1,0:T(8,128)(2,1)} copy(bf16[2,4096,384]{1,2,0:T(8,128)(2,1)} %fusion.4) | data formatting | bytes 12582912 | tf_op jit(solution)/shard_map/convert_element_type | solution.py:34
  32.7 6.8 %gather_fusion.2 = bf16[128,64,384]{2,1,0:T(8,128)(2,1)} fusion(bf16[128,64,384]{2,1,0:T(8,128)(2,1)} %bitcast.72, s32[1024]{0:T(1024)S(1)} %pad_clamp_fusion.1), kind=kCustom, calls=%fused_computation.clone | custom fusion | bytes 12583424 | tf_op jit(solution)/shard_map/jit(_take)/gather | solution.py:39
  39.5 6.2 %broadcast_select_fusion.1 = bf16[128,64,384]{2,1,0:T(8,128)(2,1)} fusion(bf16[128,64,384]{2,1,0:T(8,128)(2,1)} %gather_fusion.2, pred[128]{0:T(512)(128)(4,1)S(1)} %compare_and_fusion.1), kind=kLoop, calls=%fused_computation.14 | loop fusion | flops 3145728 | bytes 12583040 | tf_op jit(solution)/shard_map/jit(_take)/select_n | solution.py:39
  45.7 8.6 %copy.23 = bf16[32,256,384]{1,2,0:T(8,128)(2,1)} copy(bf16[32,256,384]{2,1,0:T(8,128)(2,1)} %bitcast.73) | data formatting | bytes 12582912 | tf_op jit(solution)/shard_map/all_to_all | solution.py:40
  54.4 81.5 %all_to_all.35 = bf16[32,256,384]{1,2,0:T(8,128)(2,1)} all-to-all(bf16[32,256,384]{1,2,0:T(8,128)(2,1)} %copy.23), channel_id=1, replica_groups=mesh['aux'=32,'grp'=4] {'aux'}, dimensions={0} | all-to-all | bytes 12582912 | tf_op jit(solution)/shard_map/all_to_all | solution.py:40
  135.9 8.7 %copy.28 = bf16[256,12288]{1,0:T(8,128)(2,1)} copy(bf16[256,12288]{0,1:T(8,128)(2,1)} %bitcast.74) | data formatting | bytes 12582912
  144.7 62.1 %reduce-scatter.4.cloned.1.call-done = bf16[64,12288]{1,0:T(8,128)(2,1)} async-done(((bf16[256,12288]{1,0:T(8,128)(2,1)}), bf16[64,12288]{1,0:T(8,128)(2,1)}) %reduce-scatter.4.cloned.1.call-update) | async-done | bytes 1572880
  207.1 5.7 %while.1 = (s32[]{:T(128)}, f32[8192]{0:T(1024)S(1)}, s32[4,1]{0,1:T(1,128)S(1)}, f32[4,64]{1,0:T(4,128)S(1)}, s32[]{:T(128)}, /*index=5*/s32[]{:T(128)}) while((s32[]{:T(128)}, f32[8192]{0:T(1024)S(1)}, s32[4,1]{0,1:T(1,128)S(1)}, f32[4,64]{1,0:T(4,128)S(1)}, s32[]{:T(128)}, /*index=5*/s32[]{:T(128)}) %tuple.30), condition=%wide.while_cond, body=%wide.while_body.sunk | while | flops 2 | bytes 1121 | solution.py:47
  207.1 0.6 constant_dynamic-slice_fusion.2
  207.7 0.7 dynamic-slice_bitcast_fusion.2
  208.5 0.6 constant_dynamic-slice_fusion.2
  209.1 0.7 dynamic-slice_bitcast_fusion.2
  209.9 0.6 constant_dynamic-slice_fusion.2
  210.6 0.7 dynamic-slice_bitcast_fusion.2
  211.3 0.6 constant_dynamic-slice_fusion.2
  212.0 0.7 dynamic-slice_bitcast_fusion.2
  214.2 59.7 %all-gather.3.cloned.1.call-done = bf16[256,12288]{1,0:T(8,128)(2,1)} async-done(((bf16[64,12288]{1,0:T(8,128)(2,1)}), bf16[256,12288]{1,0:T(8,128)(2,1)}) %all-gather.3.cloned.1.call-update) | async-done | bytes 6291472 | tf_op jit(solution)/shard_map/all_gather | solution.py:52
  273.9 10.7 %convolution_convert_fusion = bf16[64,12288]{1,0:T(8,128)(2,1)} fusion(bf16[256,12288]{1,0:T(8,128)(2,1)} %all-gather.3.cloned.1.call-done, bf16[64,12288]{1,0:T(8,128)(2,1)} %reduce-scatter.4.cloned.1.call-done, f32[256]{0:T(256)S(1)} %add.70, f32[64]{0:T(128)S(1)} %dynamic_slice.10), kind=kOutput, calls=%fused_computation.6 | convolution fusion | flops 806141952 | bytes 9438464 | tf_op jit(solution)/shard_map/dot_general | solution.py:57
  284.6 66.5 %all-gather.5.cloned.1.call-done = bf16[256,12288]{1,0:T(8,128)(2,1)} async-done(((bf16[64,12288]{1,0:T(8,128)(2,1)}), bf16[256,12288]{1,0:T(8,128)(2,1)}) %all-gather.5.cloned.1.call-update) | async-done | bytes 6291472 | tf_op jit(solution)/shard_map/all_gather | solution.py:59
  351.1 6.5 %copy.43 = bf16[32,32,8,384]{3,2,0,1:T(8,128)(2,1)} copy(bf16[32,32,8,384]{3,2,1,0:T(8,128)(2,1)} %bitcast.75) | data formatting | bytes 12582912 | tf_op jit(solution)/shard_map/all_to_all | solution.py:60
  357.6 7.7 %all-to-all-start.1 = ((bf16[256,32,384]{2,0,1:T(8,128)(2,1)}), bf16[256,32,384]{2,0,1:T(8,128)(2,1)}, u32[]{:S(2)}, u32[]{:S(2)}) async-start(bf16[256,32,384]{2,0,1:T(8,128)(2,1)} %bitcast.71), calls=%async_computation.1 | async-start | bytes 12582912 | tf_op jit(solution)/shard_map/all_to_all | solution.py:60
  365.3 79.8 %all-to-all-done.1 = bf16[256,32,384]{2,0,1:T(8,128)(2,1)} async-done(((bf16[256,32,384]{2,0,1:T(8,128)(2,1)}), bf16[256,32,384]{2,0,1:T(8,128)(2,1)}, u32[]{:S(2)}, u32[]{:S(2)}) %all-to-all-start.1) | async-done | bytes 6291488 | tf_op jit(solution)/shard_map/all_to_all | solution.py:60
  445.1 6.8 %gather_fusion.3 = bf16[128,64,384]{2,1,0:T(8,128)(2,1)} fusion(bf16[128,64,384]{2,1,0:T(8,128)(2,1)} %bitcast.22, s32[1024]{0:T(1024)S(1)} %pad_clamp_fusion), kind=kCustom, calls=%fused_computation.1.clone | custom fusion | bytes 12583424 | tf_op jit(solution)/shard_map/jit(_take)/gather | solution.py:61
  452.0 3.6 broadcast_select_fusion
  455.6 10.5 %fusion.8 = bf16[2,1088,384]{2,1,0:T(8,128)(2,1)} fusion(bf16[2,4096,384]{2,1,0:T(8,128)(2,1)S(1)} %bitcast.76, bf16[1088,4096]{1,0:T(8,128)(2,1)} %param.12), kind=kOutput, calls=%fused_computation.17 | convolution fusion | flops 6845939712 | bytes 16875520 | tf_op jit(solution)/shard_map/na,iap->inp/dot_general | solution.py:63
  (35 shorter events, 1.9 us)
Async XLA Ops:
  6.5 200.3 %reduce-scatter.4.cloned.1.call-start = ((), (), s32[]{:S(2)}) async-start(), calls=%async_computation.5 | async-start | bytes 7864320
  144.6 62.3 %copy-start = (f32[4096]{0:T(1024)S(1)}, f32[4096]{0:T(1024)}, u32[]{:S(2)}) copy-start(f32[4096]{0:T(1024)} %param.14) | copy-start | bytes 49156
  144.6 62.3 %copy-start.1 = (f32[2]{0:T(128)S(1)}, f32[2]{0:T(128)}, u32[]{:S(2)}) copy-start(f32[2]{0:T(128)} %param.13) | copy-start | bytes 28
  144.6 129.3 %all-gather.3.cloned.1.call-start = ((), (), s32[]{:S(2)}) async-start(), calls=%async_computation.3 | async-start | bytes 7864320 | tf_op jit(solution)/shard_map/all_gather | solution.py:52
  206.8 144.2 %all-gather.5.cloned.1.call-start = ((), (), s32[]{:S(2)}) async-start(), calls=%async_computation.4 | async-start | bytes 7864320 | tf_op jit(solution)/shard_map/all_gather | solution.py:59
  357.6 7.7 %copy-start.2 = (s32[128]{0:T(128)S(1)}, s32[128]{0:T(128)}, u32[]{:S(2)}) copy-start(s32[128]{0:T(128)} %param.15) | copy-start | bytes 1540
  357.6 87.5 %all-to-all-start.1 = ((bf16[256,32,384]{2,0,1:T(8,128)(2,1)}), bf16[256,32,384]{2,0,1:T(8,128)(2,1)}, u32[]{:S(2)}, u32[]{:S(2)}) async-start(bf16[256,32,384]{2,0,1:T(8,128)(2,1)} %bitcast.71), calls=%async_computation.1 | async-start | bytes 12582912 | tf_op jit(solution)/shard_map/all_to_all | solution.py:60
Sparse Core Ops, SparseCore 0:
  144.7 62.0 reduce-scatter.3
  208.5 65.3 all-gather.2
  284.7 66.3 all-gather.4
where the time goes:
time: 481 us; the launch traced here: 473 us
  waiting for transfers between devices  268 us (56%)
  blocking collectives  81.5 us (17%)
  local copies, waits for them, and re-layouts  58.3 us (12%)
  matrix products  30.5 us (6%)
  between operations  13.9 us (3%)
  other arithmetic  12.4 us (3%)
  starting transfers between devices  7.77 us (2%)
    all_to_all x1, blocking collectives, body(): lax.all_to_all(outgoing, 'aux', split_axis=0, concat_axis=1, tiled=True)  81.5 us
    all_to_all x1, waiting for transfers between devices, body(): lax.all_to_all(group_rows, 'aux', split_axis=1, concat_axis=0, tiled=True)  79.8 us
    all_gather x1, waiting for transfers between devices, body(): group_rows = lax.all_gather(density_rows, 'grp', axis=0, tiled=True)  66.5 us
    unnamed x4, waiting for transfers between devices  62.2 us
    all_gather x1, waiting for transfers between devices, body(): piece = lax.all_gather(own_rows, 'grp', axis=0, tiled=True)  59.7 us
    dot_general x1, matrix products, body(): density_rows = jnp.dot(amplitude, piece, preferred_element_type=jnp.float32)  10.7 us
    dot_general x1, matrix products, body(): jnp.einsum('na,iap->inp', vir_coeff, density, preferred_element_type=jnp....  10.5 us
  transfers between devices with their start and end apart: 4, of which 4 were waited for; matrix products, arithmetic and copies ran while one was open for 1% of the time, Pallas kernels for 0%

commit v1 on v0

v1 whole, which is shorter than its diff:
```python
import functools

import jax
import jax.numpy as jnp
from jax import lax
from jax.experimental import pallas as pl
from jax.experimental.pallas import tpu as pltpu
from jax.sharding import PartitionSpec as P

BF = jnp.bfloat16
F32 = jnp.float32
CHUNKS = 2
STEP_GROUPS = 4


def pair_of_blocks(left, right, left_odd, right_odd, lane):
    def swapped(tile):
        return jnp.concatenate([tile[:, 64:], tile[:, :64]], axis=1)

    low = jnp.where(left_odd == 1, swapped(left), left)
    high = jnp.where(right_odd == 1, right, swapped(right))
    return jnp.where(lane < 64, low, high)


def partial_kernel(
    blocks, owner, place, occ, ao, *refs, slots, groups, width, shell, grp_count, chunk_rows
):
    vir = refs[:slots]
    outs = refs[slots:-4]
    half, half_abs, half_rel, slot_block = refs[-4:]
    step = pl.program_id(0)
    slice_rows = width // grp_count
    blocks_per_occ = owner.shape[0] // 2

    @pl.when(step == 0)
    def _():
        def put(b, carry):
            slot_block[owner[b]] = b
            return carry

        lax.fori_loop(0, owner.shape[0], put, 0)

    @pl.when(step < slots)
    def _():
        base = blocks[step, 0] * shell
        totals = [jnp.zeros((shell, width), F32) for _ in range(2)]
        for mu in range(shell):
            tile = ao[0, mu].astype(F32)
            for i in range(2):
                totals[i] = totals[i] + occ[i, base + mu] * tile
        position = lax.broadcasted_iota(jnp.int32, (shell, width), 1) + place[0] * width
        inside = (position >= blocks[step, 2]) & (position < blocks[step, 3])
        for i in range(2):
            rows = pl.ds(pl.multiple_of(step * shell, shell), shell)
            half[i, rows, :] = jnp.where(inside, totals[i], 0.0).astype(BF)

    @pl.when(step == slots)
    def _():
        for i in range(2):
            half_abs[i] = half[i].T
        for i in range(2):
            for r in range(grp_count):
                source = lax.rem(place[1] + r, grp_count) * slice_rows
                half_rel[i, pl.ds(r * slice_rows, slice_rows), :] = half_abs[
                    i, pl.ds(pl.multiple_of(source, 16), slice_rows), :
                ]

    @pl.when(step >= slots)
    def _():
        turn = step - slots
        first_half = turn < groups // STEP_GROUPS // 2
        lane = lax.broadcasted_iota(jnp.int32, (slots * shell, 128), 1)
        wide_lane = lax.broadcasted_iota(jnp.int32, (width, 256), 1)
        for at in range(STEP_GROUPS):
            g = turn * STEP_GROUPS + at
            tiles = []
            occ_is = []
            for pair in range(2):
                found = [slot_block[g * 4 + pair * 2 + j] for j in range(2)]
                read = []
                for b in found:
                    column = lax.rem(b, blocks_per_occ)
                    occ_is.append(b // blocks_per_occ)
                    lanes = pl.ds(pl.multiple_of((column // 2) * 128, 128), 128)
                    read.append(jnp.concatenate([v[:, lanes] for v in vir], axis=0))
                odd = [lax.rem(b, 2) for b in found]
                tiles.append(pair_of_blocks(read[0], read[1], odd[0], odd[1], lane))
            panel = jnp.concatenate(tiles, axis=1)
            both = [jnp.dot(half_rel[i], panel, preferred_element_type=F32) for i in range(2)]
            which = jnp.where(
                wide_lane < 128,
                jnp.where(wide_lane < 64, occ_is[0], occ_is[1]),
                jnp.where(wide_lane < 192, occ_is[2], occ_is[3]),
            )
            value = jnp.where(which == 0, both[0], both[1]).astype(BF)
            for c in range(CHUNKS):

                def rows(r):
                    begin = r * slice_rows + c * chunk_rows
                    return value[begin : begin + chunk_rows]

                mine = outs[c * 7 : c * 7 + 7]
                mine[0][at] = rows(0)

                @pl.when(first_half)
                def _():
                    mine[1][at] = rows(1)
                    mine[2][at] = rows(2)
                    mine[3][at] = rows(3)

                @pl.when(jnp.logical_not(first_half))
                def _():
                    mine[4][at] = rows(1)
                    mine[5][at] = rows(2)
                    mine[6][at] = rows(3)


def partial_pieces(ao_blocks, blocks, occ, vir_coeff, owner, place, groups):
    slots, shell, _, width = ao_blocks.shape
    virtuals = vir_coeff.shape[1]
    grp_count = 4
    chunk_rows = width // grp_count // CHUNKS
    turns = groups // STEP_GROUPS
    half_turns = turns // 2

    def vir_spec(k):
        return pl.BlockSpec((shell, virtuals), lambda t, blk, own, plc, oc: (blk[k, 1], 0))

    whole = pl.BlockSpec(
        (STEP_GROUPS, chunk_rows, 256), lambda t, *_: (jnp.maximum(t - slots, 0), 0, 0)
    )
    early = pl.BlockSpec(
        (STEP_GROUPS, chunk_rows, 256),
        lambda t, *_: (jnp.clip(t - slots, 0, half_turns - 1), 0, 0),
    )
    late = pl.BlockSpec(
        (STEP_GROUPS, chunk_rows, 256),
        lambda t, *_: (jnp.maximum(t - slots - half_turns, 0), 0, 0),
    )
    out_specs = ([whole] + [early] * 3 + [late] * 3) * CHUNKS
    full = jax.ShapeDtypeStruct((groups, chunk_rows, 256), BF)
    part = jax.ShapeDtypeStruct((groups // 2, chunk_rows, 256), BF)
    out_shape = ([full] + [part] * 6) * CHUNKS
    kernel = functools.partial(
        partial_kernel,
        slots=slots,
        groups=groups,
        width=width,
        shell=shell,
        grp_count=grp_count,
        chunk_rows=chunk_rows,
    )
    return pl.pallas_call(
        kernel,
        grid_spec=pltpu.PrefetchScalarGridSpec(
            num_scalar_prefetch=4,
            grid=(slots + turns,),
            in_specs=[
                pl.BlockSpec(
                    (1, shell, shell, width),
                    lambda t, *_: (jnp.minimum(t, slots - 1), 0, 0, 0),
                )
            ]
            + [vir_spec(k) for k in range(slots)],
            out_specs=out_specs,
            scratch_shapes=[
                pltpu.VMEM((2, slots * shell, width), BF),
                pltpu.VMEM((2, width, slots * shell), BF),
                pltpu.VMEM((2, width, slots * shell), BF),
                pltpu.SMEM((owner.shape[0],), jnp.int32),
            ],
        ),
        out_shape=out_shape,
        compiler_params=pltpu.CompilerParams(vmem_limit_bytes=48 * 1024 * 1024),
        cost_estimate=pl.CostEstimate(
            flops=4 * 1024 * 1024 * 1024, bytes_accessed=16 * 1024 * 1024, transcendentals=0
        ),
        name="partial_rows",
    )(blocks, owner, place, occ, ao_blocks, *([vir_coeff] * slots))


def back_kernel(owner, place, vir, *refs, groups, width, grp_count, chunk_rows):
    pieces = refs[: CHUNKS * 8]
    out = refs[CHUNKS * 8]
    density = refs[-1]
    slice_rows = width // grp_count
    half_groups = groups // 2
    tiles = density.shape[2] // 128

    @pl.when(pl.program_id(0) == 0)
    def _():
        lane = lax.broadcasted_iota(jnp.int32, (chunk_rows, 128), 1)

        def tile_of(t, carry):
            for i in range(2):
                slots = [owner[i * 2 * tiles + t * 2 + j] for j in range(2)]
                low_group = [d // 4 for d in slots]
                tile_at = [lax.rem(d // 2, 2) * 128 for d in slots]
                odd = [lax.rem(d, 2) for d in slots]
                for c in range(CHUNKS):
                    for r in range(grp_count):
                        pair = pieces[c * 8 + r * 2 : c * 8 + r * 2 + 2]
                        read = []
                        for j in range(2):
                            lanes = pl.ds(pl.multiple_of(tile_at[j], 128), 128)
                            inside = lax.rem(low_group[j], half_groups)
                            read.append(
                                jnp.where(
                                    low_group[j] < half_groups,
                                    pair[0][inside, :, lanes],
                                    pair[1][inside, :, lanes],
                                )
                            )
                        source = lax.rem(place[1] + r, grp_count) * slice_rows + c * chunk_rows
                        density[
                            i,
                            pl.ds(pl.multiple_of(source, 16), chunk_rows),
                            pl.ds(pl.multiple_of(t * 128, 128), 128),
                        ] = pair_of_blocks(read[0], read[1], odd[0], odd[1], lane)
            return carry

        lax.fori_loop(0, tiles, tile_of, 0)

    for i in range(2):
        out[i] = lax.dot_general(
            vir[...], density[i], (((1,), (1,)), ((), ())), preferred_element_type=F32
        ).astype(BF)


def back_transform(vir_coeff, owner, place, pieces, groups, width):
    rows, virtuals = vir_coeff.shape
    grp_count = 4
    chunk_rows = width // grp_count // CHUNKS
    tile_rows = 272
    piece = pl.BlockSpec((groups // 2, chunk_rows, 256), lambda t, *_: (0, 0, 0))
    return pl.pallas_call(
        functools.partial(
            back_kernel, groups=groups, width=width, grp_count=grp_count, chunk_rows=chunk_rows
        ),
        grid_spec=pltpu.PrefetchScalarGridSpec(
            num_scalar_prefetch=2,
            grid=(rows // tile_rows,),
            in_specs=[pl.BlockSpec((tile_rows, virtuals), lambda t, *_: (t, 0))]
            + [piece] * (CHUNKS * 8),
            out_specs=pl.BlockSpec((2, tile_rows, width), lambda t, *_: (0, t, 0)),
            scratch_shapes=[pltpu.VMEM((2, width, virtuals), BF)],
        ),
        out_shape=jax.ShapeDtypeStruct((2, rows, width), BF),
        compiler_params=pltpu.CompilerParams(vmem_limit_bytes=56 * 1024 * 1024),
        cost_estimate=pl.CostEstimate(
            flops=7 * 1024 * 1024 * 1024, bytes_accessed=18 * 1024 * 1024, transcendentals=0
        ),
        name="back_transform",
    )(owner, place, vir_coeff, *pieces)


def body(ao_blocks, blocks, occ_coeff, vir_coeff, occ_energy, vir_energy, owner):
    aux_place = lax.axis_index("aux")
    grp_place = lax.axis_index("grp")
    groups = lax.axis_size("aux")
    grp_count = lax.axis_size("grp")
    devices = groups * grp_count
    virtuals = vir_coeff.shape[1]
    shell = ao_blocks.shape[1]
    width = ao_blocks.shape[3]
    quarter_shells = vir_coeff.shape[0] // shell
    block_rows = 2 * virtuals // devices
    place = jnp.stack([aux_place, grp_place]).astype(jnp.int32)
    local_blocks = blocks - jnp.array([0, 1, 0, 0], jnp.int32)[None, :] * (grp_place * quarter_shells)
    pieces = partial_pieces(
        ao_blocks, local_blocks, occ_coeff.astype(F32), vir_coeff, owner, place, groups
    )

    def shift(value, by):
        return lax.ppermute(
            value, "grp", [(j, (j + by) % grp_count) for j in range(grp_count)]
        )

    device_ids = jnp.arange(devices, dtype=jnp.int32)
    members = aux_place * grp_count + jnp.arange(grp_count, dtype=jnp.int32)
    member_block = jnp.sum(
        (owner[None, :] == members[:, None]).astype(jnp.int32) * device_ids[None, :], axis=1
    )
    row_ids = (member_block[:, None] * block_rows + jnp.arange(block_rows, dtype=jnp.int32)).reshape(-1)
    pair_energy = (occ_energy[:, None] - vir_energy[None, :]).reshape(devices, block_rows)
    picked = (member_block[:, None] == device_ids[None, :]).astype(F32)
    panel_energy = jnp.sum(picked[:, :, None] * pair_energy[None], axis=1).reshape(-1)
    del row_ids

    arrived = []
    scores = None
    for c in range(CHUNKS):
        own, one_a, two_a, three_a, one_b, two_b, three_b = pieces[c * 7 : c * 7 + 7]
        relay_up = shift(two_a, 1)
        relay_down = shift(two_b, -1)
        up_b = shift(one_b, 1)
        down_a = shift(three_a, -1)
        up_a = shift((one_a.astype(F32) + relay_up.astype(F32)).astype(BF), 1)
        down_b = shift((three_b.astype(F32) + relay_down.astype(F32)).astype(BF), -1)
        half = groups // 2
        total = own.astype(F32) + jnp.concatenate(
            [
                up_a.astype(F32) + down_a.astype(F32),
                up_b.astype(F32) + down_b.astype(F32),
            ],
            axis=0,
        )
        rows = lax.all_to_all(total.astype(BF), "aux", split_axis=0, concat_axis=0, tiled=True)
        rows = rows.reshape(-1, 256)
        arrived.append(rows)
        term = lax.dot_general(rows, rows, (((0,), (0,)), ((), ())), preferred_element_type=F32)
        scores = term if scores is None else scores + term

    sent = scores.astype(BF)
    others = [shift(sent, by) for by in (1, 2, 3)]
    scores = scores + others[0].astype(F32) + others[1].astype(F32) + others[2].astype(F32)
    amplitude = (scores / (panel_energy[:, None] + panel_energy[None, :])).astype(BF)

    gathered = []
    for c in range(CHUNKS):
        density = jnp.dot(arrived[c], amplitude, preferred_element_type=F32).astype(BF)
        density = density.reshape(groups, -1, 256)
        back = lax.all_to_all(density, "aux", split_axis=0, concat_axis=0, tiled=True)
        first, second = back[: groups // 2], back[groups // 2 :]
        below_a, below_b = shift(first, 1), shift(second, 1)
        above_a, above_b = shift(first, -1), shift(second, -1)
        far_a = shift(below_a, 1)
        far_b = shift(above_b, -1)
        gathered += [first, second, above_a, above_b, far_a, far_b, below_a, below_b]

    return back_transform(vir_coeff, owner, place, gathered, groups, width)


def solution(mesh):
    return jax.shard_map(
        body,
        mesh=mesh,
        in_specs=(
            P(("aux", "grp"), None, None, None),
            P(("aux", "grp"), None),
            P(),
            P("grp", None),
            P(),
            P(),
            P(),
        ),
        out_specs=P(None, "grp", "aux"),
        check_vma=False,
    )
```

time: 481 us -> 238 us (0.49); the launches traced: 473 us -> 236 us
  waiting for transfers between devices: 268 us -> 121 us
  blocking collectives: 81.5 us -> 0 us
  local copies, waits for them, and re-layouts: 58.3 us -> 2.86 us
  starting transfers between devices: 7.77 us -> 54.8 us
  Pallas kernels: 0 us -> 46.6 us
  matrix products: 30.5 us -> 3.3 us
  between operations: 13.9 us -> 0.41 us
    all_gather x2 -> x0, waiting for transfers between devices: 126 us -> none  [the longest x1 66.5 us: body(): group_rows = lax.all_gather(density_rows, 'grp', axis=0, tiled=True)]
    all_to_all x1 -> x0, blocking collectives: 81.5 us -> none  [body(): lax.all_to_all(outgoing, 'aux', split_axis=0, concat_axis=1, tiled=True)]
    ppermute x0 -> x27, waiting for transfers between devices: none -> 79 us  [shift(): lax.ppermute(value, 'grp', [(j, (j + by) % grp_count) for j in range(grp_...]
    unnamed x4 -> x0, waiting for transfers between devices: 62.2 us -> none
    pallas_call x0 -> x2, Pallas kernels: none -> 46.6 us  [the longest x1 24.1 us: partial_pieces(): pl.pallas_call(kernel, grid_spec=pltpu.PrefetchScalarGridSpec(num_scalar_...]
    all_to_all x1 -> x4, waiting for transfers between devices: 79.8 us -> 41.6 us  [the longest x2 21.8 us: body(): lax.all_to_all(total.astype(BF), 'aux', split_axis=0, concat_axis=0, tile...]
    ppermute x0 -> x27, starting transfers between devices: none -> 33.9 us  [shift(): lax.ppermute(value, 'grp', [(j, (j + by) % grp_count) for j in range(grp_...]
    dot_general x4, matrix products: 30.5 us -> 3.3 us  [the longest x2 2.49 us: body(): jnp.dot(arrived[c], amplitude, preferred_element_type=F32).astype(BF)]
  transfers between devices with their start and end apart: 4 -> 31, of which waited for: 4 -> 19; matrix products, arithmetic and copies ran while one was open for 1% -> 4% of each run, Pallas kernels for 0% -> 0%
where the time goes in v1:
time: 238 us; the launch traced here: 236 us
  waiting for transfers between devices  121 us (51%)
  starting transfers between devices  54.8 us (23%)
  Pallas kernels  46.6 us (20%)
  other arithmetic  7.86 us (3%)
  matrix products  3.3 us (1%)
  local copies, waits for them, and re-layouts  2.86 us (1%)
    ppermute x27, waiting for transfers between devices, shift(): lax.ppermute(value, 'grp', [(j, (j + by) % grp_count) for j in range(grp_...  79 us
    ppermute x27, starting transfers between devices, shift(): lax.ppermute(value, 'grp', [(j, (j + by) % grp_count) for j in range(grp_...  33.9 us
    pallas_call x1, Pallas kernels, partial_pieces(): pl.pallas_call(kernel, grid_spec=pltpu.PrefetchScalarGridSpec(num_scalar_...  24.1 us
    pallas_call x1, Pallas kernels, back_transform(): pl.pallas_call(functools.partial(back_kernel, groups=groups, width=width,...  22.5 us
    all_to_all x2, waiting for transfers between devices, body(): lax.all_to_all(total.astype(BF), 'aux', split_axis=0, concat_axis=0, tile...  21.8 us
    all_to_all x2, waiting for transfers between devices, body(): lax.all_to_all(density, 'aux', split_axis=0, concat_axis=0, tiled=True)  19.8 us
    all_to_all x2, starting transfers between devices, body(): lax.all_to_all(total.astype(BF), 'aux', split_axis=0, concat_axis=0, tile...  12.6 us
    all_to_all x2, starting transfers between devices, body(): lax.all_to_all(density, 'aux', split_axis=0, concat_axis=0, tiled=True)  8.29 us
  transfers between devices with their start and end apart: 31, of which 19 were waited for; matrix products, arithmetic and copies ran while one was open for 4% of the time, Pallas kernels for 0%

profile of v1, /device:TPU:0, one launch (start us, length us, event | category | flops | bytes accessed | tf_op | source)
XLA Modules:
  0.0 236.5 jit_solution(16618013595285677722)
XLA Ops:
  2.9 24.1 %partial_rows.1 = (bf16[32,48,256]{2,1,0:T(8,128)(2,1)S(1)}, bf16[16,48,256]{2,1,0:T(8,128)(2,1)S(1)}, bf16[16,48,256]{2,1,0:T(8,128)(2,1)S(1)}, bf16[16,48,256]...) custom-call(s32[8,4]{1,0:T(8,128)S(1)} %broadcast_subtract_fusion.1., ...), custom_call_target="tpu_custom_call" | custom-call | flops 4294967296 | bytes 16777216 | tf_op jit(solution)/shard_map/partial_rows/pallas_call | solution.py:153
  27.0 1.5 collective-permute-start
  28.6 1.5 collective-permute-start.6
  30.1 1.7 collective-permute-start.2
  33.8 6.4 %collective-permute-done = bf16[16,48,256]{2,1,0:T(8,128)(2,1)S(1)} collective-permute-done((bf16[16,48,256]{2,1,0:T(8,128)(2,1)S(1)}, bf16[16,48,256]{2,1,0:T(8,128)(2,1)S(1)}, u32[]{:S(2)}, u32[]{:S(2)}) %collective-permute-start) | collective-permute-done | bytes 393248 | tf_op jit(solution)/shard_map/ppermute | solution.py:275
  41.8 5.6 %collective-permute-done.6 = bf16[16,48,256]{2,1,0:T(8,128)(2,1)S(1)} collective-permute-done((bf16[16,48,256]{2,1,0:T(8,128)(2,1)S(1)}, bf16[16,48,256]{2,1,0:T(8,128)(2,1)S(1)}, u32[]{:S(2)}, u32[]{:S(2)}) %collective-permute-start.6) | collective-permute-done | bytes 393248 | tf_op jit(solution)/shard_map/ppermute | solution.py:275
  48.0 17.7 %collective-permute-done.10 = bf16[16,48,256]{2,1,0:T(8,128)(2,1)S(1)} collective-permute-done((bf16[16,48,256]{2,1,0:T(8,128)(2,1)S(1)}, bf16[16,48,256]{2,1,0:T(8,128)(2,1)S(1)}, u32[]{:S(2)}, u32[]{:S(2)}) %collective-permute-start.10) | collective-permute-done | bytes 393248 | tf_op jit(solution)/shard_map/ppermute | solution.py:275
  67.0 2.1 collective-permute-start.11
  70.0 9.0 %collective-permute-done.7 = bf16[16,48,256]{2,1,0:T(8,128)(2,1)S(1)} collective-permute-done((bf16[16,48,256]{2,1,0:T(8,128)(2,1)S(1)}, bf16[16,48,256]{2,1,0:T(8,128)(2,1)S(1)}, u32[]{:S(2)}, u32[]{:S(2)}) %collective-permute-start.7) | collective-permute-done | bytes 393248 | tf_op jit(solution)/shard_map/ppermute | solution.py:275
  79.1 3.3 %collective-permute-start.5 = (bf16[16,48,256]{2,1,0:T(8,128)(2,1)}, bf16[16,48,256]{2,1,0:T(8,128)(2,1)}, u32[]{:S(2)}, u32[]{:S(2)}) collective-permute-start(bf16[16,48,256]{2,1,0:T(8,128)(2,1)} %add_convert_fusion.2), channel_id=1, source_target_pairs={{0,3},{1,0},{2,1},{3,2},{4,7},{5,4},{6,5},{7,6},{8,11},{9,8},{10,9... | collective-permute-start | bytes 1179656 | tf_op jit(solution)/shard_map/ppermute | solution.py:275
  83.6 8.4 %all-to-all-start.1 = ((bf16[32,48,256]{2,1,0:T(8,128)(2,1)}), bf16[32,48,256]{2,1,0:T(8,128)(2,1)S(1)}, u32[]{:S(2)}, u32[]{:S(2)}) async-start(bf16[32,48,256]{2,1,0:T(8,128)(2,1)} %fusion.1), calls=%async_computation.1 | async-start | bytes 1572864 | tf_op jit(solution)/shard_map/all_to_all | solution.py:308
  96.8 9.1 %all-to-all-done.1 = bf16[32,48,256]{2,1,0:T(8,128)(2,1)S(1)} async-done(((bf16[32,48,256]{2,1,0:T(8,128)(2,1)}), bf16[32,48,256]{2,1,0:T(8,128)(2,1)S(1)}, u32[]{:S(2)}, u32[]{:S(2)}) %all-to-all-start.1) | async-done | bytes 786464 | tf_op jit(solution)/shard_map/all_to_all | solution.py:308
  105.8 4.2 %all-to-all-start = ((bf16[32,48,256]{2,1,0:T(8,128)(2,1)}), bf16[32,48,256]{2,1,0:T(8,128)(2,1)S(1)}, u32[]{:S(2)}, u32[]{:S(2)}) async-start(bf16[32,48,256]{2,1,0:T(8,128)(2,1)} %fusion), calls=%async_computation | async-start | bytes 1572864 | tf_op jit(solution)/shard_map/all_to_all | solution.py:308
  111.1 12.8 %all-to-all-done = bf16[32,48,256]{2,1,0:T(8,128)(2,1)S(1)} async-done(((bf16[32,48,256]{2,1,0:T(8,128)(2,1)}), bf16[32,48,256]{2,1,0:T(8,128)(2,1)S(1)}, u32[]{:S(2)}, u32[]{:S(2)}) %all-to-all-start) | async-done | bytes 786464 | tf_op jit(solution)/shard_map/all_to_all | solution.py:308
  126.7 4.1 %collective-permute-done.14 = bf16[256,256]{1,0:T(8,128)(2,1)S(1)} collective-permute-done((bf16[256,256]{1,0:T(8,128)(2,1)S(1)}, bf16[256,256]{1,0:T(8,128)(2,1)S(1)}, u32[]{:S(2)}, u32[]{:S(2)}) %collective-permute-start.14) | collective-permute-done | bytes 131104 | tf_op jit(solution)/shard_map/ppermute | solution.py:275
  130.7 1.8 collective-permute-done.13
  132.6 2.3 collective-permute-done.12
  136.2 3.9 %all-to-all-start.2 = ((bf16[32,48,256]{2,1,0:T(8,128)(2,1)}), bf16[32,48,256]{2,1,0:T(8,128)(2,1)S(1)}, u32[]{:S(2)}, u32[]{:S(2)}) async-start(bf16[32,48,256]{2,1,0:T(8,128)(2,1)} %bitcast.5), calls=%async_computation.2 | async-start | bytes 1572864 | tf_op jit(solution)/shard_map/all_to_all | solution.py:323
  141.4 12.6 %all-to-all-done.2 = bf16[32,48,256]{2,1,0:T(8,128)(2,1)S(1)} async-done(((bf16[32,48,256]{2,1,0:T(8,128)(2,1)}), bf16[32,48,256]{2,1,0:T(8,128)(2,1)S(1)}, u32[]{:S(2)}, u32[]{:S(2)}) %all-to-all-start.2) | async-done | bytes 786464 | tf_op jit(solution)/shard_map/all_to_all | solution.py:323
  153.9 4.4 %all-to-all-start.3 = ((bf16[32,48,256]{2,1,0:T(8,128)(2,1)}), bf16[32,48,256]{2,1,0:T(8,128)(2,1)S(1)}, u32[]{:S(2)}, u32[]{:S(2)}) async-start(bf16[32,48,256]{2,1,0:T(8,128)(2,1)} %bitcast.7), calls=%async_computation.3 | async-start | bytes 1572864 | tf_op jit(solution)/shard_map/all_to_all | solution.py:323
  158.5 3.2 %collective-permute-start.16 = (bf16[16,48,256]{2,1,0:T(8,128)(2,1)S(1)}, bf16[16,48,256]{2,1,0:T(8,128)(2,1)S(1)}, u32[]{:S(2)}, u32[]{:S(2)}) collective-permute-start(bf16[16,48,256]{2,1,0:T(8,128)(2,1)S(1)} %get-tuple-element.35.refs_1_), channel_id=1, source_target_pairs={{0,3},{1,0},{2,1},{3,2},{4,7},{5,4},{6,5},{7,6},{8,11},{9,8},{10,9... | collective-permute-start | bytes 1179656 | tf_op jit(solution)/shard_map/ppermute | solution.py:275
  161.7 3.2 %collective-permute-start.15 = (bf16[16,48,256]{2,1,0:T(8,128)(2,1)S(1)}, bf16[16,48,256]{2,1,0:T(8,128)(2,1)}, u32[]{:S(2)}, u32[]{:S(2)}) collective-permute-start(bf16[16,48,256]{2,1,0:T(8,128)(2,1)S(1)} %get-tuple-element.36.refs_0_), channel_id=1, source_target_pairs={{0,3},{1,0},{2,1},{3,2},{4,7},{5,4},{6,5},{7,6},{8,11},{9,8},{10,9... | collective-permute-start | bytes 1179656 | tf_op jit(solution)/shard_map/ppermute | solution.py:275
  164.9 7.2 %all-to-all-done.3 = bf16[32,48,256]{2,1,0:T(8,128)(2,1)S(1)} async-done(((bf16[32,48,256]{2,1,0:T(8,128)(2,1)}), bf16[32,48,256]{2,1,0:T(8,128)(2,1)S(1)}, u32[]{:S(2)}, u32[]{:S(2)}) %all-to-all-start.3) | async-done | bytes 786464 | tf_op jit(solution)/shard_map/all_to_all | solution.py:323
  172.3 3.2 %collective-permute-start.22 = (bf16[16,48,256]{2,1,0:T(8,128)(2,1)S(1)}, bf16[16,48,256]{2,1,0:T(8,128)(2,1)S(1)}, u32[]{:S(2)}, u32[]{:S(2)}) collective-permute-start(bf16[16,48,256]{2,1,0:T(8,128)(2,1)S(1)} %get-tuple-element.33.refs_9_), channel_id=1, source_target_pairs={{0,3},{1,0},{2,1},{3,2},{4,7},{5,4},{6,5},{7,6},{8,11},{9,8},{10,9... | collective-permute-start | bytes 1179656 | tf_op jit(solution)/shard_map/ppermute | solution.py:275
  175.6 4.5 %collective-permute-done.17.refs_6_ = bf16[16,48,256]{2,1,0:T(8,128)(2,1)S(1)} collective-permute-done((bf16[16,48,256]{2,1,0:T(8,128)(2,1)S(1)}, bf16[16,48,256]{2,1,0:T(8,128)(2,1)S(1)}, u32[]{:S(2)}, u32[]{:S(2)}) %collective-permute-start.17) | collective-permute-done | bytes 393248 | tf_op jit(solution)/shard_map/ppermute | solution.py:275
  180.1 3.4 %collective-permute-start.19 = (bf16[16,48,256]{2,1,0:T(8,128)(2,1)S(1)}, bf16[16,48,256]{2,1,0:T(8,128)(2,1)S(1)}, u32[]{:S(2)}, u32[]{:S(2)}) collective-permute-start(bf16[16,48,256]{2,1,0:T(8,128)(2,1)S(1)} %collective-permute-done.16.refs_3_), channel_id=1, source_target_pairs={{0,3},{1,0},{2,1},{3,2},{4,7},{5,4},{6,5},{7,6},{8,11},{9,8},{10,9... | collective-permute-start | bytes 1179656 | tf_op jit(solution)/shard_map/ppermute | solution.py:275
  183.4 5.0 %collective-permute-done.26.refs_15_ = bf16[16,48,256]{2,1,0:T(8,128)(2,1)S(1)} collective-permute-done((bf16[16,48,256]{2,1,0:T(8,128)(2,1)S(1)}, bf16[16,48,256]{2,1,0:T(8,128)(2,1)S(1)}, u32[]{:S(2)}, u32[]{:S(2)}) %collective-permute-start.26) | collective-permute-done | bytes 393248 | tf_op jit(solution)/shard_map/ppermute | solution.py:275
  188.5 3.3 %collective-permute-start.25 = (bf16[16,48,256]{2,1,0:T(8,128)(2,1)S(1)}, bf16[16,48,256]{2,1,0:T(8,128)(2,1)S(1)}, u32[]{:S(2)}, u32[]{:S(2)}) collective-permute-start(bf16[16,48,256]{2,1,0:T(8,128)(2,1)S(1)} %collective-permute-done.22.refs_11_), channel_id=1, source_target_pairs={{0,3},{1,0},{2,1},{3,2},{4,7},{5,4},{6,5},{7,6},{8,11},{9,8},{10,9... | collective-permute-start | bytes 1179656 | tf_op jit(solution)/shard_map/ppermute | solution.py:275
  191.8 5.1 %collective-permute-done.23.refs_14_ = bf16[16,48,256]{2,1,0:T(8,128)(2,1)S(1)} collective-permute-done((bf16[16,48,256]{2,1,0:T(8,128)(2,1)S(1)}, bf16[16,48,256]{2,1,0:T(8,128)(2,1)S(1)}, u32[]{:S(2)}, u32[]{:S(2)}) %collective-permute-start.23) | collective-permute-done | bytes 393248 | tf_op jit(solution)/shard_map/ppermute | solution.py:275
  196.9 8.0 %collective-permute-done.19.refs_5_ = bf16[16,48,256]{2,1,0:T(8,128)(2,1)S(1)} collective-permute-done((bf16[16,48,256]{2,1,0:T(8,128)(2,1)S(1)}, bf16[16,48,256]{2,1,0:T(8,128)(2,1)S(1)}, u32[]{:S(2)}, u32[]{:S(2)}) %collective-permute-start.19) | collective-permute-done | bytes 393248 | tf_op jit(solution)/shard_map/ppermute | solution.py:275
  205.3 7.0 %collective-permute-done.25.refs_13_ = bf16[16,48,256]{2,1,0:T(8,128)(2,1)S(1)} collective-permute-done((bf16[16,48,256]{2,1,0:T(8,128)(2,1)S(1)}, bf16[16,48,256]{2,1,0:T(8,128)(2,1)S(1)}, u32[]{:S(2)}, u32[]{:S(2)}) %collective-permute-start.25) | collective-permute-done | bytes 393248 | tf_op jit(solution)/shard_map/ppermute | solution.py:275
  214.0 22.5 %back_transform.1 = bf16[2,1088,384]{2,1,0:T(8,128)(2,1)} custom-call(s32[128]{0:T(128)} %owner.3, s32[2]{0:T(128)} %copy-done.2, bf16[1088,4096]{1,0:T(8,128)(2,1)} %vir.1, bf16[16,48,256]{2,1,0:T(8,128)(2,1)} %copy-done.5, bf16[16,48,256]{2,1,0:T(8,128)(2,1)} %copy-done.4, bf16[16,48,256]{2,1,0:T(8,128)(2,1)} %collective-permute-done.15.refs_2_, ...), custom_call_target="tpu_custom_call" | custom-call | flops 7516192768 | bytes 18874368 | tf_op jit(solution)/shard_map/back_transform/pallas_call | solution.py:236
  (108 shorter events, 24.0 us)
Async XLA Ops:
  27.0 13.2 %collective-permute-start = (bf16[16,48,256]{2,1,0:T(8,128)(2,1)S(1)}, bf16[16,48,256]{2,1,0:T(8,128)(2,1)S(1)}, u32[]{:S(2)}, u32[]{:S(2)}) collective-permute-start(bf16[16,48,256]{2,1,0:T(8,128)(2,1)S(1)} %get-tuple-element.21), channel_id=1, source_target_pairs={{0,1},{1,2},{2,3},{3,0},{4,5},{5,6},{6,7},{7,4},{8,9},{9,10},{10,1... | collective-permute-start | bytes 1179656 | tf_op jit(solution)/shard_map/ppermute | solution.py:275
  28.6 18.9 %collective-permute-start.6 = (bf16[16,48,256]{2,1,0:T(8,128)(2,1)S(1)}, bf16[16,48,256]{2,1,0:T(8,128)(2,1)S(1)}, u32[]{:S(2)}, u32[]{:S(2)}) collective-permute-start(bf16[16,48,256]{2,1,0:T(8,128)(2,1)S(1)} %get-tuple-element.28), channel_id=1, source_target_pairs={{0,1},{1,2},{2,3},{3,0},{4,5},{5,6},{6,7},{7,4},{8,9},{9,10},{10,1... | collective-permute-start | bytes 1179656 | tf_op jit(solution)/shard_map/ppermute | solution.py:275
  30.1 61.9 %collective-permute-start.2 = (bf16[16,48,256]{2,1,0:T(8,128)(2,1)S(1)}, bf16[16,48,256]{2,1,0:T(8,128)(2,1)S(1)}, u32[]{:S(2)}, u32[]{:S(2)}) collective-permute-start(bf16[16,48,256]{2,1,0:T(8,128)(2,1)S(1)} %get-tuple-element.22), channel_id=1, source_target_pairs={{0,3},{1,0},{2,1},{3,2},{4,7},{5,4},{6,5},{7,6},{8,11},{9,8},{10,9... | collective-permute-start | bytes 1179656 | tf_op jit(solution)/shard_map/ppermute | solution.py:275
  31.8 35.2 %collective-permute-start.4 = (bf16[16,48,256]{2,1,0:T(8,128)(2,1)S(1)}, bf16[16,48,256]{2,1,0:T(8,128)(2,1)S(1)}, u32[]{:S(2)}, u32[]{:S(2)}) collective-permute-start(bf16[16,48,256]{2,1,0:T(8,128)(2,1)S(1)} %get-tuple-element.25), channel_id=1, source_target_pairs={{0,3},{1,0},{2,1},{3,2},{4,7},{5,4},{6,5},{7,6},{8,11},{9,8},{10,9... | collective-permute-start | bytes 1179656 | tf_op jit(solution)/shard_map/ppermute | solution.py:275
  32.3 37.6 %collective-permute-start.8 = (bf16[16,48,256]{2,1,0:T(8,128)(2,1)S(1)}, bf16[16,48,256]{2,1,0:T(8,128)(2,1)S(1)}, u32[]{:S(2)}, u32[]{:S(2)}) collective-permute-start(bf16[16,48,256]{2,1,0:T(8,128)(2,1)S(1)} %get-tuple-element.29), channel_id=1, source_target_pairs={{0,3},{1,0},{2,1},{3,2},{4,7},{5,4},{6,5},{7,6},{8,11},{9,8},{10,9... | collective-permute-start | bytes 1179656 | tf_op jit(solution)/shard_map/ppermute | solution.py:275
  40.3 25.4 %collective-permute-start.10 = (bf16[16,48,256]{2,1,0:T(8,128)(2,1)S(1)}, bf16[16,48,256]{2,1,0:T(8,128)(2,1)S(1)}, u32[]{:S(2)}, u32[]{:S(2)}) collective-permute-start(bf16[16,48,256]{2,1,0:T(8,128)(2,1)S(1)} %get-tuple-element.32), channel_id=1, source_target_pairs={{0,3},{1,0},{2,1},{3,2},{4,7},{5,4},{6,5},{7,6},{8,11},{9,8},{10,9... | collective-permute-start | bytes 1179656 | tf_op jit(solution)/shard_map/ppermute | solution.py:275
  47.5 31.6 %collective-permute-start.9 = (bf16[16,48,256]{2,1,0:T(8,128)(2,1)S(1)}, bf16[16,48,256]{2,1,0:T(8,128)(2,1)S(1)}, u32[]{:S(2)}, u32[]{:S(2)}) collective-permute-start(bf16[16,48,256]{2,1,0:T(8,128)(2,1)S(1)} %get-tuple-element.30), channel_id=1, source_target_pairs={{0,1},{1,2},{2,3},{3,0},{4,5},{5,6},{6,7},{7,4},{8,9},{9,10},{10,1... | collective-permute-start | bytes 1179656 | tf_op jit(solution)/shard_map/ppermute | solution.py:275
  65.7 13.3 %collective-permute-start.7 = (bf16[16,48,256]{2,1,0:T(8,128)(2,1)S(1)}, bf16[16,48,256]{2,1,0:T(8,128)(2,1)S(1)}, u32[]{:S(2)}, u32[]{:S(2)}) collective-permute-start(bf16[16,48,256]{2,1,0:T(8,128)(2,1)S(1)} %add_convert_fusion.1), channel_id=1, source_target_pairs={{0,1},{1,2},{2,3},{3,0},{4,5},{5,6},{6,7},{7,4},{8,9},{9,10},{10,1... | collective-permute-start | bytes 1179656 | tf_op jit(solution)/shard_map/ppermute | solution.py:275
  67.0 15.3 %collective-permute-start.11 = (bf16[16,48,256]{2,1,0:T(8,128)(2,1)S(1)}, bf16[16,48,256]{2,1,0:T(8,128)(2,1)S(1)}, u32[]{:S(2)}, u32[]{:S(2)}) collective-permute-start(bf16[16,48,256]{2,1,0:T(8,128)(2,1)S(1)} %add_convert_fusion), channel_id=1, source_target_pairs={{0,3},{1,0},{2,1},{3,2},{4,7},{5,4},{6,5},{7,6},{8,11},{9,8},{10,9... | collective-permute-start | bytes 1179656 | tf_op jit(solution)/shard_map/ppermute | solution.py:275
  70.0 24.4 %collective-permute-start.3 = (bf16[16,48,256]{2,1,0:T(8,128)(2,1)S(1)}, bf16[16,48,256]{2,1,0:T(8,128)(2,1)}, u32[]{:S(2)}, u32[]{:S(2)}) collective-permute-start(bf16[16,48,256]{2,1,0:T(8,128)(2,1)S(1)} %get-tuple-element.23), channel_id=1, source_target_pairs={{0,1},{1,2},{2,3},{3,0},{4,5},{5,6},{6,7},{7,4},{8,9},{9,10},{10,1... | collective-permute-start | bytes 1179656 | tf_op jit(solution)/shard_map/ppermute | solution.py:275
  78.9 14.3 %collective-permute-start.1 = (bf16[16,48,256]{2,1,0:T(8,128)(2,1)S(1)}, bf16[16,48,256]{2,1,0:T(8,128)(2,1)}, u32[]{:S(2)}, u32[]{:S(2)}) collective-permute-start(bf16[16,48,256]{2,1,0:T(8,128)(2,1)S(1)} %add_convert_fusion.3), channel_id=1, source_target_pairs={{0,1},{1,2},{2,3},{3,0},{4,5},{5,6},{6,7},{7,4},{8,9},{9,10},{10,1... | collective-permute-start | bytes 1179656 | tf_op jit(solution)/shard_map/ppermute | solution.py:275
  79.1 15.3 %collective-permute-start.5 = (bf16[16,48,256]{2,1,0:T(8,128)(2,1)}, bf16[16,48,256]{2,1,0:T(8,128)(2,1)}, u32[]{:S(2)}, u32[]{:S(2)}) collective-permute-start(bf16[16,48,256]{2,1,0:T(8,128)(2,1)} %add_convert_fusion.2), channel_id=1, source_target_pairs={{0,3},{1,0},{2,1},{3,2},{4,7},{5,4},{6,5},{7,6},{8,11},{9,8},{10,9... | collective-permute-start | bytes 1179656 | tf_op jit(solution)/shard_map/ppermute | solution.py:275
  83.6 22.2 %all-to-all-start.1 = ((bf16[32,48,256]{2,1,0:T(8,128)(2,1)}), bf16[32,48,256]{2,1,0:T(8,128)(2,1)S(1)}, u32[]{:S(2)}, u32[]{:S(2)}) async-start(bf16[32,48,256]{2,1,0:T(8,128)(2,1)} %fusion.1), calls=%async_computation.1 | async-start | bytes 1572864 | tf_op jit(solution)/shard_map/all_to_all | solution.py:308
  105.8 18.1 %all-to-all-start = ((bf16[32,48,256]{2,1,0:T(8,128)(2,1)}), bf16[32,48,256]{2,1,0:T(8,128)(2,1)S(1)}, u32[]{:S(2)}, u32[]{:S(2)}) async-start(bf16[32,48,256]{2,1,0:T(8,128)(2,1)} %fusion), calls=%async_computation | async-start | bytes 1572864 | tf_op jit(solution)/shard_map/all_to_all | solution.py:308
  124.3 6.4 %collective-permute-start.14 = (bf16[256,256]{1,0:T(8,128)(2,1)S(1)}, bf16[256,256]{1,0:T(8,128)(2,1)S(1)}, u32[]{:S(2)}, u32[]{:S(2)}) collective-permute-start(bf16[256,256]{1,0:T(8,128)(2,1)S(1)} %get-tuple-element.37), channel_id=1, source_target_pairs={{0,3},{1,0},{2,1},{3,2},{4,7},{5,4},{6,5},{7,6},{8,11},{9,8},{10,9... | collective-permute-start | bytes 393224 | tf_op jit(solution)/shard_map/ppermute | solution.py:275
  124.7 7.8 %collective-permute-start.13 = (bf16[256,256]{1,0:T(8,128)(2,1)S(1)}, bf16[256,256]{1,0:T(8,128)(2,1)S(1)}, u32[]{:S(2)}, u32[]{:S(2)}) collective-permute-start(bf16[256,256]{1,0:T(8,128)(2,1)S(1)} %get-tuple-element.37), channel_id=1, source_target_pairs={{0,2},{1,3},{2,0},{3,1},{4,6},{5,7},{6,4},{7,5},{8,10},{9,11},{10,... | collective-permute-start | bytes 393224 | tf_op jit(solution)/shard_map/ppermute | solution.py:275
  125.3 9.6 %collective-permute-start.12 = (bf16[256,256]{1,0:T(8,128)(2,1)S(1)}, bf16[256,256]{1,0:T(8,128)(2,1)S(1)}, u32[]{:S(2)}, u32[]{:S(2)}) collective-permute-start(bf16[256,256]{1,0:T(8,128)(2,1)S(1)} %get-tuple-element.37), channel_id=1, source_target_pairs={{0,1},{1,2},{2,3},{3,0},{4,5},{5,6},{6,7},{7,4},{8,9},{9,10},{10,1... | collective-permute-start | bytes 393224 | tf_op jit(solution)/shard_map/ppermute | solution.py:275
  136.2 17.7 %all-to-all-start.2 = ((bf16[32,48,256]{2,1,0:T(8,128)(2,1)}), bf16[32,48,256]{2,1,0:T(8,128)(2,1)S(1)}, u32[]{:S(2)}, u32[]{:S(2)}) async-start(bf16[32,48,256]{2,1,0:T(8,128)(2,1)} %bitcast.5), calls=%async_computation.2 | async-start | bytes 1572864 | tf_op jit(solution)/shard_map/all_to_all | solution.py:323
  153.9 18.2 %all-to-all-start.3 = ((bf16[32,48,256]{2,1,0:T(8,128)(2,1)}), bf16[32,48,256]{2,1,0:T(8,128)(2,1)S(1)}, u32[]{:S(2)}, u32[]{:S(2)}) async-start(bf16[32,48,256]{2,1,0:T(8,128)(2,1)} %bitcast.7), calls=%async_computation.3 | async-start | bytes 1572864 | tf_op jit(solution)/shard_map/all_to_all | solution.py:323
  158.4 54.7 %copy-start.4 = (bf16[16,48,256]{2,1,0:T(8,128)(2,1)}, bf16[16,48,256]{2,1,0:T(8,128)(2,1)S(1)}, u32[]{:S(2)}) copy-start(bf16[16,48,256]{2,1,0:T(8,128)(2,1)S(1)} %get-tuple-element.35.refs_1_) | copy-start | bytes 1179652
  158.4 13.9 %collective-permute-start.20 = (bf16[16,48,256]{2,1,0:T(8,128)(2,1)S(1)}, bf16[16,48,256]{2,1,0:T(8,128)(2,1)S(1)}, u32[]{:S(2)}, u32[]{:S(2)}) collective-permute-start(bf16[16,48,256]{2,1,0:T(8,128)(2,1)S(1)} %get-tuple-element.35.refs_1_), channel_id=1, source_target_pairs={{0,1},{1,2},{2,3},{3,0},{4,5},{5,6},{6,7},{7,4},{8,9},{9,10},{10,1... | collective-permute-start | bytes 1179656 | tf_op jit(solution)/shard_map/ppermute | solution.py:275
  158.5 17.1 %collective-permute-start.16 = (bf16[16,48,256]{2,1,0:T(8,128)(2,1)S(1)}, bf16[16,48,256]{2,1,0:T(8,128)(2,1)S(1)}, u32[]{:S(2)}, u32[]{:S(2)}) collective-permute-start(bf16[16,48,256]{2,1,0:T(8,128)(2,1)S(1)} %get-tuple-element.35.refs_1_), channel_id=1, source_target_pairs={{0,3},{1,0},{2,1},{3,2},{4,7},{5,4},{6,5},{7,6},{8,11},{9,8},{10,9... | collective-permute-start | bytes 1179656 | tf_op jit(solution)/shard_map/ppermute | solution.py:275
  161.7 18.3 %collective-permute-start.17 = (bf16[16,48,256]{2,1,0:T(8,128)(2,1)S(1)}, bf16[16,48,256]{2,1,0:T(8,128)(2,1)S(1)}, u32[]{:S(2)}, u32[]{:S(2)}) collective-permute-start(bf16[16,48,256]{2,1,0:T(8,128)(2,1)S(1)} %get-tuple-element.36.refs_0_), channel_id=1, source_target_pairs={{0,1},{1,2},{2,3},{3,0},{4,5},{5,6},{6,7},{7,4},{8,9},{9,10},{10,1... | collective-permute-start | bytes 1179656 | tf_op jit(solution)/shard_map/ppermute | solution.py:275
  161.7 18.3 %collective-permute-start.15 = (bf16[16,48,256]{2,1,0:T(8,128)(2,1)S(1)}, bf16[16,48,256]{2,1,0:T(8,128)(2,1)}, u32[]{:S(2)}, u32[]{:S(2)}) collective-permute-start(bf16[16,48,256]{2,1,0:T(8,128)(2,1)S(1)} %get-tuple-element.36.refs_0_), channel_id=1, source_target_pairs={{0,3},{1,0},{2,1},{3,2},{4,7},{5,4},{6,5},{7,6},{8,11},{9,8},{10,9... | collective-permute-start | bytes 1179656 | tf_op jit(solution)/shard_map/ppermute | solution.py:275
  172.2 16.2 %collective-permute-start.26 = (bf16[16,48,256]{2,1,0:T(8,128)(2,1)S(1)}, bf16[16,48,256]{2,1,0:T(8,128)(2,1)S(1)}, u32[]{:S(2)}, u32[]{:S(2)}) collective-permute-start(bf16[16,48,256]{2,1,0:T(8,128)(2,1)S(1)} %get-tuple-element.33.refs_9_), channel_id=1, source_target_pairs={{0,1},{1,2},{2,3},{3,0},{4,5},{5,6},{6,7},{7,4},{8,9},{9,10},{10,1... | collective-permute-start | bytes 1179656 | tf_op jit(solution)/shard_map/ppermute | solution.py:275
  172.3 16.1 %collective-permute-start.22 = (bf16[16,48,256]{2,1,0:T(8,128)(2,1)S(1)}, bf16[16,48,256]{2,1,0:T(8,128)(2,1)S(1)}, u32[]{:S(2)}, u32[]{:S(2)}) collective-permute-start(bf16[16,48,256]{2,1,0:T(8,128)(2,1)S(1)} %get-tuple-element.33.refs_9_), channel_id=1, source_target_pairs={{0,3},{1,0},{2,1},{3,2},{4,7},{5,4},{6,5},{7,6},{8,11},{9,8},{10,9... | collective-permute-start | bytes 1179656 | tf_op jit(solution)/shard_map/ppermute | solution.py:275
  175.6 21.3 %collective-permute-start.23 = (bf16[16,48,256]{2,1,0:T(8,128)(2,1)S(1)}, bf16[16,48,256]{2,1,0:T(8,128)(2,1)S(1)}, u32[]{:S(2)}, u32[]{:S(2)}) collective-permute-start(bf16[16,48,256]{2,1,0:T(8,128)(2,1)S(1)} %get-tuple-element.34.refs_8_), channel_id=1, source_target_pairs={{0,1},{1,2},{2,3},{3,0},{4,5},{5,6},{6,7},{7,4},{8,9},{9,10},{10,1... | collective-permute-start | bytes 1179656 | tf_op jit(solution)/shard_map/ppermute | solution.py:275
  180.0 16.9 %collective-permute-start.21 = (bf16[16,48,256]{2,1,0:T(8,128)(2,1)S(1)}, bf16[16,48,256]{2,1,0:T(8,128)(2,1)S(1)}, u32[]{:S(2)}, u32[]{:S(2)}) collective-permute-start(bf16[16,48,256]{2,1,0:T(8,128)(2,1)S(1)} %get-tuple-element.34.refs_8_), channel_id=1, source_target_pairs={{0,3},{1,0},{2,1},{3,2},{4,7},{5,4},{6,5},{7,6},{8,11},{9,8},{10,9... | collective-permute-start | bytes 1179656 | tf_op jit(solution)/shard_map/ppermute | solution.py:275
  180.1 24.9 %collective-permute-start.19 = (bf16[16,48,256]{2,1,0:T(8,128)(2,1)S(1)}, bf16[16,48,256]{2,1,0:T(8,128)(2,1)S(1)}, u32[]{:S(2)}, u32[]{:S(2)}) collective-permute-start(bf16[16,48,256]{2,1,0:T(8,128)(2,1)S(1)} %collective-permute-done.16.refs_3_), channel_id=1, source_target_pairs={{0,3},{1,0},{2,1},{3,2},{4,7},{5,4},{6,5},{7,6},{8,11},{9,8},{10,9... | collective-permute-start | bytes 1179656 | tf_op jit(solution)/shard_map/ppermute | solution.py:275
  188.5 16.9 %collective-permute-start.18 = (bf16[16,48,256]{2,1,0:T(8,128)(2,1)S(1)}, bf16[16,48,256]{2,1,0:T(8,128)(2,1)S(1)}, u32[]{:S(2)}, u32[]{:S(2)}) collective-permute-start(bf16[16,48,256]{2,1,0:T(8,128)(2,1)S(1)} %collective-permute-done.17.refs_6_), channel_id=1, source_target_pairs={{0,1},{1,2},{2,3},{3,0},{4,5},{5,6},{6,7},{7,4},{8,9},{9,10},{10,1... | collective-permute-start | bytes 1179656 | tf_op jit(solution)/shard_map/ppermute | solution.py:275
  188.5 23.9 %collective-permute-start.25 = (bf16[16,48,256]{2,1,0:T(8,128)(2,1)S(1)}, bf16[16,48,256]{2,1,0:T(8,128)(2,1)S(1)}, u32[]{:S(2)}, u32[]{:S(2)}) collective-permute-start(bf16[16,48,256]{2,1,0:T(8,128)(2,1)S(1)} %collective-permute-done.22.refs_11_), channel_id=1, source_target_pairs={{0,3},{1,0},{2,1},{3,2},{4,7},{5,4},{6,5},{7,6},{8,11},{9,8},{10,9... | collective-permute-start | bytes 1179656 | tf_op jit(solution)/shard_map/ppermute | solution.py:275
  196.9 16.2 %collective-permute-start.24 = (bf16[16,48,256]{2,1,0:T(8,128)(2,1)S(1)}, bf16[16,48,256]{2,1,0:T(8,128)(2,1)S(1)}, u32[]{:S(2)}, u32[]{:S(2)}) collective-permute-start(bf16[16,48,256]{2,1,0:T(8,128)(2,1)S(1)} %collective-permute-done.23.refs_14_), channel_id=1, source_target_pairs={{0,1},{1,2},{2,3},{3,0},{4,5},{5,6},{6,7},{7,4},{8,9},{9,10},{10,1... | collective-permute-start | bytes 1179656 | tf_op jit(solution)/shard_map/ppermute | solution.py:275
  (20 other events, 426.8 us)

commit v2 on v0

v2 whole, which is shorter than its diff:
```python
import functools

import jax
import jax.numpy as jnp
from jax import lax
from jax.experimental import pallas as pl
from jax.experimental.pallas import tpu as pltpu
from jax.sharding import PartitionSpec as P

BF = jnp.bfloat16
F32 = jnp.float32
CHUNKS = 2
SLOTS_PER_STEP = 2
GRP = 4
MIB = 1024 * 1024
VMEM = pl.BlockSpec(memory_space=pltpu.VMEM)
SMEM = pl.BlockSpec(memory_space=pltpu.SMEM)


def swapped(tile):
    return jnp.concatenate([tile[:, 64:], tile[:, :64]], axis=1)


def half_at(tile, block, place):
    return jnp.where(lax.rem(block, 2) == place, tile, swapped(tile))


def invert(owner, slot_block):
    def put(b, carry):
        slot_block[owner[b]] = b
        return carry

    lax.fori_loop(0, owner.shape[0], put, 0)


def multiply(half_rows, vir, natural):
    inner = half_rows.shape[1] // 2
    tiles = natural.shape[0] // 2
    for t in range(tiles // 2):
        panel = jnp.concatenate([v[:, t * 256 : (t + 1) * 256] for v in vir], axis=0)
        for i in range(2):
            product = jnp.dot(
                half_rows[:, i * inner : (i + 1) * inner], panel, preferred_element_type=F32
            ).astype(BF)
            for j in range(2):
                natural[i * tiles + t * 2 + j] = product[:, j * 128 : (j + 1) * 128]


def owner_order(natural, slot_block, groups, store):
    lane = lax.broadcasted_iota(jnp.int32, natural.shape[1:], 1)

    def one(g):
        for pair in range(2):
            tiles = []
            for j in range(2):
                b = slot_block[g * 4 + pair * 2 + j]
                tiles.append(half_at(natural[b // 2], b, j))
            value = jnp.where(lane < 64, tiles[0], tiles[1])
            store(g, slice(pair * 128, (pair + 1) * 128), value)

    def two(t, carry):
        one(t * 2)
        one(t * 2 + 1)
        return carry

    lax.fori_loop(groups[0] // 2, groups[1] // 2, two, 0)


def far_kernel(blocks, owner, occ, ao, *refs, slots, groups, width, shell, quarter_shells):
    vir = refs[:slots]
    rest, *outs = refs[slots : slots + 1 + 2 * CHUNKS]
    half, half_abs, far_rows, natural, slot_block = refs[-5:]
    step = pl.program_id(0)
    inner = slots * shell
    rows = width // GRP // CHUNKS
    first_position = blocks[0, 2]
    quarter = blocks[0, 1] // quarter_shells

    position = lax.broadcasted_iota(jnp.int32, (shell, width), 1) + first_position
    spread = (128, shell * shell)
    source_lane = lax.broadcasted_iota(jnp.int32, spread, 0)
    target_mu = lax.broadcasted_iota(jnp.int32, spread, 1) // shell
    row = lax.broadcasted_iota(jnp.int32, (shell, shell * shell), 0)
    column = lax.broadcasted_iota(jnp.int32, (shell, shell * shell), 1)
    diagonal = lax.rem(column, shell) == row
    per_tile = 128 // shell
    for s in range(SLOTS_PER_STEP):
        k = step * SLOTS_PER_STEP + s
        inside = (position >= blocks[k, 2]) & (position < blocks[k, 3])
        mu_block = blocks[k, 0]
        lanes = pl.ds(pl.multiple_of((mu_block // per_tile) * 128, 128), 128)
        pick = source_lane == target_mu + lax.rem(mu_block, per_tile) * shell
        wide = jnp.dot(
            occ[:, lanes], jnp.where(pick, 1.0, 0.0).astype(BF), preferred_element_type=F32
        )
        weights = jnp.concatenate(
            [
                jnp.where(
                    diagonal, jnp.broadcast_to(wide[i : i + 1, :], (shell, shell * shell)), 0.0
                )
                for i in range(2)
            ],
            axis=0,
        ).astype(BF)
        both = jnp.dot(
            weights, ao[s].reshape(shell * shell, width), preferred_element_type=F32
        )
        for i in range(2):
            at = pl.ds(pl.multiple_of(k * shell, shell), shell)
            half[i, at, :] = jnp.where(inside, both[i * shell : (i + 1) * shell], 0.0).astype(BF)

    @pl.when(step == 0)
    def _():
        invert(owner, slot_block)

    @pl.when(step == slots // SLOTS_PER_STEP - 1)
    def _():
        for i in range(2):
            half_abs[:, i * inner : (i + 1) * inner] = half[i].T
        for at, r in enumerate((2, 0, 1, 3)):
            for c in range(CHUNKS):
                source = (c * GRP + lax.rem(quarter + r, GRP)) * rows
                value = half_abs[pl.ds(pl.multiple_of(source, 16), rows), :]
                if r == 2:
                    far_rows[c * rows : (c + 1) * rows, :] = value
                else:
                    begin = ((at - 1) * CHUNKS + c) * rows
                    rest[begin : begin + rows, :] = value
        multiply(far_rows, vir, natural)
        for h in range(2):

            def store(g, lanes, value):
                for c in range(CHUNKS):
                    outs[c * 2 + h][g - h * (groups // 2), :, lanes] = value[
                        c * rows : (c + 1) * rows
                    ]

            owner_order(
                natural, slot_block, (h * (groups // 2), (h + 1) * (groups // 2)), store
            )


def near_kernel(blocks, owner, half_rows, *refs, slots, groups):
    vir = refs[:slots]
    outs = refs[slots : slots + 5 * CHUNKS]
    natural, slot_block = refs[-2:]
    rows = half_rows.shape[0] // (3 * CHUNKS)
    half = groups // 2
    invert(owner, slot_block)
    multiply(half_rows, vir, natural)
    for h in range(2):

        def store(g, lanes, value):
            for c in range(CHUNKS):
                own, up, down = (
                    value[(r * CHUNKS + c) * rows : (r * CHUNKS + c + 1) * rows]
                    for r in range(3)
                )
                outs[c * 5][g, :, lanes] = own
                outs[c * 5 + 1 + h][g - h * half, :, lanes] = up
                outs[c * 5 + 3 + h][g - h * half, :, lanes] = down

        owner_order(natural, slot_block, (h * half, (h + 1) * half), store)


def partial_pieces(ao_blocks, blocks, occ_coeff, vir_coeff, owner, groups):
    slots, shell, _, width = ao_blocks.shape
    quarter, virtuals = vir_coeff.shape
    quarter_shells = quarter // shell
    steps = slots // SLOTS_PER_STEP
    inner = slots * shell
    rows = width // GRP // CHUNKS
    near_rows = 3 * CHUNKS * rows

    def vir_spec(k):
        return pl.BlockSpec(
            (shell, virtuals), lambda t, blk, own: (lax.rem(blk[k, 1], quarter_shells), 0)
        )

    vir_specs = [vir_spec(k) for k in range(slots)]
    full = jax.ShapeDtypeStruct((groups, rows, 256), BF)
    part = jax.ShapeDtypeStruct((groups // 2, rows, 256), BF)
    rest, *far = pl.pallas_call(
        functools.partial(
            far_kernel,
            slots=slots,
            groups=groups,
            width=width,
            shell=shell,
            quarter_shells=quarter_shells,
        ),
        grid_spec=pltpu.PrefetchScalarGridSpec(
            num_scalar_prefetch=2,
            grid=(steps,),
            in_specs=[
                pl.BlockSpec(occ_coeff.shape, lambda t, *_: (0, 0)),
                pl.BlockSpec((SLOTS_PER_STEP, shell, shell, width), lambda t, *_: (t, 0, 0, 0)),
            ]
            + vir_specs,
            out_specs=[VMEM] * (1 + 2 * CHUNKS),
            scratch_shapes=[
                pltpu.VMEM((2, inner, width), BF),
                pltpu.VMEM((width, 2 * inner), BF),
                pltpu.VMEM((CHUNKS * rows, 2 * inner), BF),
                pltpu.VMEM((virtuals // 64, CHUNKS * rows, 128), BF),
                pltpu.SMEM((owner.shape[0],), jnp.int32),
            ],
        ),
        out_shape=[jax.ShapeDtypeStruct((near_rows, 2 * inner), BF)] + [part] * (2 * CHUNKS),
        compiler_params=pltpu.CompilerParams(vmem_limit_bytes=52 * MIB),
        cost_estimate=pl.CostEstimate(
            flops=1024 * MIB, bytes_accessed=10 * MIB, transcendentals=0
        ),
        name="far_rows",
    )(blocks, owner, occ_coeff, ao_blocks, *([vir_coeff] * slots))
    near = pl.pallas_call(
        functools.partial(near_kernel, slots=slots, groups=groups),
        grid_spec=pltpu.PrefetchScalarGridSpec(
            num_scalar_prefetch=2,
            grid=(1,),
            in_specs=[VMEM] + vir_specs,
            out_specs=[VMEM] * (5 * CHUNKS),
            scratch_shapes=[
                pltpu.VMEM((virtuals // 64, near_rows, 128), BF),
                pltpu.SMEM((owner.shape[0],), jnp.int32),
            ],
        ),
        out_shape=([full] + [part] * 4) * CHUNKS,
        compiler_params=pltpu.CompilerParams(vmem_limit_bytes=32 * MIB),
        cost_estimate=pl.CostEstimate(
            flops=2 * 1024 * MIB, bytes_accessed=8 * MIB, transcendentals=0
        ),
        name="near_rows",
    )(blocks, owner, rest, *([vir_coeff] * slots))
    return far, near


def reorder_kernel(owner, x, *outs):
    rows = x.shape[1]
    blocks_per_occ = owner.shape[0] // 2
    lane = lax.broadcasted_iota(jnp.int32, (rows, 128), 1)
    for i in range(2):
        for t in range(blocks_per_occ // 2):
            tiles = []
            for j in range(2):
                d = owner[i * blocks_per_occ + t * 2 + j]
                lanes = pl.ds(pl.multiple_of(lax.rem(d // 2, 2) * 128, 128), 128)
                tiles.append(half_at(x[d // 4, :, lanes], d, j))
            outs[i][:, t * 128 : (t + 1) * 128] = jnp.where(lane < 64, tiles[0], tiles[1])


def reorder(x, owner):
    groups, rows, _ = x.shape
    return pl.pallas_call(
        reorder_kernel,
        in_specs=[SMEM, VMEM],
        out_specs=[VMEM, VMEM],
        out_shape=[jax.ShapeDtypeStruct((rows, groups * 128), BF)] * 2,
        compiler_params=pltpu.CompilerParams(vmem_limit_bytes=16 * MIB),
        cost_estimate=pl.CostEstimate(flops=0, bytes_accessed=2 * MIB, transcendentals=0),
        name="reorder_rows",
    )(owner, x)


def back_kernel(blocks, vir, *refs, quarter_shells, earlier_width):
    pieces = refs[: 2 * GRP]
    earlier = refs[2 * GRP] if earlier_width else None
    out, panel = refs[-2:]
    rows = pieces[0].shape[0]
    width = GRP * rows
    padded = panel.shape[0] // 2
    quarter = blocks[0, 1] // quarter_shells

    @pl.when(pl.program_id(0) == 0)
    def _():
        for i in range(2):
            for r in range(GRP):
                at = i * padded + lax.rem(quarter + r, GRP) * rows
                panel[pl.ds(pl.multiple_of(at, 16), rows), :] = pieces[r * 2 + i][...]
            if padded > width:
                panel[i * padded + width : (i + 1) * padded, :] = jnp.zeros(
                    (padded - width, panel.shape[1]), BF
                )

    both = lax.dot_general(
        vir[...], panel[...], (((1,), (1,)), ((), ())), preferred_element_type=F32
    ).astype(BF)
    for i in range(2):
        value = both[:, i * padded : i * padded + width]
        if earlier_width:
            value = jnp.concatenate([earlier[i], value], axis=1)
        out[i] = value


def back_transform(vir_coeff, blocks, shell, pieces, earlier=None):
    nus, virtuals = vir_coeff.shape
    rows = pieces[0].shape[0]
    width = GRP * rows
    padded = (width + 127) // 128 * 128
    earlier_width = 0 if earlier is None else earlier.shape[2]
    tile = 272
    more = () if earlier is None else (earlier,)
    return pl.pallas_call(
        functools.partial(
            back_kernel, quarter_shells=nus // shell, earlier_width=earlier_width
        ),
        grid=(nus // tile,),
        in_specs=[SMEM, pl.BlockSpec((tile, virtuals), lambda t: (t, 0))]
        + [VMEM] * (2 * GRP)
        + [pl.BlockSpec((2, tile, earlier_width), lambda t: (0, t, 0))] * len(more),
        out_specs=pl.BlockSpec((2, tile, width + earlier_width), lambda t: (0, t, 0)),
        out_shape=jax.ShapeDtypeStruct((2, nus, width + earlier_width), BF),
        scratch_shapes=[pltpu.VMEM((2 * padded, virtuals), BF)],
        compiler_params=pltpu.CompilerParams(vmem_limit_bytes=48 * MIB),
        cost_estimate=pl.CostEstimate(
            flops=2 * nus * virtuals * 2 * width, bytes_accessed=11 * MIB, transcendentals=0
        ),
        name="back_transform",
    )(blocks, vir_coeff, *pieces, *more)


def shift(value, by):
    return lax.ppermute(value, "grp", [(j, (j + by) % GRP) for j in range(GRP)])


def add(*terms):
    return sum(t.astype(F32) for t in terms).astype(BF)


def body(ao_blocks, blocks, occ_coeff, vir_coeff, occ_energy, vir_energy, owner):
    aux_place = lax.axis_index("aux")
    groups = lax.axis_size("aux")
    devices = groups * GRP
    virtuals = vir_coeff.shape[1]
    shell = ao_blocks.shape[1]
    block_rows = 2 * virtuals // devices
    half = groups // 2
    far, near = partial_pieces(ao_blocks, blocks, occ_coeff, vir_coeff, owner, groups)

    own_a, up_low_a, up_high_a, down_low_a, down_high_a = near[:5]
    own_b, up_low_b, up_high_b, down_low_b, down_high_b = near[5:]
    relay_up, relay_down = shift(far[0], 1), shift(far[1], -1)
    up_high_a, down_low_a = shift(up_high_a, 1), shift(down_low_a, -1)
    far_b = far[2:]
    *far_b, up_high_a, down_low_a = lax.optimization_barrier((*far_b, up_high_a, down_low_a))
    relay_up_b, relay_down_b = shift(far_b[0], 1), shift(far_b[1], -1)
    up_low_a = shift(add(up_low_a, relay_up), 1)
    down_high_a = shift(add(down_high_a, relay_down), -1)
    up_b = jnp.concatenate([add(up_low_b, relay_up_b), up_high_b], axis=0)
    down_b = jnp.concatenate([down_low_b, add(down_high_b, relay_down_b)], axis=0)
    up_b, down_b = shift(up_b, 1), shift(down_b, -1)
    totals = [
        jnp.concatenate(
            [add(own_a[:half], up_low_a, down_low_a), add(own_a[half:], up_high_a, down_high_a)],
            axis=0,
        ),
        add(own_b, up_b, down_b),
    ]
    arrived = []
    scores = None
    for total in totals:
        rows = lax.all_to_all(total, "aux", split_axis=0, concat_axis=0, tiled=True)
        rows = rows.reshape(-1, 4 * block_rows)
        arrived.append(rows)
        term = lax.dot_general(rows, rows, (((0,), (0,)), ((), ())), preferred_element_type=F32)
        scores = term if scores is None else scores + term

    members = aux_place * GRP + jnp.arange(GRP, dtype=jnp.int32)
    picked = owner[None, :] == members[:, None]
    pair_energy = (occ_energy[:, None] - vir_energy[None, :]).reshape(devices, block_rows)
    energy = jnp.sum(jnp.where(picked[:, :, None], pair_energy[None], 0.0), axis=1).reshape(-1)
    sent = scores.astype(BF)
    others = [shift(sent, by) for by in (1, 2, 3)]
    scores = scores + others[0].astype(F32) + others[1].astype(F32) + others[2].astype(F32)
    amplitude = (scores / (energy[:, None] + energy[None, :])).astype(BF)

    result = None
    for rows in arrived:
        density = jnp.dot(rows, amplitude, preferred_element_type=F32).astype(BF)
        density = density.reshape(groups, -1, 4 * block_rows)
        back = lax.all_to_all(density, "aux", split_axis=0, concat_axis=0, tiled=True)
        own = reorder(back, owner)
        below = [shift(own[0], 1), shift(own[1], 1)]
        above = [shift(own[0], -1), shift(own[1], -1)]
        distant = (shift(below[0], 1), shift(above[1], -1))
        result = back_transform(
            vir_coeff, blocks, shell, (*own, *above, *distant, *below), result
        )
    return result


def solution(mesh):
    return jax.shard_map(
        body,
        mesh=mesh,
        in_specs=(
            P(("aux", "grp"), None, None, None),
            P(("aux", "grp"), None),
            P(),
            P("grp", None),
            P(),
            P(),
            P(),
        ),
        out_specs=P(None, "grp", "aux"),
        check_vma=False,
    )
```

time: 481 us -> 207 us (0.43); the launches traced: 473 us -> 206 us
  waiting for transfers between devices: 268 us -> 100 us
  blocking collectives: 81.5 us -> 0 us
  local copies, waits for them, and re-layouts: 58.3 us -> 2.66 us
  starting transfers between devices: 7.77 us -> 55.7 us
  Pallas kernels: 0 us -> 38.5 us
  matrix products: 30.5 us -> 3.32 us
  between operations: 13.9 us -> 0.19 us
  other arithmetic: 12.4 us -> 5.55 us
    all_gather x2 -> x0, waiting for transfers between devices: 126 us -> none  [the longest x1 66.5 us: body(): group_rows = lax.all_gather(density_rows, 'grp', axis=0, tiled=True)]
    all_to_all x1 -> x0, blocking collectives: 81.5 us -> none  [body(): lax.all_to_all(outgoing, 'aux', split_axis=0, concat_axis=1, tiled=True)]
    unnamed x4 -> x0, waiting for transfers between devices: 62.2 us -> none
    ppermute x0 -> x25, waiting for transfers between devices: none -> 60.6 us  [shift(): return lax.ppermute(value, 'grp', [(j, (j + by) % GRP) for j in range(GRP)])]
    all_to_all x1 -> x4, waiting for transfers between devices: 79.8 us -> 39.6 us  [the longest x2 20.7 us: body(): rows = lax.all_to_all(total, 'aux', split_axis=0, concat_axis=0, tiled=True)]
    pallas_call x0 -> x6, Pallas kernels: none -> 38.5 us  [the longest x2 16.7 us: back_transform(): pl.pallas_call(functools.partial(back_kernel, quarter_shells=nus // shell...]
    ppermute x0 -> x25, starting transfers between devices: none -> 34.8 us  [shift(): return lax.ppermute(value, 'grp', [(j, (j + by) % GRP) for j in range(GRP)])]
    dot_general x4, matrix products: 30.5 us -> 3.32 us  [the longest x2 2.51 us: body(): density = jnp.dot(rows, amplitude, preferred_element_type=F32).astype(BF)]
  transfers between devices with their start and end apart: 4 -> 29, of which waited for: 4 -> 18; matrix products, arithmetic and copies ran while one was open for 1% -> 4% of each run, Pallas kernels for 0% -> 6%
where the time goes in v2:
time: 207 us; the launch traced here: 206 us
  waiting for transfers between devices  100 us (48%)
  starting transfers between devices  55.7 us (27%)
  Pallas kernels  38.5 us (19%)
  other arithmetic  5.55 us (3%)
  matrix products  3.32 us (2%)
  local copies, waits for them, and re-layouts  2.66 us (1%)
    ppermute x25, waiting for transfers between devices, shift(): return lax.ppermute(value, 'grp', [(j, (j + by) % GRP) for j in range(GRP)])  60.6 us
    ppermute x25, starting transfers between devices, shift(): return lax.ppermute(value, 'grp', [(j, (j + by) % GRP) for j in range(GRP)])  34.8 us
    all_to_all x2, waiting for transfers between devices, body(): rows = lax.all_to_all(total, 'aux', split_axis=0, concat_axis=0, tiled=True)  20.7 us
    all_to_all x2, waiting for transfers between devices, body(): lax.all_to_all(density, 'aux', split_axis=0, concat_axis=0, tiled=True)  18.9 us
    pallas_call x2, Pallas kernels, back_transform(): pl.pallas_call(functools.partial(back_kernel, quarter_shells=nus // shell...  16.7 us
    all_to_all x2, starting transfers between devices, body(): rows = lax.all_to_all(total, 'aux', split_axis=0, concat_axis=0, tiled=True)  12.6 us
    pallas_call x1, Pallas kernels, partial_pieces(): pl.pallas_call(functools.partial(far_kernel, slots=slots, groups=groups,...  10.5 us
    all_to_all x2, starting transfers between devices, body(): lax.all_to_all(density, 'aux', split_axis=0, concat_axis=0, tiled=True)  8.28 us
  transfers between devices with their start and end apart: 29, of which 18 were waited for; matrix products, arithmetic and copies ran while one was open for 4% of the time, Pallas kernels for 6%

profile of v2, /device:TPU:0, one launch (start us, length us, event | category | flops | bytes accessed | tf_op | source)
XLA Modules:
  0.0 206.1 jit_solution(16861095682813137284)
XLA Ops:
  2.1 10.5 %far_rows.1 = (bf16[288,512]{1,0:T(8,128)(2,1)S(1)}, bf16[16,48,256]{2,1,0:T(8,128)(2,1)S(1)}, bf16[16,48,256]{2,1,0:T(8,128)(2,1)S(1)}, bf16[16,48,256]{2,1,0:T(8,128)(2,1)S(1)}, bf16[16,48,256]{2,1,0:T(8,128)(2,1)S(1)}) custom-call(s32[8,4]{1,0:T(8,128)S(1)} %copy.20.blocks, s32[128]{0:T(128)S(1)} %copy-done.2, bf16[2,4352]{1,0:T(2,128)(2,1)S(1)} %copy-done.1, ...), custom_call_target="tpu_custom_call" | custom-call | flops 1073741824 | bytes 10485760 | tf_op jit(solution)/shard_map/far_rows/pallas_call | solution.py:183
  12.7 7.0 %near_rows.1 = (bf16[32,48,256]{2,1,0:T(8,128)(2,1)S(1)}, bf16[16,48,256]{2,1,0:T(8,128)(2,1)S(1)}, bf16[16,48,256]{2,1,0:T(8,128)(2,1)S(1)}, bf16[16,48,256]{2,...) custom-call(s32[8,4]{1,0:T(8,128)S(1)} %copy.20.blocks, ...), custom_call_target="tpu_custom_call" | custom-call | flops 2147483648 | bytes 8388608 | tf_op jit(solution)/shard_map/near_rows/pallas_call | solution.py:216
  23.3 2.9 %collective-permute-start.8 = (bf16[16,48,256]{2,1,0:T(8,128)(2,1)S(1)}, bf16[16,48,256]{2,1,0:T(8,128)(2,1)S(1)}, u32[]{:S(2)}, u32[]{:S(2)}) collective-permute-start(bf16[16,48,256]{2,1,0:T(8,128)(2,1)S(1)} %get-tuple-element.46), channel_id=1, source_target_pairs={{0,3},{1,0},{2,1},{3,2},{4,7},{5,4},{6,5},{7,6},{8,11},{9,8},{10,9... | collective-permute-start | bytes 1179656 | tf_op jit(solution)/shard_map/ppermute | solution.py:323
  26.2 6.8 %collective-permute-done = bf16[16,48,256]{2,1,0:T(8,128)(2,1)S(1)} collective-permute-done((bf16[16,48,256]{2,1,0:T(8,128)(2,1)S(1)}, bf16[16,48,256]{2,1,0:T(8,128)(2,1)S(1)}, u32[]{:S(2)}, u32[]{:S(2)}) %collective-permute-start) | collective-permute-done | bytes 393248 | tf_op jit(solution)/shard_map/ppermute | solution.py:323
  34.8 6.6 %collective-permute-done.6 = bf16[16,48,256]{2,1,0:T(8,128)(2,1)S(1)} collective-permute-done((bf16[16,48,256]{2,1,0:T(8,128)(2,1)S(1)}, bf16[16,48,256]{2,1,0:T(8,128)(2,1)S(1)}, u32[]{:S(2)}, u32[]{:S(2)}) %collective-permute-start.6) | collective-permute-done | bytes 393248 | tf_op jit(solution)/shard_map/ppermute | solution.py:323
  41.9 2.9 %collective-permute-start.4 = (bf16[16,48,256]{2,1,0:T(8,128)(2,1)S(1)}, bf16[16,48,256]{2,1,0:T(8,128)(2,1)S(1)}, u32[]{:S(2)}, u32[]{:S(2)}) collective-permute-start(bf16[16,48,256]{2,1,0:T(8,128)(2,1)S(1)} %get-tuple-element.39), channel_id=1, source_target_pairs={{0,3},{1,0},{2,1},{3,2},{4,7},{5,4},{6,5},{7,6},{8,11},{9,8},{10,9... | collective-permute-start | bytes 1179656 | tf_op jit(solution)/shard_map/ppermute | solution.py:323
  45.4 4.4 %collective-permute-done.2 = bf16[16,48,256]{2,1,0:T(8,128)(2,1)S(1)} collective-permute-done((bf16[16,48,256]{2,1,0:T(8,128)(2,1)S(1)}, bf16[16,48,256]{2,1,0:T(8,128)(2,1)S(1)}, u32[]{:S(2)}, u32[]{:S(2)}) %collective-permute-start.2) | collective-permute-done | bytes 393248 | tf_op jit(solution)/shard_map/ppermute | solution.py:323
  50.4 3.9 %collective-permute-done.4 = bf16[16,48,256]{2,1,0:T(8,128)(2,1)S(1)} collective-permute-done((bf16[16,48,256]{2,1,0:T(8,128)(2,1)S(1)}, bf16[16,48,256]{2,1,0:T(8,128)(2,1)S(1)}, u32[]{:S(2)}, u32[]{:S(2)}) %collective-permute-start.4) | collective-permute-done | bytes 393248 | tf_op jit(solution)/shard_map/ppermute | solution.py:323
  55.4 3.7 %collective-permute-start.5 = (bf16[32,48,256]{2,1,0:T(8,128)(2,1)}, bf16[32,48,256]{2,1,0:T(8,128)(2,1)}, u32[]{:S(2)}, u32[]{:S(2)}) collective-permute-start(bf16[32,48,256]{2,1,0:T(8,128)(2,1)} %pad_maximum_fusion.1), channel_id=1, source_target_pairs={{0,3},{1,0},{2,1},{3,2},{4,7},{5,4},{6,5},{7,6},{8,11},{9,8},{10,9... | collective-permute-start | bytes 2359304 | tf_op jit(solution)/shard_map/ppermute | solution.py:323
  59.1 3.7 %collective-permute-done.9 = bf16[16,48,256]{2,1,0:T(8,128)(2,1)S(1)} collective-permute-done((bf16[16,48,256]{2,1,0:T(8,128)(2,1)S(1)}, bf16[16,48,256]{2,1,0:T(8,128)(2,1)S(1)}, u32[]{:S(2)}, u32[]{:S(2)}) %collective-permute-start.9) | collective-permute-done | bytes 393248 | tf_op jit(solution)/shard_map/ppermute | solution.py:323
  64.1 8.4 %all-to-all-start.1 = ((bf16[32,48,256]{2,1,0:T(8,128)(2,1)}), bf16[32,48,256]{2,1,0:T(8,128)(2,1)S(1)}, u32[]{:S(2)}, u32[]{:S(2)}) async-start(bf16[32,48,256]{2,1,0:T(8,128)(2,1)} %pad_maximum_fusion.2), calls=%async_computation.1 | async-start | bytes 1572864 | tf_op jit(solution)/shard_map/all_to_all | solution.py:362
  76.0 2.6 %add_convert_fusion = bf16[32,48,256]{2,1,0:T(8,128)(2,1)} fusion(bf16[32,48,256]{2,1,0:T(8,128)(2,1)} %collective-permute-done.5, bf16[32,48,256]{2,1,0:T(8,128)(2,1)} %collective-permute-done.3, bf16[32,48,256]{2,1,0:T(8,128)(2,1)S(1)} %get-tuple-element.29), kind=kLoop, calls=%fused_computation.2 | loop fusion | flops 2359296 | bytes 3145728 | tf_op jit(solution)/shard_map/convert_element_type | solution.py:327
  78.6 7.7 %all-to-all-done.1 = bf16[32,48,256]{2,1,0:T(8,128)(2,1)S(1)} async-done(((bf16[32,48,256]{2,1,0:T(8,128)(2,1)}), bf16[32,48,256]{2,1,0:T(8,128)(2,1)S(1)}, u32[]{:S(2)}, u32[]{:S(2)}) %all-to-all-start.1) | async-done | bytes 786464 | tf_op jit(solution)/shard_map/all_to_all | solution.py:362
  86.3 4.2 %all-to-all-start = ((bf16[32,48,256]{2,1,0:T(8,128)(2,1)}), bf16[32,48,256]{2,1,0:T(8,128)(2,1)S(1)}, u32[]{:S(2)}, u32[]{:S(2)}) async-start(bf16[32,48,256]{2,1,0:T(8,128)(2,1)} %add_convert_fusion), calls=%async_computation | async-start | bytes 1572864 | tf_op jit(solution)/shard_map/all_to_all | solution.py:362
  91.4 13.0 %all-to-all-done = bf16[32,48,256]{2,1,0:T(8,128)(2,1)S(1)} async-done(((bf16[32,48,256]{2,1,0:T(8,128)(2,1)}), bf16[32,48,256]{2,1,0:T(8,128)(2,1)S(1)}, u32[]{:S(2)}, u32[]{:S(2)}) %all-to-all-start) | async-done | bytes 786464 | tf_op jit(solution)/shard_map/all_to_all | solution.py:362
  105.9 4.1 %collective-permute-start.11 = (bf16[256,256]{1,0:T(8,128)(2,1)S(1)}, bf16[256,256]{1,0:T(8,128)(2,1)S(1)}, u32[]{:S(2)}, u32[]{:S(2)}) collective-permute-start(bf16[256,256]{1,0:T(8,128)(2,1)S(1)} %get-tuple-element.53), channel_id=1, source_target_pairs={{0,2},{1,3},{2,0},{3,1},{4,6},{5,7},{6,4},{7,5},{8,10},{9,11},{10,... | collective-permute-start | bytes 393224 | tf_op jit(solution)/shard_map/ppermute | solution.py:323
  110.3 2.6 %collective-permute-done.10 = bf16[256,256]{1,0:T(8,128)(2,1)S(1)} collective-permute-done((bf16[256,256]{1,0:T(8,128)(2,1)S(1)}, bf16[256,256]{1,0:T(8,128)(2,1)S(1)}, u32[]{:S(2)}, u32[]{:S(2)}) %collective-permute-start.10) | collective-permute-done | bytes 131104 | tf_op jit(solution)/shard_map/ppermute | solution.py:323
  112.9 4.0 %collective-permute-done.11 = bf16[256,256]{1,0:T(8,128)(2,1)S(1)} collective-permute-done((bf16[256,256]{1,0:T(8,128)(2,1)S(1)}, bf16[256,256]{1,0:T(8,128)(2,1)S(1)}, u32[]{:S(2)}, u32[]{:S(2)}) %collective-permute-start.11) | collective-permute-done | bytes 131104 | tf_op jit(solution)/shard_map/ppermute | solution.py:323
  118.2 4.1 %all-to-all-start.3 = ((bf16[32,48,256]{2,1,0:T(8,128)(2,1)}), bf16[32,48,256]{2,1,0:T(8,128)(2,1)S(1)}, u32[]{:S(2)}, u32[]{:S(2)}) async-start(bf16[32,48,256]{2,1,0:T(8,128)(2,1)} %bitcast.5), calls=%async_computation.3 | async-start | bytes 1572864 | tf_op jit(solution)/shard_map/all_to_all | solution.py:381
  123.6 12.6 %all-to-all-done.3.x = bf16[32,48,256]{2,1,0:T(8,128)(2,1)S(1)} async-done(((bf16[32,48,256]{2,1,0:T(8,128)(2,1)}), bf16[32,48,256]{2,1,0:T(8,128)(2,1)S(1)}, u32[]{:S(2)}, u32[]{:S(2)}) %all-to-all-start.3) | async-done | bytes 786464 | tf_op jit(solution)/shard_map/all_to_all | solution.py:381
  136.2 4.2 %all-to-all-start.2 = ((bf16[32,48,256]{2,1,0:T(8,128)(2,1)}), bf16[32,48,256]{2,1,0:T(8,128)(2,1)S(1)}, u32[]{:S(2)}, u32[]{:S(2)}) async-start(bf16[32,48,256]{2,1,0:T(8,128)(2,1)} %bitcast.3), calls=%async_computation.2 | async-start | bytes 1572864 | tf_op jit(solution)/shard_map/all_to_all | solution.py:381
  140.4 2.2 %reorder_rows.3 = (bf16[48,4096]{1,0:T(8,128)(2,1)S(1)}, bf16[48,4096]{1,0:T(8,128)(2,1)S(1)}) custom-call(s32[128]{0:T(128)S(1)} %copy-done.3, bf16[32,48,256]{2,1,0:T(8,128)(2,1)S(1)} %all-to-all-done.3.x), custom_call_target="tpu_custom_call" | custom-call | bytes 2097152 | tf_op jit(solution)/shard_map/reorder_rows/pallas_call | solution.py:254
  143.0 2.8 %collective-permute-start.20 = (bf16[48,4096]{1,0:T(8,128)(2,1)S(1)}, bf16[48,4096]{1,0:T(8,128)(2,1)S(1)}, u32[]{:S(2)}, u32[]{:S(2)}) collective-permute-start(bf16[48,4096]{1,0:T(8,128)(2,1)S(1)} %get-tuple-element.50.refs_1_), channel_id=1, source_target_pairs={{0,3},{1,0},{2,1},{3,2},{4,7},{5,4},{6,5},{7,6},{8,11},{9,8},{10,9... | collective-permute-start | bytes 1179656 | tf_op jit(solution)/shard_map/ppermute | solution.py:323
  147.9 6.3 %all-to-all-done.2.x = bf16[32,48,256]{2,1,0:T(8,128)(2,1)S(1)} async-done(((bf16[32,48,256]{2,1,0:T(8,128)(2,1)}), bf16[32,48,256]{2,1,0:T(8,128)(2,1)S(1)}, u32[]{:S(2)}, u32[]{:S(2)}) %all-to-all-start.2) | async-done | bytes 786464 | tf_op jit(solution)/shard_map/all_to_all | solution.py:381
  156.9 2.8 %collective-permute-start.14 = (bf16[48,4096]{1,0:T(8,128)(2,1)S(1)}, bf16[48,4096]{1,0:T(8,128)(2,1)S(1)}, u32[]{:S(2)}, u32[]{:S(2)}) collective-permute-start(bf16[48,4096]{1,0:T(8,128)(2,1)S(1)} %get-tuple-element.48.refs_1_), channel_id=1, source_target_pairs={{0,3},{1,0},{2,1},{3,2},{4,7},{5,4},{6,5},{7,6},{8,11},{9,8},{10,9... | collective-permute-start | bytes 1179656 | tf_op jit(solution)/shard_map/ppermute | solution.py:323
  159.7 4.1 %collective-permute-done.19.refs_2_ = bf16[48,4096]{1,0:T(8,128)(2,1)S(1)} collective-permute-done((bf16[48,4096]{1,0:T(8,128)(2,1)S(1)}, bf16[48,4096]{1,0:T(8,128)(2,1)S(1)}, u32[]{:S(2)}, u32[]{:S(2)}) %collective-permute-start.19) | collective-permute-done | bytes 393248 | tf_op jit(solution)/shard_map/ppermute | solution.py:323
  163.8 3.7 %collective-permute-start.23 = (bf16[48,4096]{1,0:T(8,128)(2,1)S(1)}, bf16[48,4096]{1,0:T(8,128)(2,1)S(1)}, u32[]{:S(2)}, u32[]{:S(2)}) collective-permute-start(bf16[48,4096]{1,0:T(8,128)(2,1)S(1)} %collective-permute-done.20.refs_3_), channel_id=1, source_target_pairs={{0,3},{1,0},{2,1},{3,2},{4,7},{5,4},{6,5},{7,6},{8,11},{9,8},{10,9... | collective-permute-start | bytes 1179656 | tf_op jit(solution)/shard_map/ppermute | solution.py:323
  167.5 5.1 %collective-permute-done.15.refs_6_ = bf16[48,4096]{1,0:T(8,128)(2,1)S(1)} collective-permute-done((bf16[48,4096]{1,0:T(8,128)(2,1)S(1)}, bf16[48,4096]{1,0:T(8,128)(2,1)S(1)}, u32[]{:S(2)}, u32[]{:S(2)}) %collective-permute-start.15) | collective-permute-done | bytes 393248 | tf_op jit(solution)/shard_map/ppermute | solution.py:323
  173.0 8.1 %collective-permute-done.22.refs_4_ = bf16[48,4096]{1,0:T(8,128)(2,1)S(1)} collective-permute-done((bf16[48,4096]{1,0:T(8,128)(2,1)S(1)}, bf16[48,4096]{1,0:T(8,128)(2,1)S(1)}, u32[]{:S(2)}, u32[]{:S(2)}) %collective-permute-start.22) | collective-permute-done | bytes 393248 | tf_op jit(solution)/shard_map/ppermute | solution.py:323
  182.0 7.8 %back_transform.2.refs_8_ = bf16[2,1088,192]{2,1,0:T(8,128)(2,1)S(1)} custom-call(s32[8,4]{1,0:T(8,128)S(1)} %copy.20.blocks, bf16[1088,4096]{1,0:T(8,128)(2,1)} %vir.3, bf16[48,4096]{1,0:T(8,128)(2,1)S(1)} %get-tuple-element.49.refs_0_, bf16[48,4096]{1,0:T(8,128)(2,1)S(1)} %get-tuple-element.50.refs_1_, ...), custom_call_target="tpu_custom_call" | custom-call | flops 3422552064 | bytes 11534336 | tf_op jit(solution)/shard_map/back_transform/pallas_call | solution.py:303
  189.8 7.4 %collective-permute-done.16.refs_4_ = bf16[48,4096]{1,0:T(8,128)(2,1)S(1)} collective-permute-done((bf16[48,4096]{1,0:T(8,128)(2,1)S(1)}, bf16[48,4096]{1,0:T(8,128)(2,1)S(1)}, u32[]{:S(2)}, u32[]{:S(2)}) %collective-permute-start.16) | collective-permute-done | bytes 393248 | tf_op jit(solution)/shard_map/ppermute | solution.py:323
  197.2 8.9 %back_transform.3 = bf16[2,1088,384]{2,1,0:T(8,128)(2,1)} custom-call(s32[8,4]{1,0:T(8,128)S(1)} %copy.20.blocks, bf16[1088,4096]{1,0:T(8,128)(2,1)} %vir.3, bf16[48,4096]{1,0:T(8,128)(2,1)S(1)} %get-tuple-element.47.refs_0_, bf16[48,4096]{1,0:T(8,128)(2,1)S(1)} %get-tuple-element.48.refs_1_, bf16[48,4096]{1,0:T(8,128)(2,1)S(1)} %collective-permute-done.13.refs_2_, ...), custom_call_target="tpu_custom_call" | custom-call | flops 3422552064 | bytes 11534336 | tf_op jit(solution)/shard_map/back_transform/pallas_call | solution.py:303
  (70 shorter events, 27.0 us)
Async XLA Ops:
  19.7 13.3 %collective-permute-start = (bf16[16,48,256]{2,1,0:T(8,128)(2,1)S(1)}, bf16[16,48,256]{2,1,0:T(8,128)(2,1)S(1)}, u32[]{:S(2)}, u32[]{:S(2)}) collective-permute-start(bf16[16,48,256]{2,1,0:T(8,128)(2,1)S(1)} %get-tuple-element.33), channel_id=1, source_target_pairs={{0,1},{1,2},{2,3},{3,0},{4,5},{5,6},{6,7},{7,4},{8,9},{9,10},{10,1... | collective-permute-start | bytes 1179656 | tf_op jit(solution)/shard_map/ppermute | solution.py:323
  21.3 12.0 %collective-permute-start.1 = (bf16[16,48,256]{2,1,0:T(8,128)(2,1)S(1)}, bf16[16,48,256]{2,1,0:T(8,128)(2,1)S(1)}, u32[]{:S(2)}, u32[]{:S(2)}) collective-permute-start(bf16[16,48,256]{2,1,0:T(8,128)(2,1)S(1)} %get-tuple-element.34), channel_id=1, source_target_pairs={{0,3},{1,0},{2,1},{3,2},{4,7},{5,4},{6,5},{7,6},{8,11},{9,8},{10,9... | collective-permute-start | bytes 1179656 | tf_op jit(solution)/shard_map/ppermute | solution.py:323
  23.0 18.4 %collective-permute-start.6 = (bf16[16,48,256]{2,1,0:T(8,128)(2,1)S(1)}, bf16[16,48,256]{2,1,0:T(8,128)(2,1)S(1)}, u32[]{:S(2)}, u32[]{:S(2)}) collective-permute-start(bf16[16,48,256]{2,1,0:T(8,128)(2,1)S(1)} %get-tuple-element.42), channel_id=1, source_target_pairs={{0,1},{1,2},{2,3},{3,0},{4,5},{5,6},{6,7},{7,4},{8,9},{9,10},{10,1... | collective-permute-start | bytes 1179656 | tf_op jit(solution)/shard_map/ppermute | solution.py:323
  23.3 21.5 %collective-permute-start.8 = (bf16[16,48,256]{2,1,0:T(8,128)(2,1)S(1)}, bf16[16,48,256]{2,1,0:T(8,128)(2,1)S(1)}, u32[]{:S(2)}, u32[]{:S(2)}) collective-permute-start(bf16[16,48,256]{2,1,0:T(8,128)(2,1)S(1)} %get-tuple-element.46), channel_id=1, source_target_pairs={{0,3},{1,0},{2,1},{3,2},{4,7},{5,4},{6,5},{7,6},{8,11},{9,8},{10,9... | collective-permute-start | bytes 1179656 | tf_op jit(solution)/shard_map/ppermute | solution.py:323
  33.4 16.5 %collective-permute-start.2 = (bf16[16,48,256]{2,1,0:T(8,128)(2,1)S(1)}, bf16[16,48,256]{2,1,0:T(8,128)(2,1)S(1)}, u32[]{:S(2)}, u32[]{:S(2)}) collective-permute-start(bf16[16,48,256]{2,1,0:T(8,128)(2,1)S(1)} %get-tuple-element.35), channel_id=1, source_target_pairs={{0,1},{1,2},{2,3},{3,0},{4,5},{5,6},{6,7},{7,4},{8,9},{9,10},{10,1... | collective-permute-start | bytes 1179656 | tf_op jit(solution)/shard_map/ppermute | solution.py:323
  41.5 17.6 %collective-permute-start.7 = (bf16[16,48,256]{2,1,0:T(8,128)(2,1)S(1)}, bf16[16,48,256]{2,1,0:T(8,128)(2,1)S(1)}, u32[]{:S(2)}, u32[]{:S(2)}) collective-permute-start(bf16[16,48,256]{2,1,0:T(8,128)(2,1)S(1)} %add_convert_fusion.4), channel_id=1, source_target_pairs={{0,1},{1,2},{2,3},{3,0},{4,5},{5,6},{6,7},{7,4},{8,9},{9,10},{10,1... | collective-permute-start | bytes 1179656 | tf_op jit(solution)/shard_map/ppermute | solution.py:323
  41.9 12.5 %collective-permute-start.4 = (bf16[16,48,256]{2,1,0:T(8,128)(2,1)S(1)}, bf16[16,48,256]{2,1,0:T(8,128)(2,1)S(1)}, u32[]{:S(2)}, u32[]{:S(2)}) collective-permute-start(bf16[16,48,256]{2,1,0:T(8,128)(2,1)S(1)} %get-tuple-element.39), channel_id=1, source_target_pairs={{0,3},{1,0},{2,1},{3,2},{4,7},{5,4},{6,5},{7,6},{8,11},{9,8},{10,9... | collective-permute-start | bytes 1179656 | tf_op jit(solution)/shard_map/ppermute | solution.py:323
  44.9 17.9 %collective-permute-start.9 = (bf16[16,48,256]{2,1,0:T(8,128)(2,1)S(1)}, bf16[16,48,256]{2,1,0:T(8,128)(2,1)S(1)}, u32[]{:S(2)}, u32[]{:S(2)}) collective-permute-start(bf16[16,48,256]{2,1,0:T(8,128)(2,1)S(1)} %add_convert_fusion.2), channel_id=1, source_target_pairs={{0,3},{1,0},{2,1},{3,2},{4,7},{5,4},{6,5},{7,6},{8,11},{9,8},{10,9... | collective-permute-start | bytes 1179656 | tf_op jit(solution)/shard_map/ppermute | solution.py:323
  50.0 23.9 %collective-permute-start.3 = (bf16[32,48,256]{2,1,0:T(8,128)(2,1)S(1)}, bf16[32,48,256]{2,1,0:T(8,128)(2,1)}, u32[]{:S(2)}, u32[]{:S(2)}) collective-permute-start(bf16[32,48,256]{2,1,0:T(8,128)(2,1)S(1)} %pad_maximum_fusion), channel_id=1, source_target_pairs={{0,1},{1,2},{2,3},{3,0},{4,5},{5,6},{6,7},{7,4},{8,9},{9,10},{10,1... | collective-permute-start | bytes 2359304 | tf_op jit(solution)/shard_map/ppermute | solution.py:323
  55.4 20.6 %collective-permute-start.5 = (bf16[32,48,256]{2,1,0:T(8,128)(2,1)}, bf16[32,48,256]{2,1,0:T(8,128)(2,1)}, u32[]{:S(2)}, u32[]{:S(2)}) collective-permute-start(bf16[32,48,256]{2,1,0:T(8,128)(2,1)} %pad_maximum_fusion.1), channel_id=1, source_target_pairs={{0,3},{1,0},{2,1},{3,2},{4,7},{5,4},{6,5},{7,6},{8,11},{9,8},{10,9... | collective-permute-start | bytes 2359304 | tf_op jit(solution)/shard_map/ppermute | solution.py:323
  64.1 22.2 %all-to-all-start.1 = ((bf16[32,48,256]{2,1,0:T(8,128)(2,1)}), bf16[32,48,256]{2,1,0:T(8,128)(2,1)S(1)}, u32[]{:S(2)}, u32[]{:S(2)}) async-start(bf16[32,48,256]{2,1,0:T(8,128)(2,1)} %pad_maximum_fusion.2), calls=%async_computation.1 | async-start | bytes 1572864 | tf_op jit(solution)/shard_map/all_to_all | solution.py:362
  78.6 12.0 %copy-start.4 = (f32[4096]{0:T(1024)S(1)}, f32[4096]{0:T(1024)}, u32[]{:S(2)}) copy-start(f32[4096]{0:T(1024)} %param.12) | copy-start | bytes 49156
  78.6 12.3 %copy-start.5 = (f32[2]{0:T(128)S(1)}, f32[2]{0:T(128)}, u32[]{:S(2)}) copy-start(f32[2]{0:T(128)} %param.11) | copy-start | bytes 28
  86.3 18.1 %all-to-all-start = ((bf16[32,48,256]{2,1,0:T(8,128)(2,1)}), bf16[32,48,256]{2,1,0:T(8,128)(2,1)S(1)}, u32[]{:S(2)}, u32[]{:S(2)}) async-start(bf16[32,48,256]{2,1,0:T(8,128)(2,1)} %add_convert_fusion), calls=%async_computation | async-start | bytes 1572864 | tf_op jit(solution)/shard_map/all_to_all | solution.py:362
  91.4 18.6 %copy-start.3 = (s32[128]{0:T(128)S(1)}, s32[128]{0:T(128)}, u32[]{:S(2)}) copy-start(s32[128]{0:T(128)} %owner.7) | copy-start | bytes 1540
  104.8 8.1 %collective-permute-start.10 = (bf16[256,256]{1,0:T(8,128)(2,1)S(1)}, bf16[256,256]{1,0:T(8,128)(2,1)S(1)}, u32[]{:S(2)}, u32[]{:S(2)}) collective-permute-start(bf16[256,256]{1,0:T(8,128)(2,1)S(1)} %get-tuple-element.53), channel_id=1, source_target_pairs={{0,1},{1,2},{2,3},{3,0},{4,5},{5,6},{6,7},{7,4},{8,9},{9,10},{10,1... | collective-permute-start | bytes 393224 | tf_op jit(solution)/shard_map/ppermute | solution.py:323
  105.9 10.9 %collective-permute-start.11 = (bf16[256,256]{1,0:T(8,128)(2,1)S(1)}, bf16[256,256]{1,0:T(8,128)(2,1)S(1)}, u32[]{:S(2)}, u32[]{:S(2)}) collective-permute-start(bf16[256,256]{1,0:T(8,128)(2,1)S(1)} %get-tuple-element.53), channel_id=1, source_target_pairs={{0,2},{1,3},{2,0},{3,1},{4,6},{5,7},{6,4},{7,5},{8,10},{9,11},{10,... | collective-permute-start | bytes 393224 | tf_op jit(solution)/shard_map/ppermute | solution.py:323
  110.0 6.8 %collective-permute-start.12 = (bf16[256,256]{1,0:T(8,128)(2,1)S(1)}, bf16[256,256]{1,0:T(8,128)(2,1)S(1)}, u32[]{:S(2)}, u32[]{:S(2)}) collective-permute-start(bf16[256,256]{1,0:T(8,128)(2,1)S(1)} %get-tuple-element.53), channel_id=1, source_target_pairs={{0,3},{1,0},{2,1},{3,2},{4,7},{5,4},{6,5},{7,6},{8,11},{9,8},{10,9... | collective-permute-start | bytes 393224 | tf_op jit(solution)/shard_map/ppermute | solution.py:323
  118.2 17.9 %all-to-all-start.3 = ((bf16[32,48,256]{2,1,0:T(8,128)(2,1)}), bf16[32,48,256]{2,1,0:T(8,128)(2,1)S(1)}, u32[]{:S(2)}, u32[]{:S(2)}) async-start(bf16[32,48,256]{2,1,0:T(8,128)(2,1)} %bitcast.5), calls=%async_computation.3 | async-start | bytes 1572864 | tf_op jit(solution)/shard_map/all_to_all | solution.py:381
  136.2 18.0 %all-to-all-start.2 = ((bf16[32,48,256]{2,1,0:T(8,128)(2,1)}), bf16[32,48,256]{2,1,0:T(8,128)(2,1)S(1)}, u32[]{:S(2)}, u32[]{:S(2)}) async-start(bf16[32,48,256]{2,1,0:T(8,128)(2,1)} %bitcast.3), calls=%async_computation.2 | async-start | bytes 1572864 | tf_op jit(solution)/shard_map/all_to_all | solution.py:381
  142.5 14.3 %collective-permute-start.21 = (bf16[48,4096]{1,0:T(8,128)(2,1)S(1)}, bf16[48,4096]{1,0:T(8,128)(2,1)S(1)}, u32[]{:S(2)}, u32[]{:S(2)}) collective-permute-start(bf16[48,4096]{1,0:T(8,128)(2,1)S(1)} %get-tuple-element.49.refs_0_), channel_id=1, source_target_pairs={{0,1},{1,2},{2,3},{3,0},{4,5},{5,6},{6,7},{7,4},{8,9},{9,10},{10,1... | collective-permute-start | bytes 1179656 | tf_op jit(solution)/shard_map/ppermute | solution.py:323
  143.0 16.7 %collective-permute-start.20 = (bf16[48,4096]{1,0:T(8,128)(2,1)S(1)}, bf16[48,4096]{1,0:T(8,128)(2,1)S(1)}, u32[]{:S(2)}, u32[]{:S(2)}) collective-permute-start(bf16[48,4096]{1,0:T(8,128)(2,1)S(1)} %get-tuple-element.50.refs_1_), channel_id=1, source_target_pairs={{0,3},{1,0},{2,1},{3,2},{4,7},{5,4},{6,5},{7,6},{8,11},{9,8},{10,9... | collective-permute-start | bytes 1179656 | tf_op jit(solution)/shard_map/ppermute | solution.py:323
  145.8 17.9 %collective-permute-start.19 = (bf16[48,4096]{1,0:T(8,128)(2,1)S(1)}, bf16[48,4096]{1,0:T(8,128)(2,1)S(1)}, u32[]{:S(2)}, u32[]{:S(2)}) collective-permute-start(bf16[48,4096]{1,0:T(8,128)(2,1)S(1)} %get-tuple-element.49.refs_0_), channel_id=1, source_target_pairs={{0,3},{1,0},{2,1},{3,2},{4,7},{5,4},{6,5},{7,6},{8,11},{9,8},{10,9... | collective-permute-start | bytes 1179656 | tf_op jit(solution)/shard_map/ppermute | solution.py:323
  146.8 20.7 %collective-permute-start.24 = (bf16[48,4096]{1,0:T(8,128)(2,1)S(1)}, bf16[48,4096]{1,0:T(8,128)(2,1)S(1)}, u32[]{:S(2)}, u32[]{:S(2)}) collective-permute-start(bf16[48,4096]{1,0:T(8,128)(2,1)S(1)} %get-tuple-element.50.refs_1_), channel_id=1, source_target_pairs={{0,1},{1,2},{2,3},{3,0},{4,5},{5,6},{6,7},{7,4},{8,9},{9,10},{10,1... | collective-permute-start | bytes 1179656 | tf_op jit(solution)/shard_map/ppermute | solution.py:323
  156.4 16.2 %collective-permute-start.15 = (bf16[48,4096]{1,0:T(8,128)(2,1)S(1)}, bf16[48,4096]{1,0:T(8,128)(2,1)S(1)}, u32[]{:S(2)}, u32[]{:S(2)}) collective-permute-start(bf16[48,4096]{1,0:T(8,128)(2,1)S(1)} %get-tuple-element.47.refs_0_), channel_id=1, source_target_pairs={{0,1},{1,2},{2,3},{3,0},{4,5},{5,6},{6,7},{7,4},{8,9},{9,10},{10,1... | collective-permute-start | bytes 1179656 | tf_op jit(solution)/shard_map/ppermute | solution.py:323
  156.9 15.7 %collective-permute-start.14 = (bf16[48,4096]{1,0:T(8,128)(2,1)S(1)}, bf16[48,4096]{1,0:T(8,128)(2,1)S(1)}, u32[]{:S(2)}, u32[]{:S(2)}) collective-permute-start(bf16[48,4096]{1,0:T(8,128)(2,1)S(1)} %get-tuple-element.48.refs_1_), channel_id=1, source_target_pairs={{0,3},{1,0},{2,1},{3,2},{4,7},{5,4},{6,5},{7,6},{8,11},{9,8},{10,9... | collective-permute-start | bytes 1179656 | tf_op jit(solution)/shard_map/ppermute | solution.py:323
  159.7 21.3 %collective-permute-start.22 = (bf16[48,4096]{1,0:T(8,128)(2,1)S(1)}, bf16[48,4096]{1,0:T(8,128)(2,1)S(1)}, u32[]{:S(2)}, u32[]{:S(2)}) collective-permute-start(bf16[48,4096]{1,0:T(8,128)(2,1)S(1)} %collective-permute-done.21.refs_6_), channel_id=1, source_target_pairs={{0,1},{1,2},{2,3},{3,0},{4,5},{5,6},{6,7},{7,4},{8,9},{9,10},{10,1... | collective-permute-start | bytes 1179656 | tf_op jit(solution)/shard_map/ppermute | solution.py:323
  163.8 18.2 %collective-permute-start.23 = (bf16[48,4096]{1,0:T(8,128)(2,1)S(1)}, bf16[48,4096]{1,0:T(8,128)(2,1)S(1)}, u32[]{:S(2)}, u32[]{:S(2)}) collective-permute-start(bf16[48,4096]{1,0:T(8,128)(2,1)S(1)} %collective-permute-done.20.refs_3_), channel_id=1, source_target_pairs={{0,3},{1,0},{2,1},{3,2},{4,7},{5,4},{6,5},{7,6},{8,11},{9,8},{10,9... | collective-permute-start | bytes 1179656 | tf_op jit(solution)/shard_map/ppermute | solution.py:323
  167.5 22.3 %collective-permute-start.13 = (bf16[48,4096]{1,0:T(8,128)(2,1)S(1)}, bf16[48,4096]{1,0:T(8,128)(2,1)S(1)}, u32[]{:S(2)}, u32[]{:S(2)}) collective-permute-start(bf16[48,4096]{1,0:T(8,128)(2,1)S(1)} %get-tuple-element.47.refs_0_), channel_id=1, source_target_pairs={{0,3},{1,0},{2,1},{3,2},{4,7},{5,4},{6,5},{7,6},{8,11},{9,8},{10,9... | collective-permute-start | bytes 1179656 | tf_op jit(solution)/shard_map/ppermute | solution.py:323
  172.6 17.2 %collective-permute-start.18 = (bf16[48,4096]{1,0:T(8,128)(2,1)S(1)}, bf16[48,4096]{1,0:T(8,128)(2,1)S(1)}, u32[]{:S(2)}, u32[]{:S(2)}) collective-permute-start(bf16[48,4096]{1,0:T(8,128)(2,1)S(1)} %get-tuple-element.48.refs_1_), channel_id=1, source_target_pairs={{0,1},{1,2},{2,3},{3,0},{4,5},{5,6},{6,7},{7,4},{8,9},{9,10},{10,1... | collective-permute-start | bytes 1179656 | tf_op jit(solution)/shard_map/ppermute | solution.py:323
  172.6 24.6 %collective-permute-start.16 = (bf16[48,4096]{1,0:T(8,128)(2,1)S(1)}, bf16[48,4096]{1,0:T(8,128)(2,1)S(1)}, u32[]{:S(2)}, u32[]{:S(2)}) collective-permute-start(bf16[48,4096]{1,0:T(8,128)(2,1)S(1)} %collective-permute-done.15.refs_6_), channel_id=1, source_target_pairs={{0,1},{1,2},{2,3},{3,0},{4,5},{5,6},{6,7},{7,4},{8,9},{9,10},{10,1... | collective-permute-start | bytes 1179656 | tf_op jit(solution)/shard_map/ppermute | solution.py:323
  181.0 16.2 %collective-permute-start.17 = (bf16[48,4096]{1,0:T(8,128)(2,1)S(1)}, bf16[48,4096]{1,0:T(8,128)(2,1)S(1)}, u32[]{:S(2)}, u32[]{:S(2)}) collective-permute-start(bf16[48,4096]{1,0:T(8,128)(2,1)S(1)} %collective-permute-done.14.refs_3_), channel_id=1, source_target_pairs={{0,3},{1,0},{2,1},{3,2},{4,7},{5,4},{6,5},{7,6},{8,11},{9,8},{10,9... | collective-permute-start | bytes 1179656 | tf_op jit(solution)/shard_map/ppermute | solution.py:323
  (3 other events, 11.9 us)

commit v3 on v2

--- a/solution.py
+++ b/solution.py
@@ -340,14 +340,18 @@
     own_a, up_low_a, up_high_a, down_low_a, down_high_a = near[:5]
     own_b, up_low_b, up_high_b, down_low_b, down_high_b = near[5:]
     relay_up, relay_down = shift(far[0], 1), shift(far[1], -1)
+    relay_up_b, relay_down_b = shift(far[2], 1), shift(far[3], -1)
+    up_high_a, down_low_a, relay_up, relay_down = lax.optimization_barrier(
+        (up_high_a, down_low_a, relay_up, relay_down)
+    )
     up_high_a, down_low_a = shift(up_high_a, 1), shift(down_low_a, -1)
-    far_b = far[2:]
-    *far_b, up_high_a, down_low_a = lax.optimization_barrier((*far_b, up_high_a, down_low_a))
-    relay_up_b, relay_down_b = shift(far_b[0], 1), shift(far_b[1], -1)
     up_low_a = shift(add(up_low_a, relay_up), 1)
     down_high_a = shift(add(down_high_a, relay_down), -1)
     up_b = jnp.concatenate([add(up_low_b, relay_up_b), up_high_b], axis=0)
     down_b = jnp.concatenate([down_low_b, add(down_high_b, relay_down_b)], axis=0)
+    up_b, down_b, up_high_a, down_low_a = lax.optimization_barrier(
+        (up_b, down_b, up_high_a, down_low_a)
+    )
     up_b, down_b = shift(up_b, 1), shift(down_b, -1)
     totals = [
         jnp.concatenate(

time: 207 us -> 195 us (0.942)
  waiting for transfers between devices: 100 us -> 88.8 us
    ppermute x25, waiting for transfers between devices: 60.6 us -> 51.6 us  [shift(): return lax.ppermute(value, 'grp', [(j, (j + by) % GRP) for j in range(GRP)])]
    all_to_all x2, waiting for transfers between devices: 20.7 us -> 18.3 us  [body(): rows = lax.all_to_all(total, 'aux', split_axis=0, concat_axis=0, tiled=True)]
  transfers between devices with their start and end apart: 29 -> 29, of which waited for: 18 -> 18; matrix products, arithmetic and copies ran while one was open for 4% -> 4% of each run, Pallas kernels for 6% -> 10%
where the time goes in v3:
time: 195 us; the launch traced here: 194 us
  waiting for transfers between devices  88.8 us (46%)
  starting transfers between devices  55.1 us (28%)
  Pallas kernels  38.6 us (20%)
  other arithmetic  5.59 us (3%)
  matrix products  3.33 us (2%)
  local copies, waits for them, and re-layouts  2.73 us (1%)
    ppermute x25, waiting for transfers between devices, shift(): return lax.ppermute(value, 'grp', [(j, (j + by) % GRP) for j in range(GRP)])  51.6 us
    ppermute x25, starting transfers between devices, shift(): return lax.ppermute(value, 'grp', [(j, (j + by) % GRP) for j in range(GRP)])  34.2 us
    all_to_all x2, waiting for transfers between devices, body(): lax.all_to_all(density, 'aux', split_axis=0, concat_axis=0, tiled=True)  18.9 us
    all_to_all x2, waiting for transfers between devices, body(): rows = lax.all_to_all(total, 'aux', split_axis=0, concat_axis=0, tiled=True)  18.3 us
    pallas_call x2, Pallas kernels, back_transform(): pl.pallas_call(functools.partial(back_kernel, quarter_shells=nus // shell...  16.7 us
    all_to_all x2, starting transfers between devices, body(): rows = lax.all_to_all(total, 'aux', split_axis=0, concat_axis=0, tiled=True)  12.6 us
    pallas_call x1, Pallas kernels, partial_pieces(): pl.pallas_call(functools.partial(far_kernel, slots=slots, groups=groups,...  10.6 us
    all_to_all x2, starting transfers between devices, body(): lax.all_to_all(density, 'aux', split_axis=0, concat_axis=0, tiled=True)  8.28 us
  transfers between devices with their start and end apart: 29, of which 18 were waited for; matrix products, arithmetic and copies ran while one was open for 4% of the time, Pallas kernels for 10%

profile of v3, /device:TPU:0, one launch (start us, length us, event | category | flops | bytes accessed | tf_op | source)
XLA Modules:
  0.0 194.4 jit_solution(2501708689892905722)
XLA Ops:
  2.2 10.6 %far_rows.1 = (bf16[288,512]{1,0:T(8,128)(2,1)S(1)}, bf16[16,48,256]{2,1,0:T(8,128)(2,1)S(1)}, bf16[16,48,256]{2,1,0:T(8,128)(2,1)S(1)}, bf16[16,48,256]{2,1,0:T(8,128)(2,1)S(1)}, bf16[16,48,256]{2,1,0:T(8,128)(2,1)S(1)}) custom-call(s32[8,4]{1,0:T(8,128)S(1)} %copy.20.blocks, s32[128]{0:T(128)S(1)} %copy-done.1, bf16[2,4352]{1,0:T(2,128)(2,1)S(1)} %copy-done, ...), custom_call_target="tpu_custom_call" | custom-call | flops 1073741824 | bytes 10485760 | tf_op jit(solution)/shard_map/far_rows/pallas_call | solution.py:183
  14.4 1.7 collective-permute-start.3
  18.2 7.0 %near_rows.1 = (bf16[32,48,256]{2,1,0:T(8,128)(2,1)S(1)}, bf16[16,48,256]{2,1,0:T(8,128)(2,1)S(1)}, bf16[16,48,256]{2,1,0:T(8,128)(2,1)S(1)}, bf16[16,48,256]{2,...) custom-call(s32[8,4]{1,0:T(8,128)S(1)} %copy.20.blocks, ...), custom_call_target="tpu_custom_call" | custom-call | flops 2147483648 | bytes 8388608 | tf_op jit(solution)/shard_map/near_rows/pallas_call | solution.py:216
  28.0 1.7 collective-permute-start.5
  29.8 1.8 collective-permute-start.9
  31.7 3.2 %collective-permute-done.1 = bf16[16,48,256]{2,1,0:T(8,128)(2,1)S(1)} collective-permute-done((bf16[16,48,256]{2,1,0:T(8,128)(2,1)S(1)}, bf16[16,48,256]{2,1,0:T(8,128)(2,1)S(1)}, u32[]{:S(2)}, u32[]{:S(2)}) %collective-permute-start.1) | collective-permute-done | bytes 393248 | tf_op jit(solution)/shard_map/ppermute | solution.py:323
  37.6 5.3 %collective-permute-done.4 = bf16[16,48,256]{2,1,0:T(8,128)(2,1)S(1)} collective-permute-done((bf16[16,48,256]{2,1,0:T(8,128)(2,1)S(1)}, bf16[16,48,256]{2,1,0:T(8,128)(2,1)S(1)}, u32[]{:S(2)}, u32[]{:S(2)}) %collective-permute-start.4) | collective-permute-done | bytes 393248 | tf_op jit(solution)/shard_map/ppermute | solution.py:323
  44.8 1.7 collective-permute-start.7
  46.5 5.2 %collective-permute-done.9 = bf16[16,48,256]{2,1,0:T(8,128)(2,1)S(1)} collective-permute-done((bf16[16,48,256]{2,1,0:T(8,128)(2,1)S(1)}, bf16[16,48,256]{2,1,0:T(8,128)(2,1)S(1)}, u32[]{:S(2)}, u32[]{:S(2)}) %collective-permute-start.9) | collective-permute-done | bytes 393248 | tf_op jit(solution)/shard_map/ppermute | solution.py:323
  53.0 8.3 %all-to-all-start.1 = ((bf16[32,48,256]{2,1,0:T(8,128)(2,1)}), bf16[32,48,256]{2,1,0:T(8,128)(2,1)S(1)}, u32[]{:S(2)}, u32[]{:S(2)}) async-start(bf16[32,48,256]{2,1,0:T(8,128)(2,1)} %pad_maximum_fusion.2), calls=%async_computation.1 | async-start | bytes 1572864 | tf_op jit(solution)/shard_map/all_to_all | solution.py:366
  61.4 5.8 %collective-permute-done.6 = bf16[32,48,256]{2,1,0:T(8,128)(2,1)} collective-permute-done((bf16[32,48,256]{2,1,0:T(8,128)(2,1)}, bf16[32,48,256]{2,1,0:T(8,128)(2,1)}, u32[]{:S(2)}, u32[]{:S(2)}) %collective-permute-start.6) | collective-permute-done | bytes 786464 | tf_op jit(solution)/shard_map/ppermute | solution.py:323
  67.3 2.6 %add_convert_fusion = bf16[32,48,256]{2,1,0:T(8,128)(2,1)} fusion(bf16[32,48,256]{2,1,0:T(8,128)(2,1)} %collective-permute-done.7, bf16[32,48,256]{2,1,0:T(8,128)(2,1)} %collective-permute-done.6, bf16[32,48,256]{2,1,0:T(8,128)(2,1)S(1)} %get-tuple-element.33), kind=kLoop, calls=%fused_computation.2 | loop fusion | flops 2359296 | bytes 3145728 | tf_op jit(solution)/shard_map/convert_element_type | solution.py:327
  69.9 5.3 %all-to-all-done.1 = bf16[32,48,256]{2,1,0:T(8,128)(2,1)S(1)} async-done(((bf16[32,48,256]{2,1,0:T(8,128)(2,1)}), bf16[32,48,256]{2,1,0:T(8,128)(2,1)S(1)}, u32[]{:S(2)}, u32[]{:S(2)}) %all-to-all-start.1) | async-done | bytes 786464 | tf_op jit(solution)/shard_map/all_to_all | solution.py:366
  75.2 4.2 %all-to-all-start = ((bf16[32,48,256]{2,1,0:T(8,128)(2,1)}), bf16[32,48,256]{2,1,0:T(8,128)(2,1)S(1)}, u32[]{:S(2)}, u32[]{:S(2)}) async-start(bf16[32,48,256]{2,1,0:T(8,128)(2,1)} %add_convert_fusion), calls=%async_computation | async-start | bytes 1572864 | tf_op jit(solution)/shard_map/all_to_all | solution.py:366
  80.3 13.0 %all-to-all-done = bf16[32,48,256]{2,1,0:T(8,128)(2,1)S(1)} async-done(((bf16[32,48,256]{2,1,0:T(8,128)(2,1)}), bf16[32,48,256]{2,1,0:T(8,128)(2,1)S(1)}, u32[]{:S(2)}, u32[]{:S(2)}) %all-to-all-start) | async-done | bytes 786464 | tf_op jit(solution)/shard_map/all_to_all | solution.py:366
  95.3 2.9 %collective-permute-start.11 = (bf16[256,256]{1,0:T(8,128)(2,1)S(1)}, bf16[256,256]{1,0:T(8,128)(2,1)S(1)}, u32[]{:S(2)}, u32[]{:S(2)}) collective-permute-start(bf16[256,256]{1,0:T(8,128)(2,1)S(1)} %get-tuple-element.61), channel_id=1, source_target_pairs={{0,2},{1,3},{2,0},{3,1},{4,6},{5,7},{6,4},{7,5},{8,10},{9,11},{10,... | collective-permute-start | bytes 393224 | tf_op jit(solution)/shard_map/ppermute | solution.py:323
  101.1 4.0 %collective-permute-done.11 = bf16[256,256]{1,0:T(8,128)(2,1)S(1)} collective-permute-done((bf16[256,256]{1,0:T(8,128)(2,1)S(1)}, bf16[256,256]{1,0:T(8,128)(2,1)S(1)}, u32[]{:S(2)}, u32[]{:S(2)}) %collective-permute-start.11) | collective-permute-done | bytes 131104 | tf_op jit(solution)/shard_map/ppermute | solution.py:323
  106.5 4.1 %all-to-all-start.3 = ((bf16[32,48,256]{2,1,0:T(8,128)(2,1)}), bf16[32,48,256]{2,1,0:T(8,128)(2,1)S(1)}, u32[]{:S(2)}, u32[]{:S(2)}) async-start(bf16[32,48,256]{2,1,0:T(8,128)(2,1)} %bitcast.5), calls=%async_computation.3 | async-start | bytes 1572864 | tf_op jit(solution)/shard_map/all_to_all | solution.py:385
  111.8 12.6 %all-to-all-done.3.x = bf16[32,48,256]{2,1,0:T(8,128)(2,1)S(1)} async-done(((bf16[32,48,256]{2,1,0:T(8,128)(2,1)}), bf16[32,48,256]{2,1,0:T(8,128)(2,1)S(1)}, u32[]{:S(2)}, u32[]{:S(2)}) %all-to-all-start.3) | async-done | bytes 786464 | tf_op jit(solution)/shard_map/all_to_all | solution.py:385
  124.4 4.2 %all-to-all-start.2 = ((bf16[32,48,256]{2,1,0:T(8,128)(2,1)}), bf16[32,48,256]{2,1,0:T(8,128)(2,1)S(1)}, u32[]{:S(2)}, u32[]{:S(2)}) async-start(bf16[32,48,256]{2,1,0:T(8,128)(2,1)} %bitcast.3), calls=%async_computation.2 | async-start | bytes 1572864 | tf_op jit(solution)/shard_map/all_to_all | solution.py:385
  128.6 2.2 %reorder_rows.3 = (bf16[48,4096]{1,0:T(8,128)(2,1)S(1)}, bf16[48,4096]{1,0:T(8,128)(2,1)S(1)}) custom-call(s32[128]{0:T(128)S(1)} %copy-done.2, bf16[32,48,256]{2,1,0:T(8,128)(2,1)S(1)} %all-to-all-done.3.x), custom_call_target="tpu_custom_call" | custom-call | bytes 2097152 | tf_op jit(solution)/shard_map/reorder_rows/pallas_call | solution.py:254
  132.1 2.0 %collective-permute-start.20 = (bf16[48,4096]{1,0:T(8,128)(2,1)S(1)}, bf16[48,4096]{1,0:T(8,128)(2,1)S(1)}, u32[]{:S(2)}, u32[]{:S(2)}) collective-permute-start(bf16[48,4096]{1,0:T(8,128)(2,1)S(1)} %get-tuple-element.58.refs_1_), channel_id=1, source_target_pairs={{0,3},{1,0},{2,1},{3,2},{4,7},{5,4},{6,5},{7,6},{8,11},{9,8},{10,9... | collective-permute-start | bytes 1179656 | tf_op jit(solution)/shard_map/ppermute | solution.py:323
  136.1 6.3 %all-to-all-done.2.x = bf16[32,48,256]{2,1,0:T(8,128)(2,1)S(1)} async-done(((bf16[32,48,256]{2,1,0:T(8,128)(2,1)}), bf16[32,48,256]{2,1,0:T(8,128)(2,1)S(1)}, u32[]{:S(2)}, u32[]{:S(2)}) %all-to-all-start.2) | async-done | bytes 786464 | tf_op jit(solution)/shard_map/all_to_all | solution.py:385
  142.4 2.2 %reorder_rows.2 = (bf16[48,4096]{1,0:T(8,128)(2,1)S(1)}, bf16[48,4096]{1,0:T(8,128)(2,1)S(1)}) custom-call(s32[128]{0:T(128)S(1)} %copy-done.2, bf16[32,48,256]{2,1,0:T(8,128)(2,1)S(1)} %all-to-all-done.2.x), custom_call_target="tpu_custom_call" | custom-call | bytes 2097152 | tf_op jit(solution)/shard_map/reorder_rows/pallas_call | solution.py:254
  145.9 2.0 %collective-permute-start.14 = (bf16[48,4096]{1,0:T(8,128)(2,1)S(1)}, bf16[48,4096]{1,0:T(8,128)(2,1)S(1)}, u32[]{:S(2)}, u32[]{:S(2)}) collective-permute-start(bf16[48,4096]{1,0:T(8,128)(2,1)S(1)} %get-tuple-element.56.refs_1_), channel_id=1, source_target_pairs={{0,3},{1,0},{2,1},{3,2},{4,7},{5,4},{6,5},{7,6},{8,11},{9,8},{10,9... | collective-permute-start | bytes 1179656 | tf_op jit(solution)/shard_map/ppermute | solution.py:323
  147.9 4.5 %collective-permute-done.19.refs_2_ = bf16[48,4096]{1,0:T(8,128)(2,1)S(1)} collective-permute-done((bf16[48,4096]{1,0:T(8,128)(2,1)S(1)}, bf16[48,4096]{1,0:T(8,128)(2,1)S(1)}, u32[]{:S(2)}, u32[]{:S(2)}) %collective-permute-start.19) | collective-permute-done | bytes 393248 | tf_op jit(solution)/shard_map/ppermute | solution.py:323
  152.5 3.2 %collective-permute-start.23 = (bf16[48,4096]{1,0:T(8,128)(2,1)S(1)}, bf16[48,4096]{1,0:T(8,128)(2,1)S(1)}, u32[]{:S(2)}, u32[]{:S(2)}) collective-permute-start(bf16[48,4096]{1,0:T(8,128)(2,1)S(1)} %collective-permute-done.20.refs_3_), channel_id=1, source_target_pairs={{0,3},{1,0},{2,1},{3,2},{4,7},{5,4},{6,5},{7,6},{8,11},{9,8},{10,9... | collective-permute-start | bytes 1179656 | tf_op jit(solution)/shard_map/ppermute | solution.py:323
  155.7 5.1 %collective-permute-done.15.refs_6_ = bf16[48,4096]{1,0:T(8,128)(2,1)S(1)} collective-permute-done((bf16[48,4096]{1,0:T(8,128)(2,1)S(1)}, bf16[48,4096]{1,0:T(8,128)(2,1)S(1)}, u32[]{:S(2)}, u32[]{:S(2)}) %collective-permute-start.15) | collective-permute-done | bytes 393248 | tf_op jit(solution)/shard_map/ppermute | solution.py:323
  161.7 7.5 %collective-permute-done.22.refs_4_ = bf16[48,4096]{1,0:T(8,128)(2,1)S(1)} collective-permute-done((bf16[48,4096]{1,0:T(8,128)(2,1)S(1)}, bf16[48,4096]{1,0:T(8,128)(2,1)S(1)}, u32[]{:S(2)}, u32[]{:S(2)}) %collective-permute-start.22) | collective-permute-done | bytes 393248 | tf_op jit(solution)/shard_map/ppermute | solution.py:323
  170.2 7.8 %back_transform.2.refs_8_ = bf16[2,1088,192]{2,1,0:T(8,128)(2,1)S(1)} custom-call(s32[8,4]{1,0:T(8,128)S(1)} %copy.20.blocks, bf16[1088,4096]{1,0:T(8,128)(2,1)} %vir.3, bf16[48,4096]{1,0:T(8,128)(2,1)S(1)} %get-tuple-element.57.refs_0_, bf16[48,4096]{1,0:T(8,128)(2,1)S(1)} %get-tuple-element.58.refs_1_, ...), custom_call_target="tpu_custom_call" | custom-call | flops 3422552064 | bytes 11534336 | tf_op jit(solution)/shard_map/back_transform/pallas_call | solution.py:303
  178.0 7.5 %collective-permute-done.16.refs_4_ = bf16[48,4096]{1,0:T(8,128)(2,1)S(1)} collective-permute-done((bf16[48,4096]{1,0:T(8,128)(2,1)S(1)}, bf16[48,4096]{1,0:T(8,128)(2,1)S(1)}, u32[]{:S(2)}, u32[]{:S(2)}) %collective-permute-start.16) | collective-permute-done | bytes 393248 | tf_op jit(solution)/shard_map/ppermute | solution.py:323
  185.5 8.9 %back_transform.3 = bf16[2,1088,384]{2,1,0:T(8,128)(2,1)} custom-call(s32[8,4]{1,0:T(8,128)S(1)} %copy.20.blocks, bf16[1088,4096]{1,0:T(8,128)(2,1)} %vir.3, bf16[48,4096]{1,0:T(8,128)(2,1)S(1)} %get-tuple-element.55.refs_0_, bf16[48,4096]{1,0:T(8,128)(2,1)S(1)} %get-tuple-element.56.refs_1_, bf16[48,4096]{1,0:T(8,128)(2,1)S(1)} %collective-permute-done.13.refs_2_, ...), custom_call_target="tpu_custom_call" | custom-call | flops 3422552064 | bytes 11534336 | tf_op jit(solution)/shard_map/back_transform/pallas_call | solution.py:303
  (75 shorter events, 29.7 us)
Async XLA Ops:
  0.0 18.1 %slice-start = ((s8[8912896]{0:T(1024)(128)(4,1)}), s8[524288]{0:T(1024)(128)(4,1)S(1)}, s32[]{:S(2)}) async-start(s8[8912896]{0:T(1024)(128)(4,1)} %bitcast.20), calls=%async_computation.4 | async-start | bytes 1048576
  2.2 16.0 %slice-start.2 = ((s8[8912896]{0:T(1024)(128)(4,1)}), s8[4194304]{0:T(1024)(128)(4,1)S(1)}, s32[]{:S(2)}) async-start(s8[8912896]{0:T(1024)(128)(4,1)} %bitcast.20), calls=%async_computation.6 | async-start | bytes 8388608
  12.8 13.3 %collective-permute-start.2 = (bf16[16,48,256]{2,1,0:T(8,128)(2,1)S(1)}, bf16[16,48,256]{2,1,0:T(8,128)(2,1)S(1)}, u32[]{:S(2)}, u32[]{:S(2)}) collective-permute-start(bf16[16,48,256]{2,1,0:T(8,128)(2,1)S(1)} %get-tuple-element.42), channel_id=1, source_target_pairs={{0,1},{1,2},{2,3},{3,0},{4,5},{5,6},{6,7},{7,4},{8,9},{9,10},{10,1... | collective-permute-start | bytes 1179656 | tf_op jit(solution)/shard_map/ppermute | solution.py:323
  14.4 12.0 %collective-permute-start.3 = (bf16[16,48,256]{2,1,0:T(8,128)(2,1)S(1)}, bf16[16,48,256]{2,1,0:T(8,128)(2,1)S(1)}, u32[]{:S(2)}, u32[]{:S(2)}) collective-permute-start(bf16[16,48,256]{2,1,0:T(8,128)(2,1)S(1)} %get-tuple-element.43), channel_id=1, source_target_pairs={{0,3},{1,0},{2,1},{3,2},{4,7},{5,4},{6,5},{7,6},{8,11},{9,8},{10,9... | collective-permute-start | bytes 1179656 | tf_op jit(solution)/shard_map/ppermute | solution.py:323
  16.1 18.8 %collective-permute-start.1 = (bf16[16,48,256]{2,1,0:T(8,128)(2,1)S(1)}, bf16[16,48,256]{2,1,0:T(8,128)(2,1)S(1)}, u32[]{:S(2)}, u32[]{:S(2)}) collective-permute-start(bf16[16,48,256]{2,1,0:T(8,128)(2,1)S(1)} %get-tuple-element.39), channel_id=1, source_target_pairs={{0,3},{1,0},{2,1},{3,2},{4,7},{5,4},{6,5},{7,6},{8,11},{9,8},{10,9... | collective-permute-start | bytes 1179656 | tf_op jit(solution)/shard_map/ppermute | solution.py:323
  17.8 18.8 %collective-permute-start = (bf16[16,48,256]{2,1,0:T(8,128)(2,1)S(1)}, bf16[16,48,256]{2,1,0:T(8,128)(2,1)S(1)}, u32[]{:S(2)}, u32[]{:S(2)}) collective-permute-start(bf16[16,48,256]{2,1,0:T(8,128)(2,1)S(1)} %get-tuple-element.35), channel_id=1, source_target_pairs={{0,1},{1,2},{2,3},{3,0},{4,5},{5,6},{6,7},{7,4},{8,9},{9,10},{10,1... | collective-permute-start | bytes 1179656 | tf_op jit(solution)/shard_map/ppermute | solution.py:323
  26.5 16.5 %collective-permute-start.4 = (bf16[16,48,256]{2,1,0:T(8,128)(2,1)S(1)}, bf16[16,48,256]{2,1,0:T(8,128)(2,1)S(1)}, u32[]{:S(2)}, u32[]{:S(2)}) collective-permute-start(bf16[16,48,256]{2,1,0:T(8,128)(2,1)S(1)} %get-tuple-element.44), channel_id=1, source_target_pairs={{0,1},{1,2},{2,3},{3,0},{4,5},{5,6},{6,7},{7,4},{8,9},{9,10},{10,1... | collective-permute-start | bytes 1179656 | tf_op jit(solution)/shard_map/ppermute | solution.py:323
  28.0 15.3 %collective-permute-start.5 = (bf16[16,48,256]{2,1,0:T(8,128)(2,1)S(1)}, bf16[16,48,256]{2,1,0:T(8,128)(2,1)S(1)}, u32[]{:S(2)}, u32[]{:S(2)}) collective-permute-start(bf16[16,48,256]{2,1,0:T(8,128)(2,1)S(1)} %get-tuple-element.45), channel_id=1, source_target_pairs={{0,3},{1,0},{2,1},{3,2},{4,7},{5,4},{6,5},{7,6},{8,11},{9,8},{10,9... | collective-permute-start | bytes 1179656 | tf_op jit(solution)/shard_map/ppermute | solution.py:323
  29.8 21.9 %collective-permute-start.9 = (bf16[16,48,256]{2,1,0:T(8,128)(2,1)S(1)}, bf16[16,48,256]{2,1,0:T(8,128)(2,1)S(1)}, u32[]{:S(2)}, u32[]{:S(2)}) collective-permute-start(bf16[16,48,256]{2,1,0:T(8,128)(2,1)S(1)} %add_convert_fusion.2), channel_id=1, source_target_pairs={{0,3},{1,0},{2,1},{3,2},{4,7},{5,4},{6,5},{7,6},{8,11},{9,8},{10,9... | collective-permute-start | bytes 1179656 | tf_op jit(solution)/shard_map/ppermute | solution.py:323
  34.9 16.9 %collective-permute-start.8 = (bf16[16,48,256]{2,1,0:T(8,128)(2,1)S(1)}, bf16[16,48,256]{2,1,0:T(8,128)(2,1)S(1)}, u32[]{:S(2)}, u32[]{:S(2)}) collective-permute-start(bf16[16,48,256]{2,1,0:T(8,128)(2,1)S(1)} %add_convert_fusion.4), channel_id=1, source_target_pairs={{0,1},{1,2},{2,3},{3,0},{4,5},{5,6},{6,7},{7,4},{8,9},{9,10},{10,1... | collective-permute-start | bytes 1179656 | tf_op jit(solution)/shard_map/ppermute | solution.py:323
  43.3 23.9 %collective-permute-start.6 = (bf16[32,48,256]{2,1,0:T(8,128)(2,1)}, bf16[32,48,256]{2,1,0:T(8,128)(2,1)}, u32[]{:S(2)}, u32[]{:S(2)}) collective-permute-start(bf16[32,48,256]{2,1,0:T(8,128)(2,1)} %pad_maximum_fusion), channel_id=1, source_target_pairs={{0,1},{1,2},{2,3},{3,0},{4,5},{5,6},{6,7},{7,4},{8,9},{9,10},{10,1... | collective-permute-start | bytes 2359304 | tf_op jit(solution)/shard_map/ppermute | solution.py:323
  44.8 22.5 %collective-permute-start.7 = (bf16[32,48,256]{2,1,0:T(8,128)(2,1)S(1)}, bf16[32,48,256]{2,1,0:T(8,128)(2,1)}, u32[]{:S(2)}, u32[]{:S(2)}) collective-permute-start(bf16[32,48,256]{2,1,0:T(8,128)(2,1)S(1)} %pad_maximum_fusion.1), channel_id=1, source_target_pairs={{0,3},{1,0},{2,1},{3,2},{4,7},{5,4},{6,5},{7,6},{8,11},{9,8},{10,9... | collective-permute-start | bytes 2359304 | tf_op jit(solution)/shard_map/ppermute | solution.py:323
  53.0 22.2 %all-to-all-start.1 = ((bf16[32,48,256]{2,1,0:T(8,128)(2,1)}), bf16[32,48,256]{2,1,0:T(8,128)(2,1)S(1)}, u32[]{:S(2)}, u32[]{:S(2)}) async-start(bf16[32,48,256]{2,1,0:T(8,128)(2,1)} %pad_maximum_fusion.2), calls=%async_computation.1 | async-start | bytes 1572864 | tf_op jit(solution)/shard_map/all_to_all | solution.py:366
  75.2 18.1 %all-to-all-start = ((bf16[32,48,256]{2,1,0:T(8,128)(2,1)}), bf16[32,48,256]{2,1,0:T(8,128)(2,1)S(1)}, u32[]{:S(2)}, u32[]{:S(2)}) async-start(bf16[32,48,256]{2,1,0:T(8,128)(2,1)} %add_convert_fusion), calls=%async_computation | async-start | bytes 1572864 | tf_op jit(solution)/shard_map/all_to_all | solution.py:366
  80.3 18.8 %copy-start.2 = (s32[128]{0:T(128)S(1)}, s32[128]{0:T(128)}, u32[]{:S(2)}) copy-start(s32[128]{0:T(128)} %owner.7) | copy-start | bytes 1540
  93.7 7.4 %collective-permute-start.10 = (bf16[256,256]{1,0:T(8,128)(2,1)S(1)}, bf16[256,256]{1,0:T(8,128)(2,1)S(1)}, u32[]{:S(2)}, u32[]{:S(2)}) collective-permute-start(bf16[256,256]{1,0:T(8,128)(2,1)S(1)} %get-tuple-element.61), channel_id=1, source_target_pairs={{0,1},{1,2},{2,3},{3,0},{4,5},{5,6},{6,7},{7,4},{8,9},{9,10},{10,1... | collective-permute-start | bytes 393224 | tf_op jit(solution)/shard_map/ppermute | solution.py:323
  95.3 9.8 %collective-permute-start.11 = (bf16[256,256]{1,0:T(8,128)(2,1)S(1)}, bf16[256,256]{1,0:T(8,128)(2,1)S(1)}, u32[]{:S(2)}, u32[]{:S(2)}) collective-permute-start(bf16[256,256]{1,0:T(8,128)(2,1)S(1)} %get-tuple-element.61), channel_id=1, source_target_pairs={{0,2},{1,3},{2,0},{3,1},{4,6},{5,7},{6,4},{7,5},{8,10},{9,11},{10,... | collective-permute-start | bytes 393224 | tf_op jit(solution)/shard_map/ppermute | solution.py:323
  98.2 6.8 %collective-permute-start.12 = (bf16[256,256]{1,0:T(8,128)(2,1)S(1)}, bf16[256,256]{1,0:T(8,128)(2,1)S(1)}, u32[]{:S(2)}, u32[]{:S(2)}) collective-permute-start(bf16[256,256]{1,0:T(8,128)(2,1)S(1)} %get-tuple-element.61), channel_id=1, source_target_pairs={{0,3},{1,0},{2,1},{3,2},{4,7},{5,4},{6,5},{7,6},{8,11},{9,8},{10,9... | collective-permute-start | bytes 393224 | tf_op jit(solution)/shard_map/ppermute | solution.py:323
  106.5 17.9 %all-to-all-start.3 = ((bf16[32,48,256]{2,1,0:T(8,128)(2,1)}), bf16[32,48,256]{2,1,0:T(8,128)(2,1)S(1)}, u32[]{:S(2)}, u32[]{:S(2)}) async-start(bf16[32,48,256]{2,1,0:T(8,128)(2,1)} %bitcast.5), calls=%async_computation.3 | async-start | bytes 1572864 | tf_op jit(solution)/shard_map/all_to_all | solution.py:385
  124.4 18.0 %all-to-all-start.2 = ((bf16[32,48,256]{2,1,0:T(8,128)(2,1)}), bf16[32,48,256]{2,1,0:T(8,128)(2,1)S(1)}, u32[]{:S(2)}, u32[]{:S(2)}) async-start(bf16[32,48,256]{2,1,0:T(8,128)(2,1)} %bitcast.3), calls=%async_computation.2 | async-start | bytes 1572864 | tf_op jit(solution)/shard_map/all_to_all | solution.py:385
  130.8 15.1 %collective-permute-start.21 = (bf16[48,4096]{1,0:T(8,128)(2,1)S(1)}, bf16[48,4096]{1,0:T(8,128)(2,1)S(1)}, u32[]{:S(2)}, u32[]{:S(2)}) collective-permute-start(bf16[48,4096]{1,0:T(8,128)(2,1)S(1)} %get-tuple-element.57.refs_0_), channel_id=1, source_target_pairs={{0,1},{1,2},{2,3},{3,0},{4,5},{5,6},{6,7},{7,4},{8,9},{9,10},{10,1... | collective-permute-start | bytes 1179656 | tf_op jit(solution)/shard_map/ppermute | solution.py:323
  132.1 15.9 %collective-permute-start.20 = (bf16[48,4096]{1,0:T(8,128)(2,1)S(1)}, bf16[48,4096]{1,0:T(8,128)(2,1)S(1)}, u32[]{:S(2)}, u32[]{:S(2)}) collective-permute-start(bf16[48,4096]{1,0:T(8,128)(2,1)S(1)} %get-tuple-element.58.refs_1_), channel_id=1, source_target_pairs={{0,3},{1,0},{2,1},{3,2},{4,7},{5,4},{6,5},{7,6},{8,11},{9,8},{10,9... | collective-permute-start | bytes 1179656 | tf_op jit(solution)/shard_map/ppermute | solution.py:323
  134.1 18.4 %collective-permute-start.19 = (bf16[48,4096]{1,0:T(8,128)(2,1)S(1)}, bf16[48,4096]{1,0:T(8,128)(2,1)S(1)}, u32[]{:S(2)}, u32[]{:S(2)}) collective-permute-start(bf16[48,4096]{1,0:T(8,128)(2,1)S(1)} %get-tuple-element.57.refs_0_), channel_id=1, source_target_pairs={{0,3},{1,0},{2,1},{3,2},{4,7},{5,4},{6,5},{7,6},{8,11},{9,8},{10,9... | collective-permute-start | bytes 1179656 | tf_op jit(solution)/shard_map/ppermute | solution.py:323
  135.0 20.7 %collective-permute-start.24 = (bf16[48,4096]{1,0:T(8,128)(2,1)S(1)}, bf16[48,4096]{1,0:T(8,128)(2,1)S(1)}, u32[]{:S(2)}, u32[]{:S(2)}) collective-permute-start(bf16[48,4096]{1,0:T(8,128)(2,1)S(1)} %get-tuple-element.58.refs_1_), channel_id=1, source_target_pairs={{0,1},{1,2},{2,3},{3,0},{4,5},{5,6},{6,7},{7,4},{8,9},{9,10},{10,1... | collective-permute-start | bytes 1179656 | tf_op jit(solution)/shard_map/ppermute | solution.py:323
  144.6 16.2 %collective-permute-start.15 = (bf16[48,4096]{1,0:T(8,128)(2,1)S(1)}, bf16[48,4096]{1,0:T(8,128)(2,1)S(1)}, u32[]{:S(2)}, u32[]{:S(2)}) collective-permute-start(bf16[48,4096]{1,0:T(8,128)(2,1)S(1)} %get-tuple-element.55.refs_0_), channel_id=1, source_target_pairs={{0,1},{1,2},{2,3},{3,0},{4,5},{5,6},{6,7},{7,4},{8,9},{9,10},{10,1... | collective-permute-start | bytes 1179656 | tf_op jit(solution)/shard_map/ppermute | solution.py:323
  145.9 15.0 %collective-permute-start.14 = (bf16[48,4096]{1,0:T(8,128)(2,1)S(1)}, bf16[48,4096]{1,0:T(8,128)(2,1)S(1)}, u32[]{:S(2)}, u32[]{:S(2)}) collective-permute-start(bf16[48,4096]{1,0:T(8,128)(2,1)S(1)} %get-tuple-element.56.refs_1_), channel_id=1, source_target_pairs={{0,3},{1,0},{2,1},{3,2},{4,7},{5,4},{6,5},{7,6},{8,11},{9,8},{10,9... | collective-permute-start | bytes 1179656 | tf_op jit(solution)/shard_map/ppermute | solution.py:323
  147.9 21.3 %collective-permute-start.22 = (bf16[48,4096]{1,0:T(8,128)(2,1)S(1)}, bf16[48,4096]{1,0:T(8,128)(2,1)S(1)}, u32[]{:S(2)}, u32[]{:S(2)}) collective-permute-start(bf16[48,4096]{1,0:T(8,128)(2,1)S(1)} %collective-permute-done.21.refs_6_), channel_id=1, source_target_pairs={{0,1},{1,2},{2,3},{3,0},{4,5},{5,6},{6,7},{7,4},{8,9},{9,10},{10,1... | collective-permute-start | bytes 1179656 | tf_op jit(solution)/shard_map/ppermute | solution.py:323
  152.5 17.7 %collective-permute-start.23 = (bf16[48,4096]{1,0:T(8,128)(2,1)S(1)}, bf16[48,4096]{1,0:T(8,128)(2,1)S(1)}, u32[]{:S(2)}, u32[]{:S(2)}) collective-permute-start(bf16[48,4096]{1,0:T(8,128)(2,1)S(1)} %collective-permute-done.20.refs_3_), channel_id=1, source_target_pairs={{0,3},{1,0},{2,1},{3,2},{4,7},{5,4},{6,5},{7,6},{8,11},{9,8},{10,9... | collective-permute-start | bytes 1179656 | tf_op jit(solution)/shard_map/ppermute | solution.py:323
  155.7 22.3 %collective-permute-start.13 = (bf16[48,4096]{1,0:T(8,128)(2,1)S(1)}, bf16[48,4096]{1,0:T(8,128)(2,1)S(1)}, u32[]{:S(2)}, u32[]{:S(2)}) collective-permute-start(bf16[48,4096]{1,0:T(8,128)(2,1)S(1)} %get-tuple-element.55.refs_0_), channel_id=1, source_target_pairs={{0,3},{1,0},{2,1},{3,2},{4,7},{5,4},{6,5},{7,6},{8,11},{9,8},{10,9... | collective-permute-start | bytes 1179656 | tf_op jit(solution)/shard_map/ppermute | solution.py:323
  160.8 17.2 %collective-permute-start.18 = (bf16[48,4096]{1,0:T(8,128)(2,1)S(1)}, bf16[48,4096]{1,0:T(8,128)(2,1)S(1)}, u32[]{:S(2)}, u32[]{:S(2)}) collective-permute-start(bf16[48,4096]{1,0:T(8,128)(2,1)S(1)} %get-tuple-element.56.refs_1_), channel_id=1, source_target_pairs={{0,1},{1,2},{2,3},{3,0},{4,5},{5,6},{6,7},{7,4},{8,9},{9,10},{10,1... | collective-permute-start | bytes 1179656 | tf_op jit(solution)/shard_map/ppermute | solution.py:323
  160.9 24.6 %collective-permute-start.16 = (bf16[48,4096]{1,0:T(8,128)(2,1)S(1)}, bf16[48,4096]{1,0:T(8,128)(2,1)S(1)}, u32[]{:S(2)}, u32[]{:S(2)}) collective-permute-start(bf16[48,4096]{1,0:T(8,128)(2,1)S(1)} %collective-permute-done.15.refs_6_), channel_id=1, source_target_pairs={{0,1},{1,2},{2,3},{3,0},{4,5},{5,6},{6,7},{7,4},{8,9},{9,10},{10,1... | collective-permute-start | bytes 1179656 | tf_op jit(solution)/shard_map/ppermute | solution.py:323
  169.3 16.2 %collective-permute-start.17 = (bf16[48,4096]{1,0:T(8,128)(2,1)S(1)}, bf16[48,4096]{1,0:T(8,128)(2,1)S(1)}, u32[]{:S(2)}, u32[]{:S(2)}) collective-permute-start(bf16[48,4096]{1,0:T(8,128)(2,1)S(1)} %collective-permute-done.14.refs_3_), channel_id=1, source_target_pairs={{0,3},{1,0},{2,1},{3,2},{4,7},{5,4},{6,5},{7,6},{8,11},{9,8},{10,9... | collective-permute-start | bytes 1179656 | tf_op jit(solution)/shard_map/ppermute | solution.py:323
  (5 other events, 36.8 us)

commit v4 on v3

v4 whole, which is shorter than its diff:
```python
import functools

import jax
import jax.numpy as jnp
from jax import lax
from jax.experimental import pallas as pl
from jax.experimental.pallas import tpu as pltpu
from jax.sharding import PartitionSpec as P

BF = jnp.bfloat16
F32 = jnp.float32
GRP = 4
MIB = 1024 * 1024
VMEM = pl.BlockSpec(memory_space=pltpu.VMEM)
ANY = pl.BlockSpec(memory_space=pl.ANY)
SMEM = pl.BlockSpec(memory_space=pltpu.SMEM)


def swapped(tile):
    return jnp.concatenate([tile[:, 64:], tile[:, :64]], axis=1)


def half_at(tile, block, place):
    return jnp.where(lax.rem(block, 2) == place, tile, swapped(tile))


def invert(owner, slot_block):
    def put(b, carry):
        slot_block[owner[b]] = b
        return carry

    lax.fori_loop(0, owner.shape[0], put, 0)


def multiply(half_rows, vir, natural):
    inner = half_rows.shape[1] // 2
    tiles = natural.shape[0] // 2
    for t in range(tiles // 2):
        panel = jnp.concatenate([v[:, t * 256 : (t + 1) * 256] for v in vir], axis=0)
        for i in range(2):
            product = jnp.dot(
                half_rows[:, i * inner : (i + 1) * inner], panel, preferred_element_type=F32
            ).astype(BF)
            for j in range(2):
                natural[i * tiles + t * 2 + j] = product[:, j * 128 : (j + 1) * 128]


def owner_order(natural, slot_block, groups, store):
    lane = lax.broadcasted_iota(jnp.int32, natural.shape[1:], 1)

    def one(g):
        for pair in range(2):
            tiles = []
            for j in range(2):
                b = slot_block[g * 4 + pair * 2 + j]
                tiles.append(half_at(natural[b // 2], b, j))
            value = jnp.where(lane < 64, tiles[0], tiles[1])
            store(g, slice(pair * 128, (pair + 1) * 128), value)

    def four(t, carry):
        for j in range(4):
            one(t * 4 + j)
        return carry

    lax.fori_loop(groups[0] // 4, groups[1] // 4, four, 0)


def far_kernel(blocks, owner, occ, ao, vir, rest, *refs, groups, quarter_shells):
    outs = refs[:4]
    tiles, vir_rows, half, half_abs, far_rows, natural, slot_block, arrived = refs[4:]
    slots, shell, _, width = ao.shape
    inner = slots * shell
    rows = width // GRP
    first_position = blocks[0, 2]
    quarter = blocks[0, 1] // quarter_shells

    copies = [pltpu.make_async_copy(ao.at[k], tiles.at[k], arrived.at[k]) for k in range(slots)]
    for k in range(slots):
        at = lax.rem(blocks[k, 1], quarter_shells) * shell
        copies.append(
            pltpu.make_async_copy(
                vir.at[pl.ds(pl.multiple_of(at, shell), shell), :],
                vir_rows.at[k],
                arrived.at[slots + k],
            )
        )
    for copy in copies:
        copy.start()
    invert(owner, slot_block)

    position = lax.broadcasted_iota(jnp.int32, (shell, width), 1) + first_position
    spread = (128, shell * shell)
    source_lane = lax.broadcasted_iota(jnp.int32, spread, 0)
    target_mu = lax.broadcasted_iota(jnp.int32, spread, 1) // shell
    row = lax.broadcasted_iota(jnp.int32, (shell, shell * shell), 0)
    column = lax.broadcasted_iota(jnp.int32, (shell, shell * shell), 1)
    diagonal = lax.rem(column, shell) == row
    per_tile = 128 // shell
    for k in range(slots):
        inside = (position >= blocks[k, 2]) & (position < blocks[k, 3])
        mu_block = blocks[k, 0]
        lanes = pl.ds(pl.multiple_of((mu_block // per_tile) * 128, 128), 128)
        pick = source_lane == target_mu + lax.rem(mu_block, per_tile) * shell
        wide = jnp.dot(
            occ[:, lanes], jnp.where(pick, 1.0, 0.0).astype(BF), preferred_element_type=F32
        )
        weights = jnp.concatenate(
            [
                jnp.where(
                    diagonal, jnp.broadcast_to(wide[i : i + 1, :], (shell, shell * shell)), 0.0
                )
                for i in range(2)
            ],
            axis=0,
        ).astype(BF)
        copies[k].wait()
        both = jnp.dot(
            weights, tiles[k].reshape(shell * shell, width), preferred_element_type=F32
        )
        for i in range(2):
            half[i, k * shell : (k + 1) * shell, :] = jnp.where(
                inside, both[i * shell : (i + 1) * shell], 0.0
            ).astype(BF)

    for i in range(2):
        half_abs[:, i * inner : (i + 1) * inner] = half[i].T
    for at, r in enumerate((2, 0, 1, 3)):
        source = lax.rem(quarter + r, GRP) * rows
        value = half_abs[pl.ds(pl.multiple_of(source, 32), rows), :]
        if r == 2:
            far_rows[...] = value
        else:
            rest[(at - 1) * rows : at * rows, :] = value
    for copy in copies[slots:]:
        copy.wait()
    multiply(far_rows, [vir_rows.at[k] for k in range(slots)], natural)
    part = groups // 4
    for p in range(4):

        def store(g, lanes, value):
            outs[p][g - p * part, :, lanes] = value

        owner_order(natural, slot_block, (p * part, (p + 1) * part), store)


def near_kernel(blocks, owner, half_rows, *refs, slots, groups):
    vir = refs[:slots]
    outs = refs[slots : slots + 10]
    natural, slot_block = refs[-2:]
    rows = half_rows.shape[0] // 3
    part = groups // 4
    invert(owner, slot_block)
    multiply(half_rows, vir, natural)
    for p in range(4):
        own, *sides = outs[p // 2 * 5 : p // 2 * 5 + 5]
        up, down = sides[p % 2], sides[2 + p % 2]

        def store(g, lanes, value):
            own[g - p // 2 * 2 * part, :, lanes] = value[:rows]
            up[g - p * part, :, lanes] = value[rows : 2 * rows]
            down[g - p * part, :, lanes] = value[2 * rows :]

        owner_order(natural, slot_block, (p * part, (p + 1) * part), store)


def partial_pieces(ao_blocks, blocks, occ_coeff, vir_coeff, owner, groups):
    slots, shell, _, width = ao_blocks.shape
    quarter, virtuals = vir_coeff.shape
    quarter_shells = quarter // shell
    inner = slots * shell
    rows = width // GRP
    near_rows = 3 * rows

    def vir_spec(k):
        return pl.BlockSpec(
            (shell, virtuals), lambda t, blk, own: (lax.rem(blk[k, 1], quarter_shells), 0)
        )

    vir_specs = [vir_spec(k) for k in range(slots)]
    full = jax.ShapeDtypeStruct((groups // 2, rows, 256), BF)
    part = jax.ShapeDtypeStruct((groups // 4, rows, 256), BF)
    rest, *far = pl.pallas_call(
        functools.partial(far_kernel, groups=groups, quarter_shells=quarter_shells),
        in_specs=[SMEM, SMEM, VMEM, ANY, ANY],
        out_specs=[VMEM] * 5,
        scratch_shapes=[
            pltpu.VMEM(ao_blocks.shape, BF),
            pltpu.VMEM((slots, shell, virtuals), BF),
            pltpu.VMEM((2, inner, width), BF),
            pltpu.VMEM((width, 2 * inner), BF),
            pltpu.VMEM((rows, 2 * inner), BF),
            pltpu.VMEM((virtuals // 64, rows, 128), BF),
            pltpu.SMEM((owner.shape[0],), jnp.int32),
            pltpu.SemaphoreType.DMA((2 * slots,)),
        ],
        out_shape=[jax.ShapeDtypeStruct((near_rows, 2 * inner), BF)] + [part] * 4,
        compiler_params=pltpu.CompilerParams(vmem_limit_bytes=52 * MIB),
        cost_estimate=pl.CostEstimate(
            flops=1024 * MIB, bytes_accessed=10 * MIB, transcendentals=0
        ),
        name="far_rows",
    )(blocks, owner, occ_coeff, ao_blocks, vir_coeff)
    near = pl.pallas_call(
        functools.partial(near_kernel, slots=slots, groups=groups),
        grid_spec=pltpu.PrefetchScalarGridSpec(
            num_scalar_prefetch=2,
            grid=(1,),
            in_specs=[VMEM] + vir_specs,
            out_specs=[VMEM] * 10,
            scratch_shapes=[
                pltpu.VMEM((virtuals // 64, near_rows, 128), BF),
                pltpu.SMEM((owner.shape[0],), jnp.int32),
            ],
        ),
        out_shape=([full] + [part] * 4) * 2,
        compiler_params=pltpu.CompilerParams(vmem_limit_bytes=32 * MIB),
        cost_estimate=pl.CostEstimate(
            flops=2 * 1024 * MIB, bytes_accessed=8 * MIB, transcendentals=0
        ),
        name="near_rows",
    )(blocks, owner, rest, *([vir_coeff] * slots))
    return far, near


def fill(owner, parts, raw, arrived, put):
    copies = []
    for r, given in enumerate(parts):
        begin = 0
        for k, part in enumerate(given):
            groups = part.shape[0]
            copies.append(
                pltpu.make_async_copy(
                    part, raw.at[r, begin : begin + groups], arrived.at[r * len(given) + k]
                )
            )
            begin += groups
    for copy in copies:
        copy.start()
    for copy in copies:
        copy.wait()
    blocks_per_occ = owner.shape[0] // 2
    lane = lax.broadcasted_iota(jnp.int32, (raw.shape[2], 128), 1)

    def one(i, t):
        found = [owner[i * blocks_per_occ + t * 2 + j] for j in range(2)]
        tiles = []
        for r in range(len(parts)):
            halves = []
            for j, d in enumerate(found):
                lanes = pl.ds(pl.multiple_of(lax.rem(d // 2, 2) * 128, 128), 128)
                halves.append(half_at(raw[r, d // 4, :, lanes], d, j))
            tiles.append(jnp.where(lane < 64, halves[0], halves[1]))
        put(i, pl.ds(pl.multiple_of(t * 128, 128), 128), tiles)

    def some(t, carry):
        for i in range(2):
            for k in range(4):
                one(i, t * 4 + k)
        return carry

    lax.fori_loop(0, blocks_per_occ // 8, some, 0)


def columns_kernel(blocks, owner, vir, *refs, quarter_shells, turns, more):
    out, raw, panel, arrived = refs[-4:]
    given = refs[: len(refs) - 4 - more]
    count = len(given) // len(turns)
    parts = [given[k * count : (k + 1) * count] for k in range(len(turns))]
    rows = raw.shape[2]
    width = len(turns) * rows
    quarter = blocks[0, 1] // quarter_shells

    @pl.when(pl.program_id(0) == 0)
    def _():
        def put(i, lanes, tiles):
            for k, tile in enumerate(tiles):
                begin = i * width + k * rows
                panel[begin : begin + rows, lanes] = tile

        fill(owner, parts, raw, arrived, put)

    both = lax.dot_general(
        vir[...], panel[...], (((1,), (1,)), ((), ())), preferred_element_type=F32
    ).astype(BF)
    source = lax.broadcasted_iota(jnp.int32, (width, out.shape[2]), 0)
    target = lax.broadcasted_iota(jnp.int32, (width, out.shape[2]), 1)
    pick = target < 0
    for k, r in enumerate(turns):
        moved = (lax.rem(quarter + r, GRP) - k) * rows
        pick = pick | ((source // rows == k) & (target == source + moved))
    pick = jnp.where(pick, 1.0, 0.0).astype(BF)
    for i in range(2):
        value = jnp.dot(
            both[:, i * width : (i + 1) * width], pick, preferred_element_type=F32
        )
        if more:
            value = value + refs[-5][i].astype(F32)
        out[i] = value.astype(BF)


def add_columns(vir, blocks, owner, shell, turns, pieces, earlier=None):
    nus, virtuals = vir.shape
    parts = [part for piece in pieces for part in piece]
    rows = parts[0].shape[1]
    groups = sum(part.shape[0] for part in pieces[0])
    tile = 272
    spec = pl.BlockSpec((2, tile, GRP * rows), lambda t: (0, t, 0))
    more = [] if earlier is None else [earlier]
    return pl.pallas_call(
        functools.partial(
            columns_kernel, quarter_shells=nus // shell, turns=turns, more=len(more)
        ),
        grid=(nus // tile,),
        in_specs=[SMEM, SMEM, pl.BlockSpec((tile, virtuals), lambda t: (t, 0))]
        + [VMEM] * len(parts)
        + [spec] * len(more),
        out_specs=spec,
        out_shape=jax.ShapeDtypeStruct((2, nus, GRP * rows), BF),
        scratch_shapes=[
            pltpu.VMEM((len(turns), groups, rows, 256), BF),
            pltpu.VMEM((2 * len(turns) * rows, virtuals), BF),
            pltpu.SemaphoreType.DMA((len(parts),)),
        ],
        compiler_params=pltpu.CompilerParams(vmem_limit_bytes=44 * MIB),
        cost_estimate=pl.CostEstimate(
            flops=4 * nus * virtuals * len(turns) * rows,
            bytes_accessed=12 * MIB,
            transcendentals=0,
        ),
        name="add_columns",
    )(blocks, owner, vir, *parts, *more)


def shift(value, by):
    return lax.ppermute(value, "grp", [(j, (j + by) % GRP) for j in range(GRP)])


def add(*terms):
    return sum(t.astype(F32) for t in terms).astype(BF)


def body(ao_blocks, blocks, occ_coeff, vir_coeff, occ_energy, vir_energy, owner):
    aux_place = lax.axis_index("aux")
    groups = lax.axis_size("aux")
    devices = groups * GRP
    virtuals = vir_coeff.shape[1]
    shell = ao_blocks.shape[1]
    block_rows = 2 * virtuals // devices
    quarter_groups = groups // 4
    far, near = partial_pieces(ao_blocks, blocks, occ_coeff, vir_coeff, owner, groups)

    own_a, up_low_a, up_high_a, down_low_a, down_high_a = near[:5]
    own_b, up_low_b, up_high_b, down_low_b, down_high_b = near[5:]
    relay_up, relay_down = shift(far[0], 1), shift(far[1], -1)
    relay_up_b, relay_down_b = shift(far[2], 1), shift(far[3], -1)
    up_high_a, down_low_a, relay_up, relay_down = lax.optimization_barrier(
        (up_high_a, down_low_a, relay_up, relay_down)
    )
    up_high_a, down_low_a = shift(up_high_a, 1), shift(down_low_a, -1)
    up_low_a = shift(add(up_low_a, relay_up), 1)
    down_high_a = shift(add(down_high_a, relay_down), -1)
    up_b = jnp.concatenate([add(up_low_b, relay_up_b), up_high_b], axis=0)
    down_b = jnp.concatenate([down_low_b, add(down_high_b, relay_down_b)], axis=0)
    up_b, down_b, up_high_a, down_low_a = lax.optimization_barrier(
        (up_b, down_b, up_high_a, down_low_a)
    )
    up_b, down_b = shift(up_b, 1), shift(down_b, -1)
    totals = [
        jnp.concatenate(
            [add(own_a[:quarter_groups], up_low_a, down_low_a),
                add(own_a[quarter_groups:], up_high_a, down_high_a),
            ],
            axis=0,
        ),
        add(own_b, up_b, down_b),
    ]
    def tie(values, *others):
        return list(lax.optimization_barrier((*values, *others)))[: len(values)]

    chips = groups // 2
    same_core = [[2 * j + core for j in range(chips)] for core in range(2)]

    def exchange(value):
        return lax.all_to_all(
            value, "aux", split_axis=0, concat_axis=0, axis_index_groups=same_core, tiled=True
        )

    pair_energy = (occ_energy[:, None] - vir_energy[None, :]).reshape(devices, block_rows)

    def amplitude_of(rows, h):
        members = (h * chips + aux_place // 2) * GRP + jnp.arange(GRP, dtype=jnp.int32)
        picked = owner[None, :] == members[:, None]
        energy = jnp.sum(jnp.where(picked[:, :, None], pair_energy[None], 0.0), axis=1).reshape(-1)
        scores = lax.dot_general(rows, rows, (((0,), (0,)), ((), ())), preferred_element_type=F32)
        scores = scores + lax.ppermute(scores, "aux", [(j, j ^ 1) for j in range(groups)])
        sent = scores.astype(BF)
        others = [shift(sent, by) for by in (1, 2, 3)]
        scores = scores + sum(other.astype(F32) for other in others)
        return (scores / (energy[:, None] + energy[None, :])).astype(BF)

    def density_of(rows, amplitude):
        density = jnp.dot(rows, amplitude, preferred_element_type=F32).astype(BF)
        return density.reshape(chips, -1, 4 * block_rows)

    def to_neighbours(own):
        parts = own[:quarter_groups], own[quarter_groups:]
        below = [shift(part, 1) for part in parts]
        above = [shift(part, -1) for part in parts]
        return parts, below, above

    rows_a = exchange(totals[0]).reshape(-1, 4 * block_rows)
    amplitude_a = amplitude_of(rows_a, 0)
    rows_b = exchange(totals[1]).reshape(-1, 4 * block_rows)
    rows_a, rows_b = tie((rows_a, rows_b))
    own_a, below_a, above_a = to_neighbours(exchange(density_of(rows_a, amplitude_a)))
    amplitude_b = amplitude_of(rows_b, 1)
    own_b, below_b, above_b = to_neighbours(exchange(density_of(rows_b, amplitude_b)))
    put = functools.partial(add_columns, vir_coeff, blocks, owner, shell)
    result = put((0,), [[*own_a, *own_b]])
    first, second, result = tie((below_a[0], above_a[1], result))
    far_a = [shift(first, 1), shift(second, -1)]
    far_b = [shift(below_b[0], 1), shift(above_b[1], -1)]
    result = put((1, 3), [[*above_a, *above_b], [*below_a, *below_b]], result)
    return put((2,), [[*far_a, *far_b]], result)


def solution(mesh):
    return jax.shard_map(
        body,
        mesh=mesh,
        in_specs=(
            P(("aux", "grp"), None, None, None),
            P(("aux", "grp"), None),
            P(),
            P("grp", None),
            P(),
            P(),
            P(),
        ),
        out_specs=P(None, "grp", "aux"),
        check_vma=False,
    )
```

time: 195 us -> 181 us (0.928)
  waiting for transfers between devices: 88.8 us -> 53.8 us
  starting transfers between devices: 55.1 us -> 66.3 us
  Pallas kernels: 38.6 us -> 48 us
    ppermute x25 -> x28, waiting for transfers between devices: 51.6 us -> 33.2 us  [shift(): return lax.ppermute(value, 'grp', [(j, (j + by) % GRP) for j in range(GRP)])]
    all_to_all x4, waiting for transfers between devices: 37.2 us -> 19.4 us  [exchange(): lax.all_to_all(value, 'aux', split_axis=0, concat_axis=0, axis_index_grou...]
    pallas_call x5 -> x4, Pallas kernels: 31.6 us -> 41.6 us  [the longest x3 34.7 us: add_columns(): pl.pallas_call(functools.partial(columns_kernel, quarter_shells=nus // sh...]
    ppermute x25 -> x28, starting transfers between devices: 34.2 us -> 43.2 us  [shift(): return lax.ppermute(value, 'grp', [(j, (j + by) % GRP) for j in range(GRP)])]
    all_to_all x4, starting transfers between devices: 20.8 us -> 23 us  [exchange(): lax.all_to_all(value, 'aux', split_axis=0, concat_axis=0, axis_index_grou...]
  transfers between devices with their start and end apart: 29 -> 34, of which waited for: 18 -> 18; matrix products, arithmetic and copies ran while one was open for 4% -> 5% of each run, Pallas kernels for 10% -> 17%
where the time goes in v4:
time: 181 us; the launch traced here: 180 us
  starting transfers between devices  66.3 us (37%)
  waiting for transfers between devices  53.8 us (30%)
  Pallas kernels  48 us (27%)
  other arithmetic  4.84 us (3%)
  matrix products  3.49 us (2%)
  local copies, waits for them, and re-layouts  2.85 us (2%)
    ppermute x28, starting transfers between devices, shift(): return lax.ppermute(value, 'grp', [(j, (j + by) % GRP) for j in range(GRP)])  43.2 us
    pallas_call x3, Pallas kernels, add_columns(): pl.pallas_call(functools.partial(columns_kernel, quarter_shells=nus // sh...  34.7 us
    ppermute x28, waiting for transfers between devices, shift(): return lax.ppermute(value, 'grp', [(j, (j + by) % GRP) for j in range(GRP)])  33.2 us
    all_to_all x4, starting transfers between devices, exchange(): lax.all_to_all(value, 'aux', split_axis=0, concat_axis=0, axis_index_grou...  23 us
    all_to_all x4, waiting for transfers between devices, exchange(): lax.all_to_all(value, 'aux', split_axis=0, concat_axis=0, axis_index_grou...  19.4 us
    pallas_call x1, Pallas kernels, partial_pieces(): pl.pallas_call(functools.partial(far_kernel, groups=groups, quarter_shell...  6.94 us
    pallas_call x1, Pallas kernels, partial_pieces(): pl.pallas_call(functools.partial(near_kernel, slots=slots, groups=groups)...  6.35 us
  transfers between devices with their start and end apart: 34, of which 18 were waited for; matrix products, arithmetic and copies ran while one was open for 5% of the time, Pallas kernels for 17%

profile of v4, /device:TPU:0, one launch (start us, length us, event | category | flops | bytes accessed | tf_op | source)
XLA Modules:
  0.0 179.8 jit_solution(10025003934003073621)
XLA Ops:
  2.1 6.9 %far_rows.1 = (bf16[288,512]{1,0:T(8,128)(2,1)S(1)}, bf16[8,96,256]{2,1,0:T(8,128)(2,1)S(1)}, bf16[8,96,256]{2,1,0:T(8,128)(2,1)S(1)}, bf16[8,96,256]{2,1,0:T(8,128)(2,1)S(1)}, bf16[8,96,256]{2,1,0:T(8,128)(2,1)S(1)}) custom-call(s32[8,4]{1,0:T(8,128)S(1)} %copy.23.blocks, s32[128]{0:T(128)S(1)} %copy-done.1, bf16[2,4352]{1,0:T(2,128)(2,1)S(1)} %copy-done.3, ...), custom_call_target="tpu_custom_call" | custom-call | flops 1073741824 | bytes 10485760 | tf_op jit(solution)/shard_map/far_rows/pallas_call | solution.py:182
  9.1 1.6 collective-permute-start
  10.7 1.7 collective-permute-start.1
  12.4 1.6 collective-permute-start.4
  14.4 6.4 %near_rows.1 = (bf16[16,96,256]{2,1,0:T(8,128)(2,1)S(1)}, bf16[8,96,256]{2,1,0:T(8,128)(2,1)S(1)}, bf16[8,96,256]{2,1,0:T(8,128)(2,1)S(1)}, bf16[8,96,256]{2,1,0...) custom-call(s32[8,4]{1,0:T(8,128)S(1)} %copy.23.blocks, ...), custom_call_target="tpu_custom_call" | custom-call | flops 2147483648 | bytes 8388608 | tf_op jit(solution)/shard_map/near_rows/pallas_call | solution.py:203
  24.3 1.7 collective-permute-start.6
  26.1 1.7 collective-permute-start.7
  28.0 3.2 %collective-permute-done.4 = bf16[8,96,256]{2,1,0:T(8,128)(2,1)S(1)} collective-permute-done((bf16[8,96,256]{2,1,0:T(8,128)(2,1)S(1)}, bf16[8,96,256]{2,1,0:T(8,128)(2,1)S(1)}, u32[]{:S(2)}, u32[]{:S(2)}) %collective-permute-start.4) | collective-permute-done | bytes 393248 | tf_op jit(solution)/shard_map/ppermute | solution.py:335
  33.1 6.2 %collective-permute-done.5 = bf16[8,96,256]{2,1,0:T(8,128)(2,1)S(1)} collective-permute-done((bf16[8,96,256]{2,1,0:T(8,128)(2,1)S(1)}, bf16[8,96,256]{2,1,0:T(8,128)(2,1)S(1)}, u32[]{:S(2)}, u32[]{:S(2)}) %collective-permute-start.5) | collective-permute-done | bytes 393248 | tf_op jit(solution)/shard_map/ppermute | solution.py:335
  41.1 1.7 collective-permute-start.9
  42.9 5.2 %collective-permute-done.7 = bf16[8,96,256]{2,1,0:T(8,128)(2,1)S(1)} collective-permute-done((bf16[8,96,256]{2,1,0:T(8,128)(2,1)S(1)}, bf16[8,96,256]{2,1,0:T(8,128)(2,1)S(1)}, u32[]{:S(2)}, u32[]{:S(2)}) %collective-permute-start.7) | collective-permute-done | bytes 393248 | tf_op jit(solution)/shard_map/ppermute | solution.py:335
  49.4 8.1 %all-to-all-start = ((bf16[16,96,256]{2,1,0:T(8,128)(2,1)}), bf16[16,96,256]{2,1,0:T(8,128)(2,1)S(1)}, u32[]{:S(2)}, u32[]{:S(2)}) async-start(bf16[16,96,256]{2,1,0:T(8,128)(2,1)} %pad_maximum_fusion.2), calls=%async_computation | async-start | bytes 1572864 | tf_op jit(solution)/shard_map/all_to_all | solution.py:384
  58.0 5.4 %collective-permute-done.8 = bf16[16,96,256]{2,1,0:T(8,128)(2,1)} collective-permute-done((bf16[16,96,256]{2,1,0:T(8,128)(2,1)S(1)}, bf16[16,96,256]{2,1,0:T(8,128)(2,1)}, u32[]{:S(2)}, u32[]{:S(2)}) %collective-permute-start.8) | collective-permute-done | bytes 786464 | tf_op jit(solution)/shard_map/ppermute | solution.py:335
  63.5 2.6 %add_convert_fusion = bf16[16,96,256]{2,1,0:T(8,128)(2,1)} fusion(bf16[16,96,256]{2,1,0:T(8,128)(2,1)} %collective-permute-done.9, bf16[16,96,256]{2,1,0:T(8,128)(2,1)} %collective-permute-done.8, bf16[16,96,256]{2,1,0:T(8,128)(2,1)S(1)} %get-tuple-element.53), kind=kLoop, calls=%fused_computation.2 | loop fusion | flops 2359296 | bytes 3145728 | tf_op jit(solution)/shard_map/convert_element_type | solution.py:339
  66.2 3.2 %all-to-all-done = bf16[16,96,256]{2,1,0:T(8,128)(2,1)S(1)} async-done(((bf16[16,96,256]{2,1,0:T(8,128)(2,1)}), bf16[16,96,256]{2,1,0:T(8,128)(2,1)S(1)}, u32[]{:S(2)}, u32[]{:S(2)}) %all-to-all-start) | async-done | bytes 786464 | tf_op jit(solution)/shard_map/all_to_all | solution.py:384
  69.4 4.9 %all-to-all-start.1 = ((bf16[16,96,256]{2,1,0:T(8,128)(2,1)}), bf16[16,96,256]{2,1,0:T(8,128)(2,1)S(1)}, u32[]{:S(2)}, u32[]{:S(2)}) async-start(bf16[16,96,256]{2,1,0:T(8,128)(2,1)} %add_convert_fusion), calls=%async_computation.1 | async-start | bytes 1572864 | tf_op jit(solution)/shard_map/all_to_all | solution.py:384
  78.0 2.9 %collective-permute-start.12 = (bf16[256,256]{1,0:T(8,128)(2,1)S(1)}, bf16[256,256]{1,0:T(8,128)(2,1)S(1)}, u32[]{:S(2)}, u32[]{:S(2)}) collective-permute-start(bf16[256,256]{1,0:T(8,128)(2,1)S(1)} %get-tuple-element.65), channel_id=1, source_target_pairs={{0,2},{1,3},{2,0},{3,1},{4,6},{5,7},{6,4},{7,5},{8,10},{9,11},{10,... | collective-permute-start | bytes 393224 | tf_op jit(solution)/shard_map/ppermute | solution.py:335
  81.9 5.9 %all-to-all-done.1 = bf16[16,96,256]{2,1,0:T(8,128)(2,1)S(1)} async-done(((bf16[16,96,256]{2,1,0:T(8,128)(2,1)}), bf16[16,96,256]{2,1,0:T(8,128)(2,1)S(1)}, u32[]{:S(2)}, u32[]{:S(2)}) %all-to-all-start.1) | async-done | bytes 786464 | tf_op jit(solution)/shard_map/all_to_all | solution.py:384
  89.7 6.1 %all-to-all-start.2 = ((bf16[16,96,256]{2,1,0:T(8,128)(2,1)}), bf16[16,96,256]{2,1,0:T(8,128)(2,1)S(1)}, u32[]{:S(2)}, u32[]{:S(2)}) async-start(bf16[16,96,256]{2,1,0:T(8,128)(2,1)} %bitcast.3), calls=%async_computation.2 | async-start | bytes 1572864 | tf_op jit(solution)/shard_map/all_to_all | solution.py:384
  97.2 2.4 %collective-permute-start.18 = (bf16[256,256]{1,0:T(8,128)(2,1)S(1)}, bf16[256,256]{1,0:T(8,128)(2,1)S(1)}, u32[]{:S(2)}, u32[]{:S(2)}) collective-permute-start(bf16[256,256]{1,0:T(8,128)(2,1)S(1)} %get-tuple-element.63), channel_id=1, source_target_pairs={{0,2},{1,3},{2,0},{3,1},{4,6},{5,7},{6,4},{7,5},{8,10},{9,11},{10,... | collective-permute-start | bytes 393224 | tf_op jit(solution)/shard_map/ppermute | solution.py:335
  100.8 2.7 %collective-permute-done.17 = bf16[256,256]{1,0:T(8,128)(2,1)S(1)} collective-permute-done((bf16[256,256]{1,0:T(8,128)(2,1)S(1)}, bf16[256,256]{1,0:T(8,128)(2,1)S(1)}, u32[]{:S(2)}, u32[]{:S(2)}) %collective-permute-start.17) | collective-permute-done | bytes 131104 | tf_op jit(solution)/shard_map/ppermute | solution.py:335
  106.5 3.1 %all-to-all-done.2 = bf16[16,96,256]{2,1,0:T(8,128)(2,1)S(1)} async-done(((bf16[16,96,256]{2,1,0:T(8,128)(2,1)}), bf16[16,96,256]{2,1,0:T(8,128)(2,1)S(1)}, u32[]{:S(2)}, u32[]{:S(2)}) %all-to-all-start.2) | async-done | bytes 786464 | tf_op jit(solution)/shard_map/all_to_all | solution.py:384
  109.6 3.8 %all-to-all-start.3 = ((bf16[16,96,256]{2,1,0:T(8,128)(2,1)}), bf16[16,96,256]{2,1,0:T(8,128)(2,1)S(1)}, u32[]{:S(2)}, u32[]{:S(2)}) async-start(bf16[16,96,256]{2,1,0:T(8,128)(2,1)} %bitcast.4), calls=%async_computation.3 | async-start | bytes 1572864 | tf_op jit(solution)/shard_map/all_to_all | solution.py:384
  114.9 1.9 %collective-permute-start.15 = (bf16[8,96,256]{2,1,0:T(8,128)(2,1)S(1)}, bf16[8,96,256]{2,1,0:T(8,128)(2,1)S(1)}, u32[]{:S(2)}, u32[]{:S(2)}) collective-permute-start(bf16[8,96,256]{2,1,0:T(8,128)(2,1)S(1)} %get-tuple-element.69.refs_1_), channel_id=1, source_target_pairs={{0,3},{1,0},{2,1},{3,2},{4,7},{5,4},{6,5},{7,6},{8,11},{9,8},{10,9... | collective-permute-start | bytes 1179656 | tf_op jit(solution)/shard_map/ppermute | solution.py:335
  118.8 7.1 %all-to-all-done.3 = bf16[16,96,256]{2,1,0:T(8,128)(2,1)S(1)} async-done(((bf16[16,96,256]{2,1,0:T(8,128)(2,1)}), bf16[16,96,256]{2,1,0:T(8,128)(2,1)S(1)}, u32[]{:S(2)}, u32[]{:S(2)}) %all-to-all-start.3) | async-done | bytes 786464 | tf_op jit(solution)/shard_map/all_to_all | solution.py:384
  126.0 1.8 %collective-permute-start.22 = (bf16[8,96,256]{2,1,0:T(8,128)(2,1)S(1)}, bf16[8,96,256]{2,1,0:T(8,128)(2,1)S(1)}, u32[]{:S(2)}, u32[]{:S(2)}) collective-permute-start(bf16[8,96,256]{2,1,0:T(8,128)(2,1)S(1)} %get-tuple-element.68.refs_2_), channel_id=1, source_target_pairs={{0,1},{1,2},{2,3},{3,0},{4,5},{5,6},{6,7},{7,4},{8,9},{9,10},{10,1... | collective-permute-start | bytes 1179656 | tf_op jit(solution)/shard_map/ppermute | solution.py:335
  130.7 4.7 %collective-permute-done.26.refs_0_ = bf16[8,96,256]{2,1,0:T(8,128)(2,1)S(1)} collective-permute-done((bf16[8,96,256]{2,1,0:T(8,128)(2,1)S(1)}, bf16[8,96,256]{2,1,0:T(8,128)(2,1)S(1)}, u32[]{:S(2)}, u32[]{:S(2)}) %collective-permute-start.26) | collective-permute-done | bytes 393248 | tf_op jit(solution)/shard_map/ppermute | solution.py:335
  136.1 10.5 %add_columns.3.refs_8_ = bf16[2,1088,384]{2,1,0:T(8,128)(2,1)S(1)} custom-call(s32[8,4]{1,0:T(8,128)S(1)} %copy.23.blocks, s32[128]{0:T(128)S(1)} %copy-done.2, bf16[1088,4096]{1,0:T(8,128)(2,1)} %vir.7, bf16[8,96,256]{2,1,0:T(8,128)(2,1)S(1)} %get-tuple-element.70.refs_0_, bf16[8,96,256]{2,1,0:T(8,128)(2,1)S(1)} %get-tuple-element.69.refs_1_, ...), custom_call_target="tpu_custom_call" | custom-call | flops 1711276032 | bytes 12582912 | tf_op jit(solution)/shard_map/add_columns/pallas_call | solution.py:309
  146.6 2.1 %collective-permute-start.20 = (bf16[8,96,256]{2,1,0:T(8,128)(2,1)S(1)}, bf16[8,96,256]{2,1,0:T(8,128)(2,1)S(1)}, u32[]{:S(2)}, u32[]{:S(2)}) collective-permute-start(bf16[8,96,256]{2,1,0:T(8,128)(2,1)S(1)} %collective-permute-done.14.refs_4_), channel_id=1, source_target_pairs={{0,1},{1,2},{2,3},{3,0},{4,5},{5,6},{6,7},{7,4},{8,9},{9,10},{10,1... | collective-permute-start | bytes 1179656 | tf_op jit(solution)/shard_map/ppermute | solution.py:335
  152.3 3.1 %collective-permute-start.25 = (bf16[8,96,256]{2,1,0:T(8,128)(2,1)S(1)}, bf16[8,96,256]{2,1,0:T(8,128)(2,1)S(1)}, u32[]{:S(2)}, u32[]{:S(2)}) collective-permute-start(bf16[8,96,256]{2,1,0:T(8,128)(2,1)S(1)} %collective-permute-done.24.refs_3_), channel_id=1, source_target_pairs={{0,3},{1,0},{2,1},{3,2},{4,7},{5,4},{6,5},{7,6},{8,11},{9,8},{10,9... | collective-permute-start | bytes 1179656 | tf_op jit(solution)/shard_map/ppermute | solution.py:335
  155.3 12.9 %add_columns.4.refs_4_ = bf16[2,1088,384]{2,1,0:T(8,128)(2,1)S(1)} custom-call(s32[8,4]{1,0:T(8,128)S(1)} %copy.23.blocks, s32[128]{0:T(128)S(1)} %copy-done.2, bf16[1088,4096]{1,0:T(8,128)(2,1)} %vir.7, bf16[8,96,256]{2,1,0:T(8,128)(2,1)S(1)} %collective-permute-done.26.refs_0_, bf16[8,96,256]{2,1,0:T(8,128)(2,1)S(1)} %collective-permute-done.15.refs_1_, ...), custom_call_target="tpu_custom_call" | custom-call | flops 3422552064 | bytes 12582912 | tf_op jit(solution)/shard_map/add_columns/pallas_call | solution.py:309
  168.3 11.4 %add_columns.5 = bf16[2,1088,384]{2,1,0:T(8,128)(2,1)} custom-call(s32[8,4]{1,0:T(8,128)S(1)} %copy.23.blocks, s32[128]{0:T(128)S(1)} %copy-done.2, bf16[1088,4096]{1,0:T(8,128)(2,1)} %vir.7, bf16[8,96,256]{2,1,0:T(8,128)(2,1)S(1)} %collective-permute-done.20.refs_0_, bf16[8,96,256]{2,1,0:T(8,128)(2,1)S(1)} %collective-permute-done.21.refs_1_, ...), custom_call_target="tpu_custom_call" | custom-call | flops 1711276032 | bytes 12582912 | tf_op jit(solution)/shard_map/add_columns/pallas_call | solution.py:309
  (83 shorter events, 34.6 us)
Async XLA Ops:
  9.1 13.3 %collective-permute-start = (bf16[8,96,256]{2,1,0:T(8,128)(2,1)S(1)}, bf16[8,96,256]{2,1,0:T(8,128)(2,1)S(1)}, u32[]{:S(2)}, u32[]{:S(2)}) collective-permute-start(bf16[8,96,256]{2,1,0:T(8,128)(2,1)S(1)} %get-tuple-element.38), channel_id=1, source_target_pairs={{0,1},{1,2},{2,3},{3,0},{4,5},{5,6},{6,7},{7,4},{8,9},{9,10},{10,1... | collective-permute-start | bytes 1179656 | tf_op jit(solution)/shard_map/ppermute | solution.py:335
  10.7 12.0 %collective-permute-start.1 = (bf16[8,96,256]{2,1,0:T(8,128)(2,1)S(1)}, bf16[8,96,256]{2,1,0:T(8,128)(2,1)S(1)}, u32[]{:S(2)}, u32[]{:S(2)}) collective-permute-start(bf16[8,96,256]{2,1,0:T(8,128)(2,1)S(1)} %get-tuple-element.39), channel_id=1, source_target_pairs={{0,3},{1,0},{2,1},{3,2},{4,7},{5,4},{6,5},{7,6},{8,11},{9,8},{10,9... | collective-permute-start | bytes 1179656 | tf_op jit(solution)/shard_map/ppermute | solution.py:335
  12.4 18.8 %collective-permute-start.4 = (bf16[8,96,256]{2,1,0:T(8,128)(2,1)S(1)}, bf16[8,96,256]{2,1,0:T(8,128)(2,1)S(1)}, u32[]{:S(2)}, u32[]{:S(2)}) collective-permute-start(bf16[8,96,256]{2,1,0:T(8,128)(2,1)S(1)} %get-tuple-element.46), channel_id=1, source_target_pairs={{0,3},{1,0},{2,1},{3,2},{4,7},{5,4},{6,5},{7,6},{8,11},{9,8},{10,9... | collective-permute-start | bytes 1179656 | tf_op jit(solution)/shard_map/ppermute | solution.py:335
  14.0 18.9 %collective-permute-start.3 = (bf16[8,96,256]{2,1,0:T(8,128)(2,1)S(1)}, bf16[8,96,256]{2,1,0:T(8,128)(2,1)S(1)}, u32[]{:S(2)}, u32[]{:S(2)}) collective-permute-start(bf16[8,96,256]{2,1,0:T(8,128)(2,1)S(1)} %get-tuple-element.42), channel_id=1, source_target_pairs={{0,1},{1,2},{2,3},{3,0},{4,5},{5,6},{6,7},{7,4},{8,9},{9,10},{10,1... | collective-permute-start | bytes 1179656 | tf_op jit(solution)/shard_map/ppermute | solution.py:335
  22.8 16.5 %collective-permute-start.5 = (bf16[8,96,256]{2,1,0:T(8,128)(2,1)S(1)}, bf16[8,96,256]{2,1,0:T(8,128)(2,1)S(1)}, u32[]{:S(2)}, u32[]{:S(2)}) collective-permute-start(bf16[8,96,256]{2,1,0:T(8,128)(2,1)S(1)} %get-tuple-element.47), channel_id=1, source_target_pairs={{0,1},{1,2},{2,3},{3,0},{4,5},{5,6},{6,7},{7,4},{8,9},{9,10},{10,1... | collective-permute-start | bytes 1179656 | tf_op jit(solution)/shard_map/ppermute | solution.py:335
  24.3 15.4 %collective-permute-start.6 = (bf16[8,96,256]{2,1,0:T(8,128)(2,1)S(1)}, bf16[8,96,256]{2,1,0:T(8,128)(2,1)S(1)}, u32[]{:S(2)}, u32[]{:S(2)}) collective-permute-start(bf16[8,96,256]{2,1,0:T(8,128)(2,1)S(1)} %get-tuple-element.48), channel_id=1, source_target_pairs={{0,3},{1,0},{2,1},{3,2},{4,7},{5,4},{6,5},{7,6},{8,11},{9,8},{10,9... | collective-permute-start | bytes 1179656 | tf_op jit(solution)/shard_map/ppermute | solution.py:335
  26.1 21.9 %collective-permute-start.7 = (bf16[8,96,256]{2,1,0:T(8,128)(2,1)S(1)}, bf16[8,96,256]{2,1,0:T(8,128)(2,1)S(1)}, u32[]{:S(2)}, u32[]{:S(2)}) collective-permute-start(bf16[8,96,256]{2,1,0:T(8,128)(2,1)S(1)} %add_convert_fusion.2), channel_id=1, source_target_pairs={{0,3},{1,0},{2,1},{3,2},{4,7},{5,4},{6,5},{7,6},{8,11},{9,8},{10,9... | collective-permute-start | bytes 1179656 | tf_op jit(solution)/shard_map/ppermute | solution.py:335
  31.2 16.9 %collective-permute-start.2 = (bf16[8,96,256]{2,1,0:T(8,128)(2,1)S(1)}, bf16[8,96,256]{2,1,0:T(8,128)(2,1)S(1)}, u32[]{:S(2)}, u32[]{:S(2)}) collective-permute-start(bf16[8,96,256]{2,1,0:T(8,128)(2,1)S(1)} %add_convert_fusion.6), channel_id=1, source_target_pairs={{0,1},{1,2},{2,3},{3,0},{4,5},{5,6},{6,7},{7,4},{8,9},{9,10},{10,1... | collective-permute-start | bytes 1179656 | tf_op jit(solution)/shard_map/ppermute | solution.py:335
  39.6 23.7 %collective-permute-start.8 = (bf16[16,96,256]{2,1,0:T(8,128)(2,1)S(1)}, bf16[16,96,256]{2,1,0:T(8,128)(2,1)}, u32[]{:S(2)}, u32[]{:S(2)}) collective-permute-start(bf16[16,96,256]{2,1,0:T(8,128)(2,1)S(1)} %pad_maximum_fusion), channel_id=1, source_target_pairs={{0,1},{1,2},{2,3},{3,0},{4,5},{5,6},{6,7},{7,4},{8,9},{9,10},{10,1... | collective-permute-start | bytes 2359304 | tf_op jit(solution)/shard_map/ppermute | solution.py:335
  41.1 22.4 %collective-permute-start.9 = (bf16[16,96,256]{2,1,0:T(8,128)(2,1)S(1)}, bf16[16,96,256]{2,1,0:T(8,128)(2,1)}, u32[]{:S(2)}, u32[]{:S(2)}) collective-permute-start(bf16[16,96,256]{2,1,0:T(8,128)(2,1)S(1)} %pad_maximum_fusion.1), channel_id=1, source_target_pairs={{0,3},{1,0},{2,1},{3,2},{4,7},{5,4},{6,5},{7,6},{8,11},{9,8},{10,9... | collective-permute-start | bytes 2359304 | tf_op jit(solution)/shard_map/ppermute | solution.py:335
  49.4 20.0 %all-to-all-start = ((bf16[16,96,256]{2,1,0:T(8,128)(2,1)}), bf16[16,96,256]{2,1,0:T(8,128)(2,1)S(1)}, u32[]{:S(2)}, u32[]{:S(2)}) async-start(bf16[16,96,256]{2,1,0:T(8,128)(2,1)} %pad_maximum_fusion.2), calls=%async_computation | async-start | bytes 1572864 | tf_op jit(solution)/shard_map/all_to_all | solution.py:384
  69.4 18.4 %all-to-all-start.1 = ((bf16[16,96,256]{2,1,0:T(8,128)(2,1)}), bf16[16,96,256]{2,1,0:T(8,128)(2,1)S(1)}, u32[]{:S(2)}, u32[]{:S(2)}) async-start(bf16[16,96,256]{2,1,0:T(8,128)(2,1)} %add_convert_fusion), calls=%async_computation.1 | async-start | bytes 1572864 | tf_op jit(solution)/shard_map/all_to_all | solution.py:384
  76.4 11.9 %collective-permute-start.11 = (bf16[256,256]{1,0:T(8,128)(2,1)S(1)}, bf16[256,256]{1,0:T(8,128)(2,1)S(1)}, u32[]{:S(2)}, u32[]{:S(2)}) collective-permute-start(bf16[256,256]{1,0:T(8,128)(2,1)S(1)} %get-tuple-element.65), channel_id=1, source_target_pairs={{0,1},{1,2},{2,3},{3,0},{4,5},{5,6},{6,7},{7,4},{8,9},{9,10},{10,1... | collective-permute-start | bytes 393224 | tf_op jit(solution)/shard_map/ppermute | solution.py:335
  78.0 10.3 %collective-permute-start.12 = (bf16[256,256]{1,0:T(8,128)(2,1)S(1)}, bf16[256,256]{1,0:T(8,128)(2,1)S(1)}, u32[]{:S(2)}, u32[]{:S(2)}) collective-permute-start(bf16[256,256]{1,0:T(8,128)(2,1)S(1)} %get-tuple-element.65), channel_id=1, source_target_pairs={{0,2},{1,3},{2,0},{3,1},{4,6},{5,7},{6,4},{7,5},{8,10},{9,11},{10,... | collective-permute-start | bytes 393224 | tf_op jit(solution)/shard_map/ppermute | solution.py:335
  80.9 7.4 %collective-permute-start.13 = (bf16[256,256]{1,0:T(8,128)(2,1)S(1)}, bf16[256,256]{1,0:T(8,128)(2,1)S(1)}, u32[]{:S(2)}, u32[]{:S(2)}) collective-permute-start(bf16[256,256]{1,0:T(8,128)(2,1)S(1)} %get-tuple-element.65), channel_id=1, source_target_pairs={{0,3},{1,0},{2,1},{3,2},{4,7},{5,4},{6,5},{7,6},{8,11},{9,8},{10,9... | collective-permute-start | bytes 393224 | tf_op jit(solution)/shard_map/ppermute | solution.py:335
  88.2 7.6 %collective-permute-start.16 = (f32[256,256]{1,0:T(8,128)S(1)}, f32[256,256]{1,0:T(8,128)S(1)}, u32[]{:S(2)}, u32[]{:S(2)}) collective-permute-start(f32[256,256]{1,0:T(8,128)S(1)} %fusion.8), channel_id=1, source_target_pairs={{0,4},{4,0},{8,12},{12,8},{16,20},{20,16},{24,28},{28,24},{32,36},... | collective-permute-start | bytes 786440 | tf_op jit(solution)/shard_map/ppermute | solution.py:395
  89.7 19.9 %all-to-all-start.2 = ((bf16[16,96,256]{2,1,0:T(8,128)(2,1)}), bf16[16,96,256]{2,1,0:T(8,128)(2,1)S(1)}, u32[]{:S(2)}, u32[]{:S(2)}) async-start(bf16[16,96,256]{2,1,0:T(8,128)(2,1)} %bitcast.3), calls=%async_computation.2 | async-start | bytes 1572864 | tf_op jit(solution)/shard_map/all_to_all | solution.py:384
  95.8 7.7 %collective-permute-start.17 = (bf16[256,256]{1,0:T(8,128)(2,1)S(1)}, bf16[256,256]{1,0:T(8,128)(2,1)S(1)}, u32[]{:S(2)}, u32[]{:S(2)}) collective-permute-start(bf16[256,256]{1,0:T(8,128)(2,1)S(1)} %get-tuple-element.63), channel_id=1, source_target_pairs={{0,1},{1,2},{2,3},{3,0},{4,5},{5,6},{6,7},{7,4},{8,9},{9,10},{10,1... | collective-permute-start | bytes 393224 | tf_op jit(solution)/shard_map/ppermute | solution.py:335
  97.2 7.9 %collective-permute-start.18 = (bf16[256,256]{1,0:T(8,128)(2,1)S(1)}, bf16[256,256]{1,0:T(8,128)(2,1)S(1)}, u32[]{:S(2)}, u32[]{:S(2)}) collective-permute-start(bf16[256,256]{1,0:T(8,128)(2,1)S(1)} %get-tuple-element.63), channel_id=1, source_target_pairs={{0,2},{1,3},{2,0},{3,1},{4,6},{5,7},{6,4},{7,5},{8,10},{9,11},{10,... | collective-permute-start | bytes 393224 | tf_op jit(solution)/shard_map/ppermute | solution.py:335
  109.6 16.4 %all-to-all-start.3 = ((bf16[16,96,256]{2,1,0:T(8,128)(2,1)}), bf16[16,96,256]{2,1,0:T(8,128)(2,1)S(1)}, u32[]{:S(2)}, u32[]{:S(2)}) async-start(bf16[16,96,256]{2,1,0:T(8,128)(2,1)} %bitcast.4), calls=%async_computation.3 | async-start | bytes 1572864 | tf_op jit(solution)/shard_map/all_to_all | solution.py:384
  113.5 14.4 %collective-permute-start.14 = (bf16[8,96,256]{2,1,0:T(8,128)(2,1)S(1)}, bf16[8,96,256]{2,1,0:T(8,128)(2,1)S(1)}, u32[]{:S(2)}, u32[]{:S(2)}) collective-permute-start(bf16[8,96,256]{2,1,0:T(8,128)(2,1)S(1)} %get-tuple-element.70.refs_0_), channel_id=1, source_target_pairs={{0,1},{1,2},{2,3},{3,0},{4,5},{5,6},{6,7},{7,4},{8,9},{9,10},{10,1... | collective-permute-start | bytes 1179656 | tf_op jit(solution)/shard_map/ppermute | solution.py:335
  114.9 14.4 %collective-permute-start.15 = (bf16[8,96,256]{2,1,0:T(8,128)(2,1)S(1)}, bf16[8,96,256]{2,1,0:T(8,128)(2,1)S(1)}, u32[]{:S(2)}, u32[]{:S(2)}) collective-permute-start(bf16[8,96,256]{2,1,0:T(8,128)(2,1)S(1)} %get-tuple-element.69.refs_1_), channel_id=1, source_target_pairs={{0,3},{1,0},{2,1},{3,2},{4,7},{5,4},{6,5},{7,6},{8,11},{9,8},{10,9... | collective-permute-start | bytes 1179656 | tf_op jit(solution)/shard_map/ppermute | solution.py:335
  116.8 18.6 %collective-permute-start.26 = (bf16[8,96,256]{2,1,0:T(8,128)(2,1)S(1)}, bf16[8,96,256]{2,1,0:T(8,128)(2,1)S(1)}, u32[]{:S(2)}, u32[]{:S(2)}) collective-permute-start(bf16[8,96,256]{2,1,0:T(8,128)(2,1)S(1)} %get-tuple-element.70.refs_0_), channel_id=1, source_target_pairs={{0,3},{1,0},{2,1},{3,2},{4,7},{5,4},{6,5},{7,6},{8,11},{9,8},{10,9... | collective-permute-start | bytes 1179656 | tf_op jit(solution)/shard_map/ppermute | solution.py:335
  118.2 28.3 %collective-permute-start.28 = (bf16[8,96,256]{2,1,0:T(8,128)(2,1)S(1)}, bf16[8,96,256]{2,1,0:T(8,128)(2,1)S(1)}, u32[]{:S(2)}, u32[]{:S(2)}) collective-permute-start(bf16[8,96,256]{2,1,0:T(8,128)(2,1)S(1)} %get-tuple-element.69.refs_1_), channel_id=1, source_target_pairs={{0,1},{1,2},{2,3},{3,0},{4,5},{5,6},{6,7},{7,4},{8,9},{9,10},{10,1... | collective-permute-start | bytes 1179656 | tf_op jit(solution)/shard_map/ppermute | solution.py:335
  126.0 22.7 %collective-permute-start.22 = (bf16[8,96,256]{2,1,0:T(8,128)(2,1)S(1)}, bf16[8,96,256]{2,1,0:T(8,128)(2,1)S(1)}, u32[]{:S(2)}, u32[]{:S(2)}) collective-permute-start(bf16[8,96,256]{2,1,0:T(8,128)(2,1)S(1)} %get-tuple-element.68.refs_2_), channel_id=1, source_target_pairs={{0,1},{1,2},{2,3},{3,0},{4,5},{5,6},{6,7},{7,4},{8,9},{9,10},{10,1... | collective-permute-start | bytes 1179656 | tf_op jit(solution)/shard_map/ppermute | solution.py:335
  127.8 22.1 %collective-permute-start.24 = (bf16[8,96,256]{2,1,0:T(8,128)(2,1)S(1)}, bf16[8,96,256]{2,1,0:T(8,128)(2,1)S(1)}, u32[]{:S(2)}, u32[]{:S(2)}) collective-permute-start(bf16[8,96,256]{2,1,0:T(8,128)(2,1)S(1)} %get-tuple-element.67.refs_3_), channel_id=1, source_target_pairs={{0,3},{1,0},{2,1},{3,2},{4,7},{5,4},{6,5},{7,6},{8,11},{9,8},{10,9... | collective-permute-start | bytes 1179656 | tf_op jit(solution)/shard_map/ppermute | solution.py:335
  129.3 23.0 %collective-permute-start.27 = (bf16[8,96,256]{2,1,0:T(8,128)(2,1)S(1)}, bf16[8,96,256]{2,1,0:T(8,128)(2,1)S(1)}, u32[]{:S(2)}, u32[]{:S(2)}) collective-permute-start(bf16[8,96,256]{2,1,0:T(8,128)(2,1)S(1)} %get-tuple-element.68.refs_2_), channel_id=1, source_target_pairs={{0,3},{1,0},{2,1},{3,2},{4,7},{5,4},{6,5},{7,6},{8,11},{9,8},{10,9... | collective-permute-start | bytes 1179656 | tf_op jit(solution)/shard_map/ppermute | solution.py:335
  135.4 19.9 %collective-permute-start.29 = (bf16[8,96,256]{2,1,0:T(8,128)(2,1)S(1)}, bf16[8,96,256]{2,1,0:T(8,128)(2,1)S(1)}, u32[]{:S(2)}, u32[]{:S(2)}) collective-permute-start(bf16[8,96,256]{2,1,0:T(8,128)(2,1)S(1)} %get-tuple-element.67.refs_3_), channel_id=1, source_target_pairs={{0,1},{1,2},{2,3},{3,0},{4,5},{5,6},{6,7},{7,4},{8,9},{9,10},{10,1... | collective-permute-start | bytes 1179656 | tf_op jit(solution)/shard_map/ppermute | solution.py:335
  146.6 21.6 %collective-permute-start.20 = (bf16[8,96,256]{2,1,0:T(8,128)(2,1)S(1)}, bf16[8,96,256]{2,1,0:T(8,128)(2,1)S(1)}, u32[]{:S(2)}, u32[]{:S(2)}) collective-permute-start(bf16[8,96,256]{2,1,0:T(8,128)(2,1)S(1)} %collective-permute-done.14.refs_4_), channel_id=1, source_target_pairs={{0,1},{1,2},{2,3},{3,0},{4,5},{5,6},{6,7},{7,4},{8,9},{9,10},{10,1... | collective-permute-start | bytes 1179656 | tf_op jit(solution)/shard_map/ppermute | solution.py:335
  148.7 19.6 %collective-permute-start.21 = (bf16[8,96,256]{2,1,0:T(8,128)(2,1)S(1)}, bf16[8,96,256]{2,1,0:T(8,128)(2,1)S(1)}, u32[]{:S(2)}, u32[]{:S(2)}) collective-permute-start(bf16[8,96,256]{2,1,0:T(8,128)(2,1)S(1)} %collective-permute-done.15.refs_1_), channel_id=1, source_target_pairs={{0,3},{1,0},{2,1},{3,2},{4,7},{5,4},{6,5},{7,6},{8,11},{9,8},{10,9... | collective-permute-start | bytes 1179656 | tf_op jit(solution)/shard_map/ppermute | solution.py:335
  149.9 18.3 %collective-permute-start.23 = (bf16[8,96,256]{2,1,0:T(8,128)(2,1)S(1)}, bf16[8,96,256]{2,1,0:T(8,128)(2,1)S(1)}, u32[]{:S(2)}, u32[]{:S(2)}) collective-permute-start(bf16[8,96,256]{2,1,0:T(8,128)(2,1)S(1)} %collective-permute-done.22.refs_6_), channel_id=1, source_target_pairs={{0,1},{1,2},{2,3},{3,0},{4,5},{5,6},{6,7},{7,4},{8,9},{9,10},{10,1... | collective-permute-start | bytes 1179656 | tf_op jit(solution)/shard_map/ppermute | solution.py:335
  152.3 16.0 %collective-permute-start.25 = (bf16[8,96,256]{2,1,0:T(8,128)(2,1)S(1)}, bf16[8,96,256]{2,1,0:T(8,128)(2,1)S(1)}, u32[]{:S(2)}, u32[]{:S(2)}) collective-permute-start(bf16[8,96,256]{2,1,0:T(8,128)(2,1)S(1)} %collective-permute-done.24.refs_3_), channel_id=1, source_target_pairs={{0,3},{1,0},{2,1},{3,2},{4,7},{5,4},{6,5},{7,6},{8,11},{9,8},{10,9... | collective-permute-start | bytes 1179656 | tf_op jit(solution)/shard_map/ppermute | solution.py:335
  (8 other events, 48.0 us)

commit v5 on v4

--- a/solution.py
+++ b/solution.py
@@ -222,29 +222,14 @@
     return far, near
 
 
-def fill(owner, parts, raw, arrived, put):
-    copies = []
-    for r, given in enumerate(parts):
-        begin = 0
-        for k, part in enumerate(given):
-            groups = part.shape[0]
-            copies.append(
-                pltpu.make_async_copy(
-                    part, raw.at[r, begin : begin + groups], arrived.at[r * len(given) + k]
-                )
-            )
-            begin += groups
-    for copy in copies:
-        copy.start()
-    for copy in copies:
-        copy.wait()
+def fill(owner, raw, put):
     blocks_per_occ = owner.shape[0] // 2
     lane = lax.broadcasted_iota(jnp.int32, (raw.shape[2], 128), 1)
 
     def one(i, t):
         found = [owner[i * blocks_per_occ + t * 2 + j] for j in range(2)]
         tiles = []
-        for r in range(len(parts)):
+        for r in range(raw.shape[0]):
             halves = []
             for j, d in enumerate(found):
                 lanes = pl.ds(pl.multiple_of(lax.rem(d // 2, 2) * 128, 128), 128)
@@ -261,67 +246,99 @@
     lax.fori_loop(0, blocks_per_occ // 8, some, 0)
 
 
-def columns_kernel(blocks, owner, vir, *refs, quarter_shells, turns, more):
-    out, raw, panel, arrived = refs[-4:]
-    given = refs[: len(refs) - 4 - more]
+def columns_kernel(blocks, owner, vir, *refs, quarter_shells, turns, more, last):
+    out, raw, panel, held, arrived = refs[-5:]
+    given = refs[: len(refs) - 5 - more]
+    earlier = refs[-6] if more else None
     count = len(given) // len(turns)
-    parts = [given[k * count : (k + 1) * count] for k in range(len(turns))]
     rows = raw.shape[2]
     width = len(turns) * rows
     quarter = blocks[0, 1] // quarter_shells
-
-    @pl.when(pl.program_id(0) == 0)
-    def _():
-        def put(i, lanes, tiles):
-            for k, tile in enumerate(tiles):
-                begin = i * width + k * rows
-                panel[begin : begin + rows, lanes] = tile
-
-        fill(owner, parts, raw, arrived, put)
-
-    both = lax.dot_general(
-        vir[...], panel[...], (((1,), (1,)), ((), ())), preferred_element_type=F32
-    ).astype(BF)
-    source = lax.broadcasted_iota(jnp.int32, (width, out.shape[2]), 0)
-    target = lax.broadcasted_iota(jnp.int32, (width, out.shape[2]), 1)
+    strips = 2
+    tile = vir.shape[0] // strips
+
+    collect = []
+    for at, part in enumerate(given):
+        begin = (at % count) * part.shape[0]
+        collect.append(
+            pltpu.make_async_copy(
+                part, raw.at[at // count, begin : begin + part.shape[0]], arrived.at[at]
+            )
+        )
+    for copy in collect:
+        copy.start()
+    for copy in collect:
+        copy.wait()
+
+    def put(i, lanes, tiles):
+        for k, value in enumerate(tiles):
+            begin = i * width + k * rows
+            panel[begin : begin + rows, lanes] = value
+
+    fill(owner, raw, put)
+
+    columns = GRP * rows
+    source = lax.broadcasted_iota(jnp.int32, (width, columns), 0)
+    target = lax.broadcasted_iota(jnp.int32, (width, columns), 1)
     pick = target < 0
     for k, r in enumerate(turns):
         moved = (lax.rem(quarter + r, GRP) - k) * rows
         pick = pick | ((source // rows == k) & (target == source + moved))
     pick = jnp.where(pick, 1.0, 0.0).astype(BF)
-    for i in range(2):
-        value = jnp.dot(
-            both[:, i * width : (i + 1) * width], pick, preferred_element_type=F32
-        )
-        if more:
-            value = value + refs[-5][i].astype(F32)
-        out[i] = value.astype(BF)
-
-
-def add_columns(vir, blocks, owner, shell, turns, pieces, earlier=None):
+    stores = []
+    for k in range(strips):
+        here = slice(k * tile, (k + 1) * tile)
+        both = lax.dot_general(
+            vir[here, :], panel[...], (((1,), (1,)), ((), ())), preferred_element_type=F32
+        ).astype(BF)
+        for i in range(2):
+            value = jnp.dot(
+                both[:, i * width : (i + 1) * width], pick, preferred_element_type=F32
+            )
+            if more:
+                value = value + earlier[i, here, :].astype(F32)
+            if last:
+                held[i, here, :] = value.astype(BF)
+            else:
+                out[i, here, :] = value.astype(BF)
+        if last:
+            stores.append(
+                pltpu.make_async_copy(
+                    held.at[:, here, :],
+                    out.at[:, here, :],
+                    arrived.at[len(given) + k],
+                )
+            )
+            stores[-1].start()
+    for copy in stores:
+        copy.wait()
+
+
+def add_columns(vir, blocks, owner, shell, turns, pieces, earlier=None, last=False):
     nus, virtuals = vir.shape
     parts = [part for piece in pieces for part in piece]
     rows = parts[0].shape[1]
     groups = sum(part.shape[0] for part in pieces[0])
-    tile = 272
-    spec = pl.BlockSpec((2, tile, GRP * rows), lambda t: (0, t, 0))
     more = [] if earlier is None else [earlier]
+    shape = (2, nus, GRP * rows)
     return pl.pallas_call(
         functools.partial(
-            columns_kernel, quarter_shells=nus // shell, turns=turns, more=len(more)
-        ),
-        grid=(nus // tile,),
-        in_specs=[SMEM, SMEM, pl.BlockSpec((tile, virtuals), lambda t: (t, 0))]
-        + [VMEM] * len(parts)
-        + [spec] * len(more),
-        out_specs=spec,
-        out_shape=jax.ShapeDtypeStruct((2, nus, GRP * rows), BF),
+            columns_kernel,
+            quarter_shells=nus // shell,
+            turns=turns,
+            more=len(more),
+            last=last,
+        ),
+        in_specs=[SMEM, SMEM] + [VMEM] * (1 + len(parts) + len(more)),
+        out_specs=ANY if last else VMEM,
+        out_shape=jax.ShapeDtypeStruct(shape, BF),
         scratch_shapes=[
             pltpu.VMEM((len(turns), groups, rows, 256), BF),
             pltpu.VMEM((2 * len(turns) * rows, virtuals), BF),
-            pltpu.SemaphoreType.DMA((len(parts),)),
+            pltpu.VMEM(shape if last else (2, 16, 128), BF),
+            pltpu.SemaphoreType.DMA((len(parts) + 2,)),
         ],
-        compiler_params=pltpu.CompilerParams(vmem_limit_bytes=44 * MIB),
+        compiler_params=pltpu.CompilerParams(vmem_limit_bytes=24 * MIB),
         cost_estimate=pl.CostEstimate(
             flops=4 * nus * virtuals * len(turns) * rows,
             bytes_accessed=12 * MIB,
@@ -411,7 +428,6 @@
     rows_a = exchange(totals[0]).reshape(-1, 4 * block_rows)
     amplitude_a = amplitude_of(rows_a, 0)
     rows_b = exchange(totals[1]).reshape(-1, 4 * block_rows)
-    rows_a, rows_b = tie((rows_a, rows_b))
     own_a, below_a, above_a = to_neighbours(exchange(density_of(rows_a, amplitude_a)))
     amplitude_b = amplitude_of(rows_b, 1)
     own_b, below_b, above_b = to_neighbours(exchange(density_of(rows_b, amplitude_b)))
@@ -421,7 +437,7 @@
     far_a = [shift(first, 1), shift(second, -1)]
     far_b = [shift(below_b[0], 1), shift(above_b[1], -1)]
     result = put((1, 3), [[*above_a, *above_b], [*below_a, *below_b]], result)
-    return put((2,), [[*far_a, *far_b]], result)
+    return put((2,), [[*far_a, *far_b]], result, last=True)
 
 
 def solution(mesh):

time: 181 us -> 178 us (0.983)
  Pallas kernels: 48 us -> 42.8 us
  local copies, waits for them, and re-layouts: 2.85 us -> 6.38 us
    pallas_call x3, Pallas kernels: 34.7 us -> 29.5 us  [add_columns(): pl.pallas_call(functools.partial(columns_kernel, quarter_shells=nus // sh...]
    unnamed x13 -> x15, local copies, waits for them, and re-layouts: 2.15 us -> 5.68 us
  transfers between devices with their start and end apart: 34 -> 34, of which waited for: 18 -> 19; matrix products, arithmetic and copies ran while one was open for 5% -> 5% of each run, Pallas kernels for 17% -> 15%
where the time goes in v5:
time: 178 us; the launch traced here: 177 us
  starting transfers between devices  66.1 us (37%)
  waiting for transfers between devices  52.9 us (30%)
  Pallas kernels  42.8 us (24%)
  local copies, waits for them, and re-layouts  6.38 us (4%)
  other arithmetic  4.83 us (3%)
  matrix products  3.48 us (2%)
    ppermute x28, starting transfers between devices, shift(): return lax.ppermute(value, 'grp', [(j, (j + by) % GRP) for j in range(GRP)])  42.3 us
    ppermute x28, waiting for transfers between devices, shift(): return lax.ppermute(value, 'grp', [(j, (j + by) % GRP) for j in range(GRP)])  32.3 us
    pallas_call x3, Pallas kernels, add_columns(): pl.pallas_call(functools.partial(columns_kernel, quarter_shells=nus // sh...  29.5 us
    all_to_all x4, starting transfers between devices, exchange(): lax.all_to_all(value, 'aux', split_axis=0, concat_axis=0, axis_index_grou...  23.6 us
    all_to_all x4, waiting for transfers between devices, exchange(): lax.all_to_all(value, 'aux', split_axis=0, concat_axis=0, axis_index_grou...  19.4 us
    pallas_call x1, Pallas kernels, partial_pieces(): pl.pallas_call(functools.partial(far_kernel, groups=groups, quarter_shell...  6.94 us
    pallas_call x1, Pallas kernels, partial_pieces(): pl.pallas_call(functools.partial(near_kernel, slots=slots, groups=groups)...  6.36 us
    unnamed x15, local copies, waits for them, and re-layouts  5.68 us
  transfers between devices with their start and end apart: 34, of which 19 were waited for; matrix products, arithmetic and copies ran while one was open for 5% of the time, Pallas kernels for 15%

profile of v5, /device:TPU:0, one launch (start us, length us, event | category | flops | bytes accessed | tf_op | source)
XLA Modules:
  0.0 177.0 jit_solution(7570565627046099044)
XLA Ops:
  2.1 6.9 %far_rows.1 = (bf16[288,512]{1,0:T(8,128)(2,1)S(1)}, bf16[8,96,256]{2,1,0:T(8,128)(2,1)S(1)}, bf16[8,96,256]{2,1,0:T(8,128)(2,1)S(1)}, bf16[8,96,256]{2,1,0:T(8,128)(2,1)S(1)}, bf16[8,96,256]{2,1,0:T(8,128)(2,1)S(1)}) custom-call(s32[8,4]{1,0:T(8,128)S(1)} %copy.23.blocks, s32[128]{0:T(128)S(1)} %copy-done.2, bf16[2,4352]{1,0:T(2,128)(2,1)S(1)} %copy-done.4, ...), custom_call_target="tpu_custom_call" | custom-call | flops 1073741824 | bytes 10485760 | tf_op jit(solution)/shard_map/far_rows/pallas_call | solution.py:182
  10.7 1.7 collective-permute-start.1
  14.4 6.4 %near_rows.1 = (bf16[16,96,256]{2,1,0:T(8,128)(2,1)S(1)}, bf16[8,96,256]{2,1,0:T(8,128)(2,1)S(1)}, bf16[8,96,256]{2,1,0:T(8,128)(2,1)S(1)}, bf16[8,96,256]{2,1,0...) custom-call(s32[8,4]{1,0:T(8,128)S(1)} %copy.23.blocks, ...), custom_call_target="tpu_custom_call" | custom-call | flops 2147483648 | bytes 8388608 | tf_op jit(solution)/shard_map/near_rows/pallas_call | solution.py:203
  24.3 1.7 collective-permute-start.6
  26.1 1.7 collective-permute-start.7
  28.0 3.2 %collective-permute-done.4 = bf16[8,96,256]{2,1,0:T(8,128)(2,1)S(1)} collective-permute-done((bf16[8,96,256]{2,1,0:T(8,128)(2,1)S(1)}, bf16[8,96,256]{2,1,0:T(8,128)(2,1)S(1)}, u32[]{:S(2)}, u32[]{:S(2)}) %collective-permute-start.4) | collective-permute-done | bytes 393248 | tf_op jit(solution)/shard_map/ppermute | solution.py:352
  33.1 6.1 %collective-permute-done.5 = bf16[8,96,256]{2,1,0:T(8,128)(2,1)S(1)} collective-permute-done((bf16[8,96,256]{2,1,0:T(8,128)(2,1)S(1)}, bf16[8,96,256]{2,1,0:T(8,128)(2,1)S(1)}, u32[]{:S(2)}, u32[]{:S(2)}) %collective-permute-start.5) | collective-permute-done | bytes 393248 | tf_op jit(solution)/shard_map/ppermute | solution.py:352
  41.1 1.7 collective-permute-start.15
  42.9 5.2 %collective-permute-done.7 = bf16[8,96,256]{2,1,0:T(8,128)(2,1)S(1)} collective-permute-done((bf16[8,96,256]{2,1,0:T(8,128)(2,1)S(1)}, bf16[8,96,256]{2,1,0:T(8,128)(2,1)S(1)}, u32[]{:S(2)}, u32[]{:S(2)}) %collective-permute-start.7) | collective-permute-done | bytes 393248 | tf_op jit(solution)/shard_map/ppermute | solution.py:352
  49.4 8.1 %all-to-all-start = ((bf16[16,96,256]{2,1,0:T(8,128)(2,1)}), bf16[16,96,256]{2,1,0:T(8,128)(2,1)S(1)}, u32[]{:S(2)}, u32[]{:S(2)}) async-start(bf16[16,96,256]{2,1,0:T(8,128)(2,1)} %pad_maximum_fusion.2), calls=%async_computation | async-start | bytes 1572864 | tf_op jit(solution)/shard_map/all_to_all | solution.py:401
  58.0 5.4 %collective-permute-done.14 = bf16[16,96,256]{2,1,0:T(8,128)(2,1)} collective-permute-done((bf16[16,96,256]{2,1,0:T(8,128)(2,1)S(1)}, bf16[16,96,256]{2,1,0:T(8,128)(2,1)}, u32[]{:S(2)}, u32[]{:S(2)}) %collective-permute-start.14) | collective-permute-done | bytes 786464 | tf_op jit(solution)/shard_map/ppermute | solution.py:352
  63.5 2.6 %add_convert_fusion = bf16[16,96,256]{2,1,0:T(8,128)(2,1)} fusion(bf16[16,96,256]{2,1,0:T(8,128)(2,1)} %collective-permute-done.15, bf16[16,96,256]{2,1,0:T(8,128)(2,1)} %collective-permute-done.14, bf16[16,96,256]{2,1,0:T(8,128)(2,1)S(1)} %get-tuple-element.51), kind=kLoop, calls=%fused_computation.2 | loop fusion | flops 2359296 | bytes 3145728 | tf_op jit(solution)/shard_map/convert_element_type | solution.py:356
  66.2 3.3 %all-to-all-done = bf16[16,96,256]{2,1,0:T(8,128)(2,1)S(1)} async-done(((bf16[16,96,256]{2,1,0:T(8,128)(2,1)}), bf16[16,96,256]{2,1,0:T(8,128)(2,1)S(1)}, u32[]{:S(2)}, u32[]{:S(2)}) %all-to-all-start) | async-done | bytes 786464 | tf_op jit(solution)/shard_map/all_to_all | solution.py:401
  69.4 4.9 %all-to-all-start.2 = ((bf16[16,96,256]{2,1,0:T(8,128)(2,1)}), bf16[16,96,256]{2,1,0:T(8,128)(2,1)S(1)}, u32[]{:S(2)}, u32[]{:S(2)}) async-start(bf16[16,96,256]{2,1,0:T(8,128)(2,1)} %add_convert_fusion), calls=%async_computation.2 | async-start | bytes 1572864 | tf_op jit(solution)/shard_map/all_to_all | solution.py:401
  76.4 2.8 %collective-permute-start.10 = (bf16[256,256]{1,0:T(8,128)(2,1)S(1)}, bf16[256,256]{1,0:T(8,128)(2,1)S(1)}, u32[]{:S(2)}, u32[]{:S(2)}) collective-permute-start(bf16[256,256]{1,0:T(8,128)(2,1)S(1)} %get-tuple-element.61), channel_id=1, source_target_pairs={{0,2},{1,3},{2,0},{3,1},{4,6},{5,7},{6,4},{7,5},{8,10},{9,11},{10,... | collective-permute-start | bytes 393224 | tf_op jit(solution)/shard_map/ppermute | solution.py:352
  81.3 6.5 %all-to-all-done.2 = bf16[16,96,256]{2,1,0:T(8,128)(2,1)S(1)} async-done(((bf16[16,96,256]{2,1,0:T(8,128)(2,1)}), bf16[16,96,256]{2,1,0:T(8,128)(2,1)S(1)}, u32[]{:S(2)}, u32[]{:S(2)}) %all-to-all-start.2) | async-done | bytes 786464 | tf_op jit(solution)/shard_map/all_to_all | solution.py:401
  89.6 5.9 %all-to-all-start.1 = ((bf16[16,96,256]{2,1,0:T(8,128)(2,1)}), bf16[16,96,256]{2,1,0:T(8,128)(2,1)S(1)}, u32[]{:S(2)}, u32[]{:S(2)}) async-start(bf16[16,96,256]{2,1,0:T(8,128)(2,1)} %bitcast.2), calls=%async_computation.1 | async-start | bytes 1572864 | tf_op jit(solution)/shard_map/all_to_all | solution.py:401
  96.5 2.9 %collective-permute-start.18 = (bf16[256,256]{1,0:T(8,128)(2,1)S(1)}, bf16[256,256]{1,0:T(8,128)(2,1)S(1)}, u32[]{:S(2)}, u32[]{:S(2)}) collective-permute-start(bf16[256,256]{1,0:T(8,128)(2,1)S(1)} %get-tuple-element.59), channel_id=1, source_target_pairs={{0,2},{1,3},{2,0},{3,1},{4,6},{5,7},{6,4},{7,5},{8,10},{9,11},{10,... | collective-permute-start | bytes 393224 | tf_op jit(solution)/shard_map/ppermute | solution.py:352
  100.5 1.8 %collective-permute-done.17 = bf16[256,256]{1,0:T(8,128)(2,1)S(1)} collective-permute-done((bf16[256,256]{1,0:T(8,128)(2,1)S(1)}, bf16[256,256]{1,0:T(8,128)(2,1)S(1)}, u32[]{:S(2)}, u32[]{:S(2)}) %collective-permute-start.17) | collective-permute-done | bytes 131104 | tf_op jit(solution)/shard_map/ppermute | solution.py:352
  102.3 3.1 %collective-permute-done.18 = bf16[256,256]{1,0:T(8,128)(2,1)S(1)} collective-permute-done((bf16[256,256]{1,0:T(8,128)(2,1)S(1)}, bf16[256,256]{1,0:T(8,128)(2,1)S(1)}, u32[]{:S(2)}, u32[]{:S(2)}) %collective-permute-start.18) | collective-permute-done | bytes 131104 | tf_op jit(solution)/shard_map/ppermute | solution.py:352
  106.8 2.2 %all-to-all-done.1 = bf16[16,96,256]{2,1,0:T(8,128)(2,1)S(1)} async-done(((bf16[16,96,256]{2,1,0:T(8,128)(2,1)}), bf16[16,96,256]{2,1,0:T(8,128)(2,1)S(1)}, u32[]{:S(2)}, u32[]{:S(2)}) %all-to-all-start.1) | async-done | bytes 786464 | tf_op jit(solution)/shard_map/all_to_all | solution.py:401
  109.0 4.8 %all-to-all-start.3 = ((bf16[16,96,256]{2,1,0:T(8,128)(2,1)}), bf16[16,96,256]{2,1,0:T(8,128)(2,1)S(1)}, u32[]{:S(2)}, u32[]{:S(2)}) async-start(bf16[16,96,256]{2,1,0:T(8,128)(2,1)} %bitcast.5), calls=%async_computation.3 | async-start | bytes 1572864 | tf_op jit(solution)/shard_map/all_to_all | solution.py:401
  115.0 2.1 %collective-permute-start.13 = (bf16[8,96,256]{2,1,0:T(8,128)(2,1)S(1)}, bf16[8,96,256]{2,1,0:T(8,128)(2,1)S(1)}, u32[]{:S(2)}, u32[]{:S(2)}) collective-permute-start(bf16[8,96,256]{2,1,0:T(8,128)(2,1)S(1)} %get-tuple-element.65.refs_1_), channel_id=1, source_target_pairs={{0,3},{1,0},{2,1},{3,2},{4,7},{5,4},{6,5},{7,6},{8,11},{9,8},{10,9... | collective-permute-start | bytes 1179656 | tf_op jit(solution)/shard_map/ppermute | solution.py:352
  119.1 7.5 %all-to-all-done.3 = bf16[16,96,256]{2,1,0:T(8,128)(2,1)S(1)} async-done(((bf16[16,96,256]{2,1,0:T(8,128)(2,1)}), bf16[16,96,256]{2,1,0:T(8,128)(2,1)S(1)}, u32[]{:S(2)}, u32[]{:S(2)}) %all-to-all-start.3) | async-done | bytes 786464 | tf_op jit(solution)/shard_map/all_to_all | solution.py:401
  126.6 1.9 %collective-permute-start.22 = (bf16[8,96,256]{2,1,0:T(8,128)(2,1)S(1)}, bf16[8,96,256]{2,1,0:T(8,128)(2,1)S(1)}, u32[]{:S(2)}, u32[]{:S(2)}) collective-permute-start(bf16[8,96,256]{2,1,0:T(8,128)(2,1)S(1)} %get-tuple-element.64.refs_2_), channel_id=1, source_target_pairs={{0,1},{1,2},{2,3},{3,0},{4,5},{5,6},{6,7},{7,4},{8,9},{9,10},{10,1... | collective-permute-start | bytes 1179656 | tf_op jit(solution)/shard_map/ppermute | solution.py:352
  131.4 4.1 %collective-permute-done.26.refs_0_ = bf16[8,96,256]{2,1,0:T(8,128)(2,1)S(1)} collective-permute-done((bf16[8,96,256]{2,1,0:T(8,128)(2,1)S(1)}, bf16[8,96,256]{2,1,0:T(8,128)(2,1)S(1)}, u32[]{:S(2)}, u32[]{:S(2)}) %collective-permute-start.26) | collective-permute-done | bytes 393248 | tf_op jit(solution)/shard_map/ppermute | solution.py:352
  136.3 3.5 %copy-done.1 = bf16[1088,4096]{1,0:T(8,128)(2,1)S(1)} copy-done((bf16[1088,4096]{1,0:T(8,128)(2,1)S(1)}, bf16[1088,4096]{1,0:T(8,128)(2,1)}, u32[]{:S(2)}) %copy-start.1) | copy-done | bytes 8912920
  139.8 9.2 %add_columns.3.refs_8_ = bf16[2,1088,384]{2,1,0:T(8,128)(2,1)S(1)} custom-call(s32[8,4]{1,0:T(8,128)S(1)} %copy.23.blocks, s32[128]{0:T(128)S(1)} %copy-done.3, bf16[1088,4096]{1,0:T(8,128)(2,1)S(1)} %copy-done.1, bf16[8,96,256]{2,1,0:T(8,128)(2,1)S(1)} %get-tuple-element.66.refs_0_, bf16[8,96,256]{2,1,0:T(8,128)(2,1)S(1)} %get-tuple-element.65.refs_1_, ...), custom_call_target="tpu_custom_call" | custom-call | flops 1711276032 | bytes 12582912 | tf_op jit(solution)/shard_map/add_columns/pallas_call | solution.py:324
  149.0 2.2 %collective-permute-start.20 = (bf16[8,96,256]{2,1,0:T(8,128)(2,1)S(1)}, bf16[8,96,256]{2,1,0:T(8,128)(2,1)S(1)}, u32[]{:S(2)}, u32[]{:S(2)}) collective-permute-start(bf16[8,96,256]{2,1,0:T(8,128)(2,1)S(1)} %collective-permute-done.12.refs_4_), channel_id=1, source_target_pairs={{0,1},{1,2},{2,3},{3,0},{4,5},{5,6},{6,7},{7,4},{8,9},{9,10},{10,1... | collective-permute-start | bytes 1179656 | tf_op jit(solution)/shard_map/ppermute | solution.py:352
  153.3 2.4 %collective-permute-start.25 = (bf16[8,96,256]{2,1,0:T(8,128)(2,1)S(1)}, bf16[8,96,256]{2,1,0:T(8,128)(2,1)S(1)}, u32[]{:S(2)}, u32[]{:S(2)}) collective-permute-start(bf16[8,96,256]{2,1,0:T(8,128)(2,1)S(1)} %collective-permute-done.24.refs_3_), channel_id=1, source_target_pairs={{0,3},{1,0},{2,1},{3,2},{4,7},{5,4},{6,5},{7,6},{8,11},{9,8},{10,9... | collective-permute-start | bytes 1179656 | tf_op jit(solution)/shard_map/ppermute | solution.py:352
  155.8 10.2 %add_columns.4.refs_4_ = bf16[2,1088,384]{2,1,0:T(8,128)(2,1)S(1)} custom-call(s32[8,4]{1,0:T(8,128)S(1)} %copy.23.blocks, s32[128]{0:T(128)S(1)} %copy-done.3, bf16[1088,4096]{1,0:T(8,128)(2,1)S(1)} %copy-done.1, bf16[8,96,256]{2,1,0:T(8,128)(2,1)S(1)} %collective-permute-done.26.refs_0_, bf16[8,96,256]{2,1,0:T(8,128)(2,1)S(1)} %collective-permute-done.13.refs_1_, ...), custom_call_target="tpu_custom_call" | custom-call | flops 3422552064 | bytes 12582912 | tf_op jit(solution)/shard_map/add_columns/pallas_call | solution.py:324
  166.7 10.1 %add_columns.5 = bf16[2,1088,384]{2,1,0:T(8,128)(2,1)} custom-call(s32[8,4]{1,0:T(8,128)S(1)} %copy.23.blocks, s32[128]{0:T(128)S(1)} %copy-done.3, bf16[1088,4096]{1,0:T(8,128)(2,1)S(1)} %copy-done.1, bf16[8,96,256]{2,1,0:T(8,128)(2,1)S(1)} %collective-permute-done.20.refs_0_, bf16[8,96,256]{2,1,0:T(8,128)(2,1)S(1)} %collective-permute-done.21.refs_1_, ...), custom_call_target="tpu_custom_call" | custom-call | flops 1711276032 | bytes 12582912 | tf_op jit(solution)/shard_map/add_columns/pallas_call | solution.py:324
  (85 shorter events, 34.2 us)
Async XLA Ops:
  9.1 13.3 %collective-permute-start = (bf16[8,96,256]{2,1,0:T(8,128)(2,1)S(1)}, bf16[8,96,256]{2,1,0:T(8,128)(2,1)S(1)}, u32[]{:S(2)}, u32[]{:S(2)}) collective-permute-start(bf16[8,96,256]{2,1,0:T(8,128)(2,1)S(1)} %get-tuple-element.36), channel_id=1, source_target_pairs={{0,1},{1,2},{2,3},{3,0},{4,5},{5,6},{6,7},{7,4},{8,9},{9,10},{10,1... | collective-permute-start | bytes 1179656 | tf_op jit(solution)/shard_map/ppermute | solution.py:352
  10.7 12.0 %collective-permute-start.1 = (bf16[8,96,256]{2,1,0:T(8,128)(2,1)S(1)}, bf16[8,96,256]{2,1,0:T(8,128)(2,1)S(1)}, u32[]{:S(2)}, u32[]{:S(2)}) collective-permute-start(bf16[8,96,256]{2,1,0:T(8,128)(2,1)S(1)} %get-tuple-element.37), channel_id=1, source_target_pairs={{0,3},{1,0},{2,1},{3,2},{4,7},{5,4},{6,5},{7,6},{8,11},{9,8},{10,9... | collective-permute-start | bytes 1179656 | tf_op jit(solution)/shard_map/ppermute | solution.py:352
  12.4 18.8 %collective-permute-start.4 = (bf16[8,96,256]{2,1,0:T(8,128)(2,1)S(1)}, bf16[8,96,256]{2,1,0:T(8,128)(2,1)S(1)}, u32[]{:S(2)}, u32[]{:S(2)}) collective-permute-start(bf16[8,96,256]{2,1,0:T(8,128)(2,1)S(1)} %get-tuple-element.44), channel_id=1, source_target_pairs={{0,3},{1,0},{2,1},{3,2},{4,7},{5,4},{6,5},{7,6},{8,11},{9,8},{10,9... | collective-permute-start | bytes 1179656 | tf_op jit(solution)/shard_map/ppermute | solution.py:352
  14.0 18.9 %collective-permute-start.3 = (bf16[8,96,256]{2,1,0:T(8,128)(2,1)S(1)}, bf16[8,96,256]{2,1,0:T(8,128)(2,1)S(1)}, u32[]{:S(2)}, u32[]{:S(2)}) collective-permute-start(bf16[8,96,256]{2,1,0:T(8,128)(2,1)S(1)} %get-tuple-element.40), channel_id=1, source_target_pairs={{0,1},{1,2},{2,3},{3,0},{4,5},{5,6},{6,7},{7,4},{8,9},{9,10},{10,1... | collective-permute-start | bytes 1179656 | tf_op jit(solution)/shard_map/ppermute | solution.py:352
  22.8 16.5 %collective-permute-start.5 = (bf16[8,96,256]{2,1,0:T(8,128)(2,1)S(1)}, bf16[8,96,256]{2,1,0:T(8,128)(2,1)S(1)}, u32[]{:S(2)}, u32[]{:S(2)}) collective-permute-start(bf16[8,96,256]{2,1,0:T(8,128)(2,1)S(1)} %get-tuple-element.45), channel_id=1, source_target_pairs={{0,1},{1,2},{2,3},{3,0},{4,5},{5,6},{6,7},{7,4},{8,9},{9,10},{10,1... | collective-permute-start | bytes 1179656 | tf_op jit(solution)/shard_map/ppermute | solution.py:352
  24.3 15.4 %collective-permute-start.6 = (bf16[8,96,256]{2,1,0:T(8,128)(2,1)S(1)}, bf16[8,96,256]{2,1,0:T(8,128)(2,1)S(1)}, u32[]{:S(2)}, u32[]{:S(2)}) collective-permute-start(bf16[8,96,256]{2,1,0:T(8,128)(2,1)S(1)} %get-tuple-element.46), channel_id=1, source_target_pairs={{0,3},{1,0},{2,1},{3,2},{4,7},{5,4},{6,5},{7,6},{8,11},{9,8},{10,9... | collective-permute-start | bytes 1179656 | tf_op jit(solution)/shard_map/ppermute | solution.py:352
  26.1 21.9 %collective-permute-start.7 = (bf16[8,96,256]{2,1,0:T(8,128)(2,1)S(1)}, bf16[8,96,256]{2,1,0:T(8,128)(2,1)S(1)}, u32[]{:S(2)}, u32[]{:S(2)}) collective-permute-start(bf16[8,96,256]{2,1,0:T(8,128)(2,1)S(1)} %add_convert_fusion.2), channel_id=1, source_target_pairs={{0,3},{1,0},{2,1},{3,2},{4,7},{5,4},{6,5},{7,6},{8,11},{9,8},{10,9... | collective-permute-start | bytes 1179656 | tf_op jit(solution)/shard_map/ppermute | solution.py:352
  31.2 16.9 %collective-permute-start.2 = (bf16[8,96,256]{2,1,0:T(8,128)(2,1)S(1)}, bf16[8,96,256]{2,1,0:T(8,128)(2,1)S(1)}, u32[]{:S(2)}, u32[]{:S(2)}) collective-permute-start(bf16[8,96,256]{2,1,0:T(8,128)(2,1)S(1)} %add_convert_fusion.6), channel_id=1, source_target_pairs={{0,1},{1,2},{2,3},{3,0},{4,5},{5,6},{6,7},{7,4},{8,9},{9,10},{10,1... | collective-permute-start | bytes 1179656 | tf_op jit(solution)/shard_map/ppermute | solution.py:352
  39.6 23.7 %collective-permute-start.14 = (bf16[16,96,256]{2,1,0:T(8,128)(2,1)S(1)}, bf16[16,96,256]{2,1,0:T(8,128)(2,1)}, u32[]{:S(2)}, u32[]{:S(2)}) collective-permute-start(bf16[16,96,256]{2,1,0:T(8,128)(2,1)S(1)} %pad_maximum_fusion), channel_id=1, source_target_pairs={{0,1},{1,2},{2,3},{3,0},{4,5},{5,6},{6,7},{7,4},{8,9},{9,10},{10,1... | collective-permute-start | bytes 2359304 | tf_op jit(solution)/shard_map/ppermute | solution.py:352
  41.1 22.4 %collective-permute-start.15 = (bf16[16,96,256]{2,1,0:T(8,128)(2,1)S(1)}, bf16[16,96,256]{2,1,0:T(8,128)(2,1)}, u32[]{:S(2)}, u32[]{:S(2)}) collective-permute-start(bf16[16,96,256]{2,1,0:T(8,128)(2,1)S(1)} %pad_maximum_fusion.1), channel_id=1, source_target_pairs={{0,3},{1,0},{2,1},{3,2},{4,7},{5,4},{6,5},{7,6},{8,11},{9,8},{10,9... | collective-permute-start | bytes 2359304 | tf_op jit(solution)/shard_map/ppermute | solution.py:352
  49.4 20.0 %all-to-all-start = ((bf16[16,96,256]{2,1,0:T(8,128)(2,1)}), bf16[16,96,256]{2,1,0:T(8,128)(2,1)S(1)}, u32[]{:S(2)}, u32[]{:S(2)}) async-start(bf16[16,96,256]{2,1,0:T(8,128)(2,1)} %pad_maximum_fusion.2), calls=%async_computation | async-start | bytes 1572864 | tf_op jit(solution)/shard_map/all_to_all | solution.py:401
  69.4 18.4 %all-to-all-start.2 = ((bf16[16,96,256]{2,1,0:T(8,128)(2,1)}), bf16[16,96,256]{2,1,0:T(8,128)(2,1)S(1)}, u32[]{:S(2)}, u32[]{:S(2)}) async-start(bf16[16,96,256]{2,1,0:T(8,128)(2,1)} %add_convert_fusion), calls=%async_computation.2 | async-start | bytes 1572864 | tf_op jit(solution)/shard_map/all_to_all | solution.py:401
  76.4 11.9 %collective-permute-start.10 = (bf16[256,256]{1,0:T(8,128)(2,1)S(1)}, bf16[256,256]{1,0:T(8,128)(2,1)S(1)}, u32[]{:S(2)}, u32[]{:S(2)}) collective-permute-start(bf16[256,256]{1,0:T(8,128)(2,1)S(1)} %get-tuple-element.61), channel_id=1, source_target_pairs={{0,2},{1,3},{2,0},{3,1},{4,6},{5,7},{6,4},{7,5},{8,10},{9,11},{10,... | collective-permute-start | bytes 393224 | tf_op jit(solution)/shard_map/ppermute | solution.py:352
  79.2 9.1 %collective-permute-start.11 = (bf16[256,256]{1,0:T(8,128)(2,1)S(1)}, bf16[256,256]{1,0:T(8,128)(2,1)S(1)}, u32[]{:S(2)}, u32[]{:S(2)}) collective-permute-start(bf16[256,256]{1,0:T(8,128)(2,1)S(1)} %get-tuple-element.61), channel_id=1, source_target_pairs={{0,3},{1,0},{2,1},{3,2},{4,7},{5,4},{6,5},{7,6},{8,11},{9,8},{10,9... | collective-permute-start | bytes 393224 | tf_op jit(solution)/shard_map/ppermute | solution.py:352
  80.7 7.6 %collective-permute-start.9 = (bf16[256,256]{1,0:T(8,128)(2,1)S(1)}, bf16[256,256]{1,0:T(8,128)(2,1)S(1)}, u32[]{:S(2)}, u32[]{:S(2)}) collective-permute-start(bf16[256,256]{1,0:T(8,128)(2,1)S(1)} %get-tuple-element.61), channel_id=1, source_target_pairs={{0,1},{1,2},{2,3},{3,0},{4,5},{5,6},{6,7},{7,4},{8,9},{9,10},{10,1... | collective-permute-start | bytes 393224 | tf_op jit(solution)/shard_map/ppermute | solution.py:352
  88.2 7.3 %collective-permute-start.16 = (f32[256,256]{1,0:T(8,128)S(1)}, f32[256,256]{1,0:T(8,128)S(1)}, u32[]{:S(2)}, u32[]{:S(2)}) collective-permute-start(f32[256,256]{1,0:T(8,128)S(1)} %convolution_bitcast_fusion), channel_id=1, source_target_pairs={{0,4},{4,0},{8,12},{12,8},{16,20},{20,16},{24,28},{28,24},{32,36},... | collective-permute-start | bytes 786440 | tf_op jit(solution)/shard_map/ppermute | solution.py:412
  89.6 19.3 %all-to-all-start.1 = ((bf16[16,96,256]{2,1,0:T(8,128)(2,1)}), bf16[16,96,256]{2,1,0:T(8,128)(2,1)S(1)}, u32[]{:S(2)}, u32[]{:S(2)}) async-start(bf16[16,96,256]{2,1,0:T(8,128)(2,1)} %bitcast.2), calls=%async_computation.1 | async-start | bytes 1572864 | tf_op jit(solution)/shard_map/all_to_all | solution.py:401
  95.6 6.7 %collective-permute-start.17 = (bf16[256,256]{1,0:T(8,128)(2,1)S(1)}, bf16[256,256]{1,0:T(8,128)(2,1)S(1)}, u32[]{:S(2)}, u32[]{:S(2)}) collective-permute-start(bf16[256,256]{1,0:T(8,128)(2,1)S(1)} %get-tuple-element.59), channel_id=1, source_target_pairs={{0,1},{1,2},{2,3},{3,0},{4,5},{5,6},{6,7},{7,4},{8,9},{9,10},{10,1... | collective-permute-start | bytes 393224 | tf_op jit(solution)/shard_map/ppermute | solution.py:352
  96.5 8.9 %collective-permute-start.18 = (bf16[256,256]{1,0:T(8,128)(2,1)S(1)}, bf16[256,256]{1,0:T(8,128)(2,1)S(1)}, u32[]{:S(2)}, u32[]{:S(2)}) collective-permute-start(bf16[256,256]{1,0:T(8,128)(2,1)S(1)} %get-tuple-element.59), channel_id=1, source_target_pairs={{0,2},{1,3},{2,0},{3,1},{4,6},{5,7},{6,4},{7,5},{8,10},{9,11},{10,... | collective-permute-start | bytes 393224 | tf_op jit(solution)/shard_map/ppermute | solution.py:352
  109.0 17.6 %all-to-all-start.3 = ((bf16[16,96,256]{2,1,0:T(8,128)(2,1)}), bf16[16,96,256]{2,1,0:T(8,128)(2,1)S(1)}, u32[]{:S(2)}, u32[]{:S(2)}) async-start(bf16[16,96,256]{2,1,0:T(8,128)(2,1)} %bitcast.5), calls=%async_computation.3 | async-start | bytes 1572864 | tf_op jit(solution)/shard_map/all_to_all | solution.py:401
  113.8 14.8 %collective-permute-start.12 = (bf16[8,96,256]{2,1,0:T(8,128)(2,1)S(1)}, bf16[8,96,256]{2,1,0:T(8,128)(2,1)S(1)}, u32[]{:S(2)}, u32[]{:S(2)}) collective-permute-start(bf16[8,96,256]{2,1,0:T(8,128)(2,1)S(1)} %get-tuple-element.66.refs_0_), channel_id=1, source_target_pairs={{0,1},{1,2},{2,3},{3,0},{4,5},{5,6},{6,7},{7,4},{8,9},{9,10},{10,1... | collective-permute-start | bytes 1179656 | tf_op jit(solution)/shard_map/ppermute | solution.py:352
  115.0 14.9 %collective-permute-start.13 = (bf16[8,96,256]{2,1,0:T(8,128)(2,1)S(1)}, bf16[8,96,256]{2,1,0:T(8,128)(2,1)S(1)}, u32[]{:S(2)}, u32[]{:S(2)}) collective-permute-start(bf16[8,96,256]{2,1,0:T(8,128)(2,1)S(1)} %get-tuple-element.65.refs_1_), channel_id=1, source_target_pairs={{0,3},{1,0},{2,1},{3,2},{4,7},{5,4},{6,5},{7,6},{8,11},{9,8},{10,9... | collective-permute-start | bytes 1179656 | tf_op jit(solution)/shard_map/ppermute | solution.py:352
  117.1 18.4 %collective-permute-start.26 = (bf16[8,96,256]{2,1,0:T(8,128)(2,1)S(1)}, bf16[8,96,256]{2,1,0:T(8,128)(2,1)S(1)}, u32[]{:S(2)}, u32[]{:S(2)}) collective-permute-start(bf16[8,96,256]{2,1,0:T(8,128)(2,1)S(1)} %get-tuple-element.66.refs_0_), channel_id=1, source_target_pairs={{0,3},{1,0},{2,1},{3,2},{4,7},{5,4},{6,5},{7,6},{8,11},{9,8},{10,9... | collective-permute-start | bytes 1179656 | tf_op jit(solution)/shard_map/ppermute | solution.py:352
  118.3 30.7 %collective-permute-start.28 = (bf16[8,96,256]{2,1,0:T(8,128)(2,1)S(1)}, bf16[8,96,256]{2,1,0:T(8,128)(2,1)S(1)}, u32[]{:S(2)}, u32[]{:S(2)}) collective-permute-start(bf16[8,96,256]{2,1,0:T(8,128)(2,1)S(1)} %get-tuple-element.65.refs_1_), channel_id=1, source_target_pairs={{0,1},{1,2},{2,3},{3,0},{4,5},{5,6},{6,7},{7,4},{8,9},{9,10},{10,1... | collective-permute-start | bytes 1179656 | tf_op jit(solution)/shard_map/ppermute | solution.py:352
  126.6 24.6 %collective-permute-start.22 = (bf16[8,96,256]{2,1,0:T(8,128)(2,1)S(1)}, bf16[8,96,256]{2,1,0:T(8,128)(2,1)S(1)}, u32[]{:S(2)}, u32[]{:S(2)}) collective-permute-start(bf16[8,96,256]{2,1,0:T(8,128)(2,1)S(1)} %get-tuple-element.64.refs_2_), channel_id=1, source_target_pairs={{0,1},{1,2},{2,3},{3,0},{4,5},{5,6},{6,7},{7,4},{8,9},{9,10},{10,1... | collective-permute-start | bytes 1179656 | tf_op jit(solution)/shard_map/ppermute | solution.py:352
  128.6 23.9 %collective-permute-start.24 = (bf16[8,96,256]{2,1,0:T(8,128)(2,1)S(1)}, bf16[8,96,256]{2,1,0:T(8,128)(2,1)S(1)}, u32[]{:S(2)}, u32[]{:S(2)}) collective-permute-start(bf16[8,96,256]{2,1,0:T(8,128)(2,1)S(1)} %get-tuple-element.63.refs_3_), channel_id=1, source_target_pairs={{0,3},{1,0},{2,1},{3,2},{4,7},{5,4},{6,5},{7,6},{8,11},{9,8},{10,9... | collective-permute-start | bytes 1179656 | tf_op jit(solution)/shard_map/ppermute | solution.py:352
  130.0 23.4 %collective-permute-start.27 = (bf16[8,96,256]{2,1,0:T(8,128)(2,1)S(1)}, bf16[8,96,256]{2,1,0:T(8,128)(2,1)S(1)}, u32[]{:S(2)}, u32[]{:S(2)}) collective-permute-start(bf16[8,96,256]{2,1,0:T(8,128)(2,1)S(1)} %get-tuple-element.64.refs_2_), channel_id=1, source_target_pairs={{0,3},{1,0},{2,1},{3,2},{4,7},{5,4},{6,5},{7,6},{8,11},{9,8},{10,9... | collective-permute-start | bytes 1179656 | tf_op jit(solution)/shard_map/ppermute | solution.py:352
  135.5 20.3 %collective-permute-start.29 = (bf16[8,96,256]{2,1,0:T(8,128)(2,1)S(1)}, bf16[8,96,256]{2,1,0:T(8,128)(2,1)S(1)}, u32[]{:S(2)}, u32[]{:S(2)}) collective-permute-start(bf16[8,96,256]{2,1,0:T(8,128)(2,1)S(1)} %get-tuple-element.63.refs_3_), channel_id=1, source_target_pairs={{0,1},{1,2},{2,3},{3,0},{4,5},{5,6},{6,7},{7,4},{8,9},{9,10},{10,1... | collective-permute-start | bytes 1179656 | tf_op jit(solution)/shard_map/ppermute | solution.py:352
  149.0 17.0 %collective-permute-start.20 = (bf16[8,96,256]{2,1,0:T(8,128)(2,1)S(1)}, bf16[8,96,256]{2,1,0:T(8,128)(2,1)S(1)}, u32[]{:S(2)}, u32[]{:S(2)}) collective-permute-start(bf16[8,96,256]{2,1,0:T(8,128)(2,1)S(1)} %collective-permute-done.12.refs_4_), channel_id=1, source_target_pairs={{0,1},{1,2},{2,3},{3,0},{4,5},{5,6},{6,7},{7,4},{8,9},{9,10},{10,1... | collective-permute-start | bytes 1179656 | tf_op jit(solution)/shard_map/ppermute | solution.py:352
  151.2 14.8 %collective-permute-start.21 = (bf16[8,96,256]{2,1,0:T(8,128)(2,1)S(1)}, bf16[8,96,256]{2,1,0:T(8,128)(2,1)S(1)}, u32[]{:S(2)}, u32[]{:S(2)}) collective-permute-start(bf16[8,96,256]{2,1,0:T(8,128)(2,1)S(1)} %collective-permute-done.13.refs_1_), channel_id=1, source_target_pairs={{0,3},{1,0},{2,1},{3,2},{4,7},{5,4},{6,5},{7,6},{8,11},{9,8},{10,9... | collective-permute-start | bytes 1179656 | tf_op jit(solution)/shard_map/ppermute | solution.py:352
  152.5 13.8 %collective-permute-start.23 = (bf16[8,96,256]{2,1,0:T(8,128)(2,1)S(1)}, bf16[8,96,256]{2,1,0:T(8,128)(2,1)S(1)}, u32[]{:S(2)}, u32[]{:S(2)}) collective-permute-start(bf16[8,96,256]{2,1,0:T(8,128)(2,1)S(1)} %collective-permute-done.22.refs_6_), channel_id=1, source_target_pairs={{0,1},{1,2},{2,3},{3,0},{4,5},{5,6},{6,7},{7,4},{8,9},{9,10},{10,1... | collective-permute-start | bytes 1179656 | tf_op jit(solution)/shard_map/ppermute | solution.py:352
  153.3 13.4 %collective-permute-start.25 = (bf16[8,96,256]{2,1,0:T(8,128)(2,1)S(1)}, bf16[8,96,256]{2,1,0:T(8,128)(2,1)S(1)}, u32[]{:S(2)}, u32[]{:S(2)}) collective-permute-start(bf16[8,96,256]{2,1,0:T(8,128)(2,1)S(1)} %collective-permute-done.24.refs_3_), channel_id=1, source_target_pairs={{0,3},{1,0},{2,1},{3,2},{4,7},{5,4},{6,5},{7,6},{8,11},{9,8},{10,9... | collective-permute-start | bytes 1179656 | tf_op jit(solution)/shard_map/ppermute | solution.py:352
  (9 other events, 51.9 us)

commit v6 on v5

--- a/solution.py
+++ b/solution.py
@@ -254,9 +254,11 @@
     rows = raw.shape[2]
     width = len(turns) * rows
     quarter = blocks[0, 1] // quarter_shells
-    strips = 2
-    tile = vir.shape[0] // strips
-
+    target = held if last else out
+
+    keep = []
+    if more:
+        keep = [pltpu.make_async_copy(earlier, target, arrived.at[len(given)])]
     collect = []
     for at, part in enumerate(given):
         begin = (at % count) * part.shape[0]
@@ -265,7 +267,7 @@
                 part, raw.at[at // count, begin : begin + part.shape[0]], arrived.at[at]
             )
         )
-    for copy in collect:
+    for copy in collect + keep:
         copy.start()
     for copy in collect:
         copy.wait()
@@ -277,41 +279,24 @@
 
     fill(owner, raw, put)
 
-    columns = GRP * rows
-    source = lax.broadcasted_iota(jnp.int32, (width, columns), 0)
-    target = lax.broadcasted_iota(jnp.int32, (width, columns), 1)
-    pick = target < 0
+    both = lax.dot_general(
+        vir[...], panel[...], (((1,), (1,)), ((), ())), preferred_element_type=F32
+    ).astype(BF)
+    for copy in keep:
+        copy.wait()
     for k, r in enumerate(turns):
-        moved = (lax.rem(quarter + r, GRP) - k) * rows
-        pick = pick | ((source // rows == k) & (target == source + moved))
-    pick = jnp.where(pick, 1.0, 0.0).astype(BF)
-    stores = []
-    for k in range(strips):
-        here = slice(k * tile, (k + 1) * tile)
-        both = lax.dot_general(
-            vir[here, :], panel[...], (((1,), (1,)), ((), ())), preferred_element_type=F32
-        ).astype(BF)
-        for i in range(2):
-            value = jnp.dot(
-                both[:, i * width : (i + 1) * width], pick, preferred_element_type=F32
-            )
-            if more:
-                value = value + earlier[i, here, :].astype(F32)
-            if last:
-                held[i, here, :] = value.astype(BF)
-            else:
-                out[i, here, :] = value.astype(BF)
-        if last:
-            stores.append(
-                pltpu.make_async_copy(
-                    held.at[:, here, :],
-                    out.at[:, here, :],
-                    arrived.at[len(given) + k],
-                )
-            )
-            stores[-1].start()
-    for copy in stores:
-        copy.wait()
+        for q in range(GRP):
+
+            @pl.when(lax.rem(quarter + r, GRP) == q)
+            def _():
+                for i in range(2):
+                    begin = i * width + k * rows
+                    target[i, :, q * rows : (q + 1) * rows] = both[:, begin : begin + rows]
+
+    if last:
+        store = pltpu.make_async_copy(held, out, arrived.at[len(given) + 1])
+        store.start()
+        store.wait()
 
 
 def add_columns(vir, blocks, owner, shell, turns, pieces, earlier=None, last=False):

time: 178 us -> 175 us (0.983)
  Pallas kernels: 42.8 us -> 38.1 us
    pallas_call x3, Pallas kernels: 29.5 us -> 24.8 us  [add_columns(): pl.pallas_call(functools.partial(columns_kernel, quarter_shells=nus // sh...]
  transfers between devices with their start and end apart: 34 -> 34, of which waited for: 19 -> 20; matrix products, arithmetic and copies ran while one was open for 5% -> 5% of each run, Pallas kernels for 15% -> 13%
where the time goes in v6:
time: 175 us
  starting transfers between devices  67 us (38%)
  waiting for transfers between devices  54.5 us (31%)
  Pallas kernels  38.1 us (22%)
  local copies, waits for them, and re-layouts  6.38 us (4%)
  other arithmetic  4.83 us (3%)
  matrix products  3.48 us (2%)
    ppermute x28, starting transfers between devices, shift(): return lax.ppermute(value, 'grp', [(j, (j + by) % GRP) for j in range(GRP)])  43.2 us
    ppermute x28, waiting for transfers between devices, shift(): return lax.ppermute(value, 'grp', [(j, (j + by) % GRP) for j in range(GRP)])  33.9 us
    pallas_call x3, Pallas kernels, add_columns(): pl.pallas_call(functools.partial(columns_kernel, quarter_shells=nus // sh...  24.8 us
    all_to_all x4, starting transfers between devices, exchange(): lax.all_to_all(value, 'aux', split_axis=0, concat_axis=0, axis_index_grou...  23.6 us
    all_to_all x4, waiting for transfers between devices, exchange(): lax.all_to_all(value, 'aux', split_axis=0, concat_axis=0, axis_index_grou...  19.4 us
    pallas_call x1, Pallas kernels, partial_pieces(): pl.pallas_call(functools.partial(far_kernel, groups=groups, quarter_shell...  6.94 us
    pallas_call x1, Pallas kernels, partial_pieces(): pl.pallas_call(functools.partial(near_kernel, slots=slots, groups=groups)...  6.36 us
    unnamed x15, local copies, waits for them, and re-layouts  5.68 us
  transfers between devices with their start and end apart: 34, of which 20 were waited for; matrix products, arithmetic and copies ran while one was open for 5% of the time, Pallas kernels for 13%

profile of v6, /device:TPU:0, one launch (start us, length us, event | category | flops | bytes accessed | tf_op | source)
XLA Modules:
  0.0 174.8 jit_solution(16362600831946099131)
XLA Ops:
  2.1 6.9 %far_rows.1 = (bf16[288,512]{1,0:T(8,128)(2,1)S(1)}, bf16[8,96,256]{2,1,0:T(8,128)(2,1)S(1)}, bf16[8,96,256]{2,1,0:T(8,128)(2,1)S(1)}, bf16[8,96,256]{2,1,0:T(8,128)(2,1)S(1)}, bf16[8,96,256]{2,1,0:T(8,128)(2,1)S(1)}) custom-call(s32[8,4]{1,0:T(8,128)S(1)} %copy.23.blocks, s32[128]{0:T(128)S(1)} %copy-done.2, bf16[2,4352]{1,0:T(2,128)(2,1)S(1)} %copy-done.4, ...), custom_call_target="tpu_custom_call" | custom-call | flops 1073741824 | bytes 10485760 | tf_op jit(solution)/shard_map/far_rows/pallas_call | solution.py:182
  14.4 6.4 %near_rows.1 = (bf16[16,96,256]{2,1,0:T(8,128)(2,1)S(1)}, bf16[8,96,256]{2,1,0:T(8,128)(2,1)S(1)}, bf16[8,96,256]{2,1,0:T(8,128)(2,1)S(1)}, bf16[8,96,256]{2,1,0...) custom-call(s32[8,4]{1,0:T(8,128)S(1)} %copy.23.blocks, ...), custom_call_target="tpu_custom_call" | custom-call | flops 2147483648 | bytes 8388608 | tf_op jit(solution)/shard_map/near_rows/pallas_call | solution.py:203
  24.3 1.7 collective-permute-start.6
  26.1 1.7 collective-permute-start.7
  28.0 3.2 %collective-permute-done.4 = bf16[8,96,256]{2,1,0:T(8,128)(2,1)S(1)} collective-permute-done((bf16[8,96,256]{2,1,0:T(8,128)(2,1)S(1)}, bf16[8,96,256]{2,1,0:T(8,128)(2,1)S(1)}, u32[]{:S(2)}, u32[]{:S(2)}) %collective-permute-start.4) | collective-permute-done | bytes 393248 | tf_op jit(solution)/shard_map/ppermute | solution.py:337
  33.1 6.2 %collective-permute-done.5 = bf16[8,96,256]{2,1,0:T(8,128)(2,1)S(1)} collective-permute-done((bf16[8,96,256]{2,1,0:T(8,128)(2,1)S(1)}, bf16[8,96,256]{2,1,0:T(8,128)(2,1)S(1)}, u32[]{:S(2)}, u32[]{:S(2)}) %collective-permute-start.5) | collective-permute-done | bytes 393248 | tf_op jit(solution)/shard_map/ppermute | solution.py:337
  41.1 1.7 collective-permute-start.15
  42.9 5.2 %collective-permute-done.7 = bf16[8,96,256]{2,1,0:T(8,128)(2,1)S(1)} collective-permute-done((bf16[8,96,256]{2,1,0:T(8,128)(2,1)S(1)}, bf16[8,96,256]{2,1,0:T(8,128)(2,1)S(1)}, u32[]{:S(2)}, u32[]{:S(2)}) %collective-permute-start.7) | collective-permute-done | bytes 393248 | tf_op jit(solution)/shard_map/ppermute | solution.py:337
  49.4 8.1 %all-to-all-start = ((bf16[16,96,256]{2,1,0:T(8,128)(2,1)}), bf16[16,96,256]{2,1,0:T(8,128)(2,1)S(1)}, u32[]{:S(2)}, u32[]{:S(2)}) async-start(bf16[16,96,256]{2,1,0:T(8,128)(2,1)} %pad_maximum_fusion.2), calls=%async_computation | async-start | bytes 1572864 | tf_op jit(solution)/shard_map/all_to_all | solution.py:386
  58.0 5.4 %collective-permute-done.14 = bf16[16,96,256]{2,1,0:T(8,128)(2,1)} collective-permute-done((bf16[16,96,256]{2,1,0:T(8,128)(2,1)S(1)}, bf16[16,96,256]{2,1,0:T(8,128)(2,1)}, u32[]{:S(2)}, u32[]{:S(2)}) %collective-permute-start.14) | collective-permute-done | bytes 786464 | tf_op jit(solution)/shard_map/ppermute | solution.py:337
  63.5 2.6 %add_convert_fusion = bf16[16,96,256]{2,1,0:T(8,128)(2,1)} fusion(bf16[16,96,256]{2,1,0:T(8,128)(2,1)} %collective-permute-done.15, bf16[16,96,256]{2,1,0:T(8,128)(2,1)} %collective-permute-done.14, bf16[16,96,256]{2,1,0:T(8,128)(2,1)S(1)} %get-tuple-element.51), kind=kLoop, calls=%fused_computation.2 | loop fusion | flops 2359296 | bytes 3145728 | tf_op jit(solution)/shard_map/convert_element_type | solution.py:341
  66.2 3.3 %all-to-all-done = bf16[16,96,256]{2,1,0:T(8,128)(2,1)S(1)} async-done(((bf16[16,96,256]{2,1,0:T(8,128)(2,1)}), bf16[16,96,256]{2,1,0:T(8,128)(2,1)S(1)}, u32[]{:S(2)}, u32[]{:S(2)}) %all-to-all-start) | async-done | bytes 786464 | tf_op jit(solution)/shard_map/all_to_all | solution.py:386
  69.4 4.9 %all-to-all-start.2 = ((bf16[16,96,256]{2,1,0:T(8,128)(2,1)}), bf16[16,96,256]{2,1,0:T(8,128)(2,1)S(1)}, u32[]{:S(2)}, u32[]{:S(2)}) async-start(bf16[16,96,256]{2,1,0:T(8,128)(2,1)} %add_convert_fusion), calls=%async_computation.2 | async-start | bytes 1572864 | tf_op jit(solution)/shard_map/all_to_all | solution.py:386
  76.4 2.8 %collective-permute-start.10 = (bf16[256,256]{1,0:T(8,128)(2,1)S(1)}, bf16[256,256]{1,0:T(8,128)(2,1)S(1)}, u32[]{:S(2)}, u32[]{:S(2)}) collective-permute-start(bf16[256,256]{1,0:T(8,128)(2,1)S(1)} %get-tuple-element.61), channel_id=1, source_target_pairs={{0,2},{1,3},{2,0},{3,1},{4,6},{5,7},{6,4},{7,5},{8,10},{9,11},{10,... | collective-permute-start | bytes 393224 | tf_op jit(solution)/shard_map/ppermute | solution.py:337
  81.3 6.5 %all-to-all-done.2 = bf16[16,96,256]{2,1,0:T(8,128)(2,1)S(1)} async-done(((bf16[16,96,256]{2,1,0:T(8,128)(2,1)}), bf16[16,96,256]{2,1,0:T(8,128)(2,1)S(1)}, u32[]{:S(2)}, u32[]{:S(2)}) %all-to-all-start.2) | async-done | bytes 786464 | tf_op jit(solution)/shard_map/all_to_all | solution.py:386
  89.7 5.9 %all-to-all-start.1 = ((bf16[16,96,256]{2,1,0:T(8,128)(2,1)}), bf16[16,96,256]{2,1,0:T(8,128)(2,1)S(1)}, u32[]{:S(2)}, u32[]{:S(2)}) async-start(bf16[16,96,256]{2,1,0:T(8,128)(2,1)} %bitcast.2), calls=%async_computation.1 | async-start | bytes 1572864 | tf_op jit(solution)/shard_map/all_to_all | solution.py:386
  96.5 2.9 %collective-permute-start.18 = (bf16[256,256]{1,0:T(8,128)(2,1)S(1)}, bf16[256,256]{1,0:T(8,128)(2,1)S(1)}, u32[]{:S(2)}, u32[]{:S(2)}) collective-permute-start(bf16[256,256]{1,0:T(8,128)(2,1)S(1)} %get-tuple-element.59), channel_id=1, source_target_pairs={{0,2},{1,3},{2,0},{3,1},{4,6},{5,7},{6,4},{7,5},{8,10},{9,11},{10,... | collective-permute-start | bytes 393224 | tf_op jit(solution)/shard_map/ppermute | solution.py:337
  100.5 1.8 %collective-permute-done.17 = bf16[256,256]{1,0:T(8,128)(2,1)S(1)} collective-permute-done((bf16[256,256]{1,0:T(8,128)(2,1)S(1)}, bf16[256,256]{1,0:T(8,128)(2,1)S(1)}, u32[]{:S(2)}, u32[]{:S(2)}) %collective-permute-start.17) | collective-permute-done | bytes 131104 | tf_op jit(solution)/shard_map/ppermute | solution.py:337
  102.3 3.1 %collective-permute-done.18 = bf16[256,256]{1,0:T(8,128)(2,1)S(1)} collective-permute-done((bf16[256,256]{1,0:T(8,128)(2,1)S(1)}, bf16[256,256]{1,0:T(8,128)(2,1)S(1)}, u32[]{:S(2)}, u32[]{:S(2)}) %collective-permute-start.18) | collective-permute-done | bytes 131104 | tf_op jit(solution)/shard_map/ppermute | solution.py:337
  106.8 2.2 %all-to-all-done.1 = bf16[16,96,256]{2,1,0:T(8,128)(2,1)S(1)} async-done(((bf16[16,96,256]{2,1,0:T(8,128)(2,1)}), bf16[16,96,256]{2,1,0:T(8,128)(2,1)S(1)}, u32[]{:S(2)}, u32[]{:S(2)}) %all-to-all-start.1) | async-done | bytes 786464 | tf_op jit(solution)/shard_map/all_to_all | solution.py:386
  109.0 4.8 %all-to-all-start.3 = ((bf16[16,96,256]{2,1,0:T(8,128)(2,1)}), bf16[16,96,256]{2,1,0:T(8,128)(2,1)S(1)}, u32[]{:S(2)}, u32[]{:S(2)}) async-start(bf16[16,96,256]{2,1,0:T(8,128)(2,1)} %bitcast.5), calls=%async_computation.3 | async-start | bytes 1572864 | tf_op jit(solution)/shard_map/all_to_all | solution.py:386
  115.0 2.1 %collective-permute-start.13 = (bf16[8,96,256]{2,1,0:T(8,128)(2,1)S(1)}, bf16[8,96,256]{2,1,0:T(8,128)(2,1)S(1)}, u32[]{:S(2)}, u32[]{:S(2)}) collective-permute-start(bf16[8,96,256]{2,1,0:T(8,128)(2,1)S(1)} %get-tuple-element.65.refs_1_), channel_id=1, source_target_pairs={{0,3},{1,0},{2,1},{3,2},{4,7},{5,4},{6,5},{7,6},{8,11},{9,8},{10,9... | collective-permute-start | bytes 1179656 | tf_op jit(solution)/shard_map/ppermute | solution.py:337
  119.1 7.4 %all-to-all-done.3 = bf16[16,96,256]{2,1,0:T(8,128)(2,1)S(1)} async-done(((bf16[16,96,256]{2,1,0:T(8,128)(2,1)}), bf16[16,96,256]{2,1,0:T(8,128)(2,1)S(1)}, u32[]{:S(2)}, u32[]{:S(2)}) %all-to-all-start.3) | async-done | bytes 786464 | tf_op jit(solution)/shard_map/all_to_all | solution.py:386
  126.6 1.9 %collective-permute-start.22 = (bf16[8,96,256]{2,1,0:T(8,128)(2,1)S(1)}, bf16[8,96,256]{2,1,0:T(8,128)(2,1)S(1)}, u32[]{:S(2)}, u32[]{:S(2)}) collective-permute-start(bf16[8,96,256]{2,1,0:T(8,128)(2,1)S(1)} %get-tuple-element.64.refs_2_), channel_id=1, source_target_pairs={{0,1},{1,2},{2,3},{3,0},{4,5},{5,6},{6,7},{7,4},{8,9},{9,10},{10,1... | collective-permute-start | bytes 1179656 | tf_op jit(solution)/shard_map/ppermute | solution.py:337
  131.4 4.1 %collective-permute-done.26.refs_0_ = bf16[8,96,256]{2,1,0:T(8,128)(2,1)S(1)} collective-permute-done((bf16[8,96,256]{2,1,0:T(8,128)(2,1)S(1)}, bf16[8,96,256]{2,1,0:T(8,128)(2,1)S(1)}, u32[]{:S(2)}, u32[]{:S(2)}) %collective-permute-start.26) | collective-permute-done | bytes 393248 | tf_op jit(solution)/shard_map/ppermute | solution.py:337
  136.3 3.5 %copy-done.1 = bf16[1088,4096]{1,0:T(8,128)(2,1)S(1)} copy-done((bf16[1088,4096]{1,0:T(8,128)(2,1)S(1)}, bf16[1088,4096]{1,0:T(8,128)(2,1)}, u32[]{:S(2)}) %copy-start.1) | copy-done | bytes 8912920
  139.8 6.4 %add_columns.3.refs_8_ = bf16[2,1088,384]{2,1,0:T(8,128)(2,1)S(1)} custom-call(s32[8,4]{1,0:T(8,128)S(1)} %copy.23.blocks, s32[128]{0:T(128)S(1)} %copy-done.3, bf16[1088,4096]{1,0:T(8,128)(2,1)S(1)} %copy-done.1, bf16[8,96,256]{2,1,0:T(8,128)(2,1)S(1)} %get-tuple-element.66.refs_0_, bf16[8,96,256]{2,1,0:T(8,128)(2,1)S(1)} %get-tuple-element.65.refs_1_, ...), custom_call_target="tpu_custom_call" | custom-call | flops 1711276032 | bytes 12582912 | tf_op jit(solution)/shard_map/add_columns/pallas_call | solution.py:309
  146.2 2.2 %collective-permute-start.20 = (bf16[8,96,256]{2,1,0:T(8,128)(2,1)S(1)}, bf16[8,96,256]{2,1,0:T(8,128)(2,1)S(1)}, u32[]{:S(2)}, u32[]{:S(2)}) collective-permute-start(bf16[8,96,256]{2,1,0:T(8,128)(2,1)S(1)} %collective-permute-done.12.refs_4_), channel_id=1, source_target_pairs={{0,1},{1,2},{2,3},{3,0},{4,5},{5,6},{6,7},{7,4},{8,9},{9,10},{10,1... | collective-permute-start | bytes 1179656 | tf_op jit(solution)/shard_map/ppermute | solution.py:337
  150.6 1.7 collective-permute-done.27.refs_2_
  152.4 3.3 %collective-permute-start.25 = (bf16[8,96,256]{2,1,0:T(8,128)(2,1)S(1)}, bf16[8,96,256]{2,1,0:T(8,128)(2,1)S(1)}, u32[]{:S(2)}, u32[]{:S(2)}) collective-permute-start(bf16[8,96,256]{2,1,0:T(8,128)(2,1)S(1)} %collective-permute-done.24.refs_3_), channel_id=1, source_target_pairs={{0,3},{1,0},{2,1},{3,2},{4,7},{5,4},{6,5},{7,6},{8,11},{9,8},{10,9... | collective-permute-start | bytes 1179656 | tf_op jit(solution)/shard_map/ppermute | solution.py:337
  155.7 10.5 %add_columns.4.refs_4_ = bf16[2,1088,384]{2,1,0:T(8,128)(2,1)S(1)} custom-call(s32[8,4]{1,0:T(8,128)S(1)} %copy.23.blocks, s32[128]{0:T(128)S(1)} %copy-done.3, bf16[1088,4096]{1,0:T(8,128)(2,1)S(1)} %copy-done.1, bf16[8,96,256]{2,1,0:T(8,128)(2,1)S(1)} %collective-permute-done.26.refs_0_, bf16[8,96,256]{2,1,0:T(8,128)(2,1)S(1)} %collective-permute-done.13.refs_1_, ...), custom_call_target="tpu_custom_call" | custom-call | flops 3422552064 | bytes 12582912 | tf_op jit(solution)/shard_map/add_columns/pallas_call | solution.py:309
  166.7 7.9 %add_columns.5 = bf16[2,1088,384]{2,1,0:T(8,128)(2,1)} custom-call(s32[8,4]{1,0:T(8,128)S(1)} %copy.23.blocks, s32[128]{0:T(128)S(1)} %copy-done.3, bf16[1088,4096]{1,0:T(8,128)(2,1)S(1)} %copy-done.1, bf16[8,96,256]{2,1,0:T(8,128)(2,1)S(1)} %collective-permute-done.20.refs_0_, bf16[8,96,256]{2,1,0:T(8,128)(2,1)S(1)} %collective-permute-done.21.refs_1_, ...), custom_call_target="tpu_custom_call" | custom-call | flops 1711276032 | bytes 12582912 | tf_op jit(solution)/shard_map/add_columns/pallas_call | solution.py:309
  (85 shorter events, 35.9 us)
Async XLA Ops:
  9.1 13.3 %collective-permute-start = (bf16[8,96,256]{2,1,0:T(8,128)(2,1)S(1)}, bf16[8,96,256]{2,1,0:T(8,128)(2,1)S(1)}, u32[]{:S(2)}, u32[]{:S(2)}) collective-permute-start(bf16[8,96,256]{2,1,0:T(8,128)(2,1)S(1)} %get-tuple-element.36), channel_id=1, source_target_pairs={{0,1},{1,2},{2,3},{3,0},{4,5},{5,6},{6,7},{7,4},{8,9},{9,10},{10,1... | collective-permute-start | bytes 1179656 | tf_op jit(solution)/shard_map/ppermute | solution.py:337
  10.7 12.0 %collective-permute-start.1 = (bf16[8,96,256]{2,1,0:T(8,128)(2,1)S(1)}, bf16[8,96,256]{2,1,0:T(8,128)(2,1)S(1)}, u32[]{:S(2)}, u32[]{:S(2)}) collective-permute-start(bf16[8,96,256]{2,1,0:T(8,128)(2,1)S(1)} %get-tuple-element.37), channel_id=1, source_target_pairs={{0,3},{1,0},{2,1},{3,2},{4,7},{5,4},{6,5},{7,6},{8,11},{9,8},{10,9... | collective-permute-start | bytes 1179656 | tf_op jit(solution)/shard_map/ppermute | solution.py:337
  12.4 18.8 %collective-permute-start.4 = (bf16[8,96,256]{2,1,0:T(8,128)(2,1)S(1)}, bf16[8,96,256]{2,1,0:T(8,128)(2,1)S(1)}, u32[]{:S(2)}, u32[]{:S(2)}) collective-permute-start(bf16[8,96,256]{2,1,0:T(8,128)(2,1)S(1)} %get-tuple-element.44), channel_id=1, source_target_pairs={{0,3},{1,0},{2,1},{3,2},{4,7},{5,4},{6,5},{7,6},{8,11},{9,8},{10,9... | collective-permute-start | bytes 1179656 | tf_op jit(solution)/shard_map/ppermute | solution.py:337
  14.0 18.9 %collective-permute-start.3 = (bf16[8,96,256]{2,1,0:T(8,128)(2,1)S(1)}, bf16[8,96,256]{2,1,0:T(8,128)(2,1)S(1)}, u32[]{:S(2)}, u32[]{:S(2)}) collective-permute-start(bf16[8,96,256]{2,1,0:T(8,128)(2,1)S(1)} %get-tuple-element.40), channel_id=1, source_target_pairs={{0,1},{1,2},{2,3},{3,0},{4,5},{5,6},{6,7},{7,4},{8,9},{9,10},{10,1... | collective-permute-start | bytes 1179656 | tf_op jit(solution)/shard_map/ppermute | solution.py:337
  22.8 16.5 %collective-permute-start.5 = (bf16[8,96,256]{2,1,0:T(8,128)(2,1)S(1)}, bf16[8,96,256]{2,1,0:T(8,128)(2,1)S(1)}, u32[]{:S(2)}, u32[]{:S(2)}) collective-permute-start(bf16[8,96,256]{2,1,0:T(8,128)(2,1)S(1)} %get-tuple-element.45), channel_id=1, source_target_pairs={{0,1},{1,2},{2,3},{3,0},{4,5},{5,6},{6,7},{7,4},{8,9},{9,10},{10,1... | collective-permute-start | bytes 1179656 | tf_op jit(solution)/shard_map/ppermute | solution.py:337
  24.3 15.4 %collective-permute-start.6 = (bf16[8,96,256]{2,1,0:T(8,128)(2,1)S(1)}, bf16[8,96,256]{2,1,0:T(8,128)(2,1)S(1)}, u32[]{:S(2)}, u32[]{:S(2)}) collective-permute-start(bf16[8,96,256]{2,1,0:T(8,128)(2,1)S(1)} %get-tuple-element.46), channel_id=1, source_target_pairs={{0,3},{1,0},{2,1},{3,2},{4,7},{5,4},{6,5},{7,6},{8,11},{9,8},{10,9... | collective-permute-start | bytes 1179656 | tf_op jit(solution)/shard_map/ppermute | solution.py:337
  26.1 21.9 %collective-permute-start.7 = (bf16[8,96,256]{2,1,0:T(8,128)(2,1)S(1)}, bf16[8,96,256]{2,1,0:T(8,128)(2,1)S(1)}, u32[]{:S(2)}, u32[]{:S(2)}) collective-permute-start(bf16[8,96,256]{2,1,0:T(8,128)(2,1)S(1)} %add_convert_fusion.2), channel_id=1, source_target_pairs={{0,3},{1,0},{2,1},{3,2},{4,7},{5,4},{6,5},{7,6},{8,11},{9,8},{10,9... | collective-permute-start | bytes 1179656 | tf_op jit(solution)/shard_map/ppermute | solution.py:337
  31.2 16.9 %collective-permute-start.2 = (bf16[8,96,256]{2,1,0:T(8,128)(2,1)S(1)}, bf16[8,96,256]{2,1,0:T(8,128)(2,1)S(1)}, u32[]{:S(2)}, u32[]{:S(2)}) collective-permute-start(bf16[8,96,256]{2,1,0:T(8,128)(2,1)S(1)} %add_convert_fusion.6), channel_id=1, source_target_pairs={{0,1},{1,2},{2,3},{3,0},{4,5},{5,6},{6,7},{7,4},{8,9},{9,10},{10,1... | collective-permute-start | bytes 1179656 | tf_op jit(solution)/shard_map/ppermute | solution.py:337
  39.6 23.7 %collective-permute-start.14 = (bf16[16,96,256]{2,1,0:T(8,128)(2,1)S(1)}, bf16[16,96,256]{2,1,0:T(8,128)(2,1)}, u32[]{:S(2)}, u32[]{:S(2)}) collective-permute-start(bf16[16,96,256]{2,1,0:T(8,128)(2,1)S(1)} %pad_maximum_fusion), channel_id=1, source_target_pairs={{0,1},{1,2},{2,3},{3,0},{4,5},{5,6},{6,7},{7,4},{8,9},{9,10},{10,1... | collective-permute-start | bytes 2359304 | tf_op jit(solution)/shard_map/ppermute | solution.py:337
  41.1 22.4 %collective-permute-start.15 = (bf16[16,96,256]{2,1,0:T(8,128)(2,1)S(1)}, bf16[16,96,256]{2,1,0:T(8,128)(2,1)}, u32[]{:S(2)}, u32[]{:S(2)}) collective-permute-start(bf16[16,96,256]{2,1,0:T(8,128)(2,1)S(1)} %pad_maximum_fusion.1), channel_id=1, source_target_pairs={{0,3},{1,0},{2,1},{3,2},{4,7},{5,4},{6,5},{7,6},{8,11},{9,8},{10,9... | collective-permute-start | bytes 2359304 | tf_op jit(solution)/shard_map/ppermute | solution.py:337
  49.4 20.0 %all-to-all-start = ((bf16[16,96,256]{2,1,0:T(8,128)(2,1)}), bf16[16,96,256]{2,1,0:T(8,128)(2,1)S(1)}, u32[]{:S(2)}, u32[]{:S(2)}) async-start(bf16[16,96,256]{2,1,0:T(8,128)(2,1)} %pad_maximum_fusion.2), calls=%async_computation | async-start | bytes 1572864 | tf_op jit(solution)/shard_map/all_to_all | solution.py:386
  69.4 18.4 %all-to-all-start.2 = ((bf16[16,96,256]{2,1,0:T(8,128)(2,1)}), bf16[16,96,256]{2,1,0:T(8,128)(2,1)S(1)}, u32[]{:S(2)}, u32[]{:S(2)}) async-start(bf16[16,96,256]{2,1,0:T(8,128)(2,1)} %add_convert_fusion), calls=%async_computation.2 | async-start | bytes 1572864 | tf_op jit(solution)/shard_map/all_to_all | solution.py:386
  76.4 11.9 %collective-permute-start.10 = (bf16[256,256]{1,0:T(8,128)(2,1)S(1)}, bf16[256,256]{1,0:T(8,128)(2,1)S(1)}, u32[]{:S(2)}, u32[]{:S(2)}) collective-permute-start(bf16[256,256]{1,0:T(8,128)(2,1)S(1)} %get-tuple-element.61), channel_id=1, source_target_pairs={{0,2},{1,3},{2,0},{3,1},{4,6},{5,7},{6,4},{7,5},{8,10},{9,11},{10,... | collective-permute-start | bytes 393224 | tf_op jit(solution)/shard_map/ppermute | solution.py:337
  79.2 9.1 %collective-permute-start.11 = (bf16[256,256]{1,0:T(8,128)(2,1)S(1)}, bf16[256,256]{1,0:T(8,128)(2,1)S(1)}, u32[]{:S(2)}, u32[]{:S(2)}) collective-permute-start(bf16[256,256]{1,0:T(8,128)(2,1)S(1)} %get-tuple-element.61), channel_id=1, source_target_pairs={{0,3},{1,0},{2,1},{3,2},{4,7},{5,4},{6,5},{7,6},{8,11},{9,8},{10,9... | collective-permute-start | bytes 393224 | tf_op jit(solution)/shard_map/ppermute | solution.py:337
  80.7 7.6 %collective-permute-start.9 = (bf16[256,256]{1,0:T(8,128)(2,1)S(1)}, bf16[256,256]{1,0:T(8,128)(2,1)S(1)}, u32[]{:S(2)}, u32[]{:S(2)}) collective-permute-start(bf16[256,256]{1,0:T(8,128)(2,1)S(1)} %get-tuple-element.61), channel_id=1, source_target_pairs={{0,1},{1,2},{2,3},{3,0},{4,5},{5,6},{6,7},{7,4},{8,9},{9,10},{10,1... | collective-permute-start | bytes 393224 | tf_op jit(solution)/shard_map/ppermute | solution.py:337
  88.2 7.3 %collective-permute-start.16 = (f32[256,256]{1,0:T(8,128)S(1)}, f32[256,256]{1,0:T(8,128)S(1)}, u32[]{:S(2)}, u32[]{:S(2)}) collective-permute-start(f32[256,256]{1,0:T(8,128)S(1)} %convolution_bitcast_fusion), channel_id=1, source_target_pairs={{0,4},{4,0},{8,12},{12,8},{16,20},{20,16},{24,28},{28,24},{32,36},... | collective-permute-start | bytes 786440 | tf_op jit(solution)/shard_map/ppermute | solution.py:397
  89.7 19.3 %all-to-all-start.1 = ((bf16[16,96,256]{2,1,0:T(8,128)(2,1)}), bf16[16,96,256]{2,1,0:T(8,128)(2,1)S(1)}, u32[]{:S(2)}, u32[]{:S(2)}) async-start(bf16[16,96,256]{2,1,0:T(8,128)(2,1)} %bitcast.2), calls=%async_computation.1 | async-start | bytes 1572864 | tf_op jit(solution)/shard_map/all_to_all | solution.py:386
  95.6 6.7 %collective-permute-start.17 = (bf16[256,256]{1,0:T(8,128)(2,1)S(1)}, bf16[256,256]{1,0:T(8,128)(2,1)S(1)}, u32[]{:S(2)}, u32[]{:S(2)}) collective-permute-start(bf16[256,256]{1,0:T(8,128)(2,1)S(1)} %get-tuple-element.59), channel_id=1, source_target_pairs={{0,1},{1,2},{2,3},{3,0},{4,5},{5,6},{6,7},{7,4},{8,9},{9,10},{10,1... | collective-permute-start | bytes 393224 | tf_op jit(solution)/shard_map/ppermute | solution.py:337
  96.5 8.9 %collective-permute-start.18 = (bf16[256,256]{1,0:T(8,128)(2,1)S(1)}, bf16[256,256]{1,0:T(8,128)(2,1)S(1)}, u32[]{:S(2)}, u32[]{:S(2)}) collective-permute-start(bf16[256,256]{1,0:T(8,128)(2,1)S(1)} %get-tuple-element.59), channel_id=1, source_target_pairs={{0,2},{1,3},{2,0},{3,1},{4,6},{5,7},{6,4},{7,5},{8,10},{9,11},{10,... | collective-permute-start | bytes 393224 | tf_op jit(solution)/shard_map/ppermute | solution.py:337
  109.0 17.6 %all-to-all-start.3 = ((bf16[16,96,256]{2,1,0:T(8,128)(2,1)}), bf16[16,96,256]{2,1,0:T(8,128)(2,1)S(1)}, u32[]{:S(2)}, u32[]{:S(2)}) async-start(bf16[16,96,256]{2,1,0:T(8,128)(2,1)} %bitcast.5), calls=%async_computation.3 | async-start | bytes 1572864 | tf_op jit(solution)/shard_map/all_to_all | solution.py:386
  113.8 14.8 %collective-permute-start.12 = (bf16[8,96,256]{2,1,0:T(8,128)(2,1)S(1)}, bf16[8,96,256]{2,1,0:T(8,128)(2,1)S(1)}, u32[]{:S(2)}, u32[]{:S(2)}) collective-permute-start(bf16[8,96,256]{2,1,0:T(8,128)(2,1)S(1)} %get-tuple-element.66.refs_0_), channel_id=1, source_target_pairs={{0,1},{1,2},{2,3},{3,0},{4,5},{5,6},{6,7},{7,4},{8,9},{9,10},{10,1... | collective-permute-start | bytes 1179656 | tf_op jit(solution)/shard_map/ppermute | solution.py:337
  115.0 14.9 %collective-permute-start.13 = (bf16[8,96,256]{2,1,0:T(8,128)(2,1)S(1)}, bf16[8,96,256]{2,1,0:T(8,128)(2,1)S(1)}, u32[]{:S(2)}, u32[]{:S(2)}) collective-permute-start(bf16[8,96,256]{2,1,0:T(8,128)(2,1)S(1)} %get-tuple-element.65.refs_1_), channel_id=1, source_target_pairs={{0,3},{1,0},{2,1},{3,2},{4,7},{5,4},{6,5},{7,6},{8,11},{9,8},{10,9... | collective-permute-start | bytes 1179656 | tf_op jit(solution)/shard_map/ppermute | solution.py:337
  117.1 18.4 %collective-permute-start.26 = (bf16[8,96,256]{2,1,0:T(8,128)(2,1)S(1)}, bf16[8,96,256]{2,1,0:T(8,128)(2,1)S(1)}, u32[]{:S(2)}, u32[]{:S(2)}) collective-permute-start(bf16[8,96,256]{2,1,0:T(8,128)(2,1)S(1)} %get-tuple-element.66.refs_0_), channel_id=1, source_target_pairs={{0,3},{1,0},{2,1},{3,2},{4,7},{5,4},{6,5},{7,6},{8,11},{9,8},{10,9... | collective-permute-start | bytes 1179656 | tf_op jit(solution)/shard_map/ppermute | solution.py:337
  118.3 27.9 %collective-permute-start.28 = (bf16[8,96,256]{2,1,0:T(8,128)(2,1)S(1)}, bf16[8,96,256]{2,1,0:T(8,128)(2,1)S(1)}, u32[]{:S(2)}, u32[]{:S(2)}) collective-permute-start(bf16[8,96,256]{2,1,0:T(8,128)(2,1)S(1)} %get-tuple-element.65.refs_1_), channel_id=1, source_target_pairs={{0,1},{1,2},{2,3},{3,0},{4,5},{5,6},{6,7},{7,4},{8,9},{9,10},{10,1... | collective-permute-start | bytes 1179656 | tf_op jit(solution)/shard_map/ppermute | solution.py:337
  126.6 21.8 %collective-permute-start.22 = (bf16[8,96,256]{2,1,0:T(8,128)(2,1)S(1)}, bf16[8,96,256]{2,1,0:T(8,128)(2,1)S(1)}, u32[]{:S(2)}, u32[]{:S(2)}) collective-permute-start(bf16[8,96,256]{2,1,0:T(8,128)(2,1)S(1)} %get-tuple-element.64.refs_2_), channel_id=1, source_target_pairs={{0,1},{1,2},{2,3},{3,0},{4,5},{5,6},{6,7},{7,4},{8,9},{9,10},{10,1... | collective-permute-start | bytes 1179656 | tf_op jit(solution)/shard_map/ppermute | solution.py:337
  128.6 21.1 %collective-permute-start.24 = (bf16[8,96,256]{2,1,0:T(8,128)(2,1)S(1)}, bf16[8,96,256]{2,1,0:T(8,128)(2,1)S(1)}, u32[]{:S(2)}, u32[]{:S(2)}) collective-permute-start(bf16[8,96,256]{2,1,0:T(8,128)(2,1)S(1)} %get-tuple-element.63.refs_3_), channel_id=1, source_target_pairs={{0,3},{1,0},{2,1},{3,2},{4,7},{5,4},{6,5},{7,6},{8,11},{9,8},{10,9... | collective-permute-start | bytes 1179656 | tf_op jit(solution)/shard_map/ppermute | solution.py:337
  129.9 22.4 %collective-permute-start.27 = (bf16[8,96,256]{2,1,0:T(8,128)(2,1)S(1)}, bf16[8,96,256]{2,1,0:T(8,128)(2,1)S(1)}, u32[]{:S(2)}, u32[]{:S(2)}) collective-permute-start(bf16[8,96,256]{2,1,0:T(8,128)(2,1)S(1)} %get-tuple-element.64.refs_2_), channel_id=1, source_target_pairs={{0,3},{1,0},{2,1},{3,2},{4,7},{5,4},{6,5},{7,6},{8,11},{9,8},{10,9... | collective-permute-start | bytes 1179656 | tf_op jit(solution)/shard_map/ppermute | solution.py:337
  135.5 20.1 %collective-permute-start.29 = (bf16[8,96,256]{2,1,0:T(8,128)(2,1)S(1)}, bf16[8,96,256]{2,1,0:T(8,128)(2,1)S(1)}, u32[]{:S(2)}, u32[]{:S(2)}) collective-permute-start(bf16[8,96,256]{2,1,0:T(8,128)(2,1)S(1)} %get-tuple-element.63.refs_3_), channel_id=1, source_target_pairs={{0,1},{1,2},{2,3},{3,0},{4,5},{5,6},{6,7},{7,4},{8,9},{9,10},{10,1... | collective-permute-start | bytes 1179656 | tf_op jit(solution)/shard_map/ppermute | solution.py:337
  146.2 20.0 %collective-permute-start.20 = (bf16[8,96,256]{2,1,0:T(8,128)(2,1)S(1)}, bf16[8,96,256]{2,1,0:T(8,128)(2,1)S(1)}, u32[]{:S(2)}, u32[]{:S(2)}) collective-permute-start(bf16[8,96,256]{2,1,0:T(8,128)(2,1)S(1)} %collective-permute-done.12.refs_4_), channel_id=1, source_target_pairs={{0,1},{1,2},{2,3},{3,0},{4,5},{5,6},{6,7},{7,4},{8,9},{9,10},{10,1... | collective-permute-start | bytes 1179656 | tf_op jit(solution)/shard_map/ppermute | solution.py:337
  148.4 17.8 %collective-permute-start.21 = (bf16[8,96,256]{2,1,0:T(8,128)(2,1)S(1)}, bf16[8,96,256]{2,1,0:T(8,128)(2,1)S(1)}, u32[]{:S(2)}, u32[]{:S(2)}) collective-permute-start(bf16[8,96,256]{2,1,0:T(8,128)(2,1)S(1)} %collective-permute-done.13.refs_1_), channel_id=1, source_target_pairs={{0,3},{1,0},{2,1},{3,2},{4,7},{5,4},{6,5},{7,6},{8,11},{9,8},{10,9... | collective-permute-start | bytes 1179656 | tf_op jit(solution)/shard_map/ppermute | solution.py:337
  149.7 16.6 %collective-permute-start.23 = (bf16[8,96,256]{2,1,0:T(8,128)(2,1)S(1)}, bf16[8,96,256]{2,1,0:T(8,128)(2,1)S(1)}, u32[]{:S(2)}, u32[]{:S(2)}) collective-permute-start(bf16[8,96,256]{2,1,0:T(8,128)(2,1)S(1)} %collective-permute-done.22.refs_6_), channel_id=1, source_target_pairs={{0,1},{1,2},{2,3},{3,0},{4,5},{5,6},{6,7},{7,4},{8,9},{9,10},{10,1... | collective-permute-start | bytes 1179656 | tf_op jit(solution)/shard_map/ppermute | solution.py:337
  152.4 14.3 %collective-permute-start.25 = (bf16[8,96,256]{2,1,0:T(8,128)(2,1)S(1)}, bf16[8,96,256]{2,1,0:T(8,128)(2,1)S(1)}, u32[]{:S(2)}, u32[]{:S(2)}) collective-permute-start(bf16[8,96,256]{2,1,0:T(8,128)(2,1)S(1)} %collective-permute-done.24.refs_3_), channel_id=1, source_target_pairs={{0,3},{1,0},{2,1},{3,2},{4,7},{5,4},{6,5},{7,6},{8,11},{9,8},{10,9... | collective-permute-start | bytes 1179656 | tf_op jit(solution)/shard_map/ppermute | solution.py:337
  (9 other events, 51.9 us)

commit v7 on v6

--- a/solution.py
+++ b/solution.py
@@ -418,8 +418,8 @@
     own_b, below_b, above_b = to_neighbours(exchange(density_of(rows_b, amplitude_b)))
     put = functools.partial(add_columns, vir_coeff, blocks, owner, shell)
     result = put((0,), [[*own_a, *own_b]])
-    first, second, result = tie((below_a[0], above_a[1], result))
-    far_a = [shift(first, 1), shift(second, -1)]
+    second, result = tie((above_a[1], result))
+    far_a = [shift(below_a[0], 1), shift(second, -1)]
     far_b = [shift(below_b[0], 1), shift(above_b[1], -1)]
     result = put((1, 3), [[*above_a, *above_b], [*below_a, *below_b]], result)
     return put((2,), [[*far_a, *far_b]], result, last=True)

time: 175 us -> 177 us (1.011)
  transfers between devices with their start and end apart: 34 -> 34, of which waited for: 20 -> 19; matrix products, arithmetic and copies ran while one was open for 5% -> 5% of each run, Pallas kernels for 13% -> 13%
where the time goes in v7:
time: 177 us
  starting transfers between devices  68 us (38%)
  waiting for transfers between devices  55.4 us (31%)
  Pallas kernels  38.1 us (22%)
  local copies, waits for them, and re-layouts  6.38 us (4%)
  other arithmetic  4.83 us (3%)
  matrix products  3.48 us (2%)
    ppermute x28, starting transfers between devices, shift(): return lax.ppermute(value, 'grp', [(j, (j + by) % GRP) for j in range(GRP)])  44.3 us
    ppermute x28, waiting for transfers between devices, shift(): return lax.ppermute(value, 'grp', [(j, (j + by) % GRP) for j in range(GRP)])  35.2 us
    pallas_call x3, Pallas kernels, add_columns(): pl.pallas_call(functools.partial(columns_kernel, quarter_shells=nus // sh...  24.8 us
    all_to_all x4, starting transfers between devices, exchange(): lax.all_to_all(value, 'aux', split_axis=0, concat_axis=0, axis_index_grou...  23.6 us
    all_to_all x4, waiting for transfers between devices, exchange(): lax.all_to_all(value, 'aux', split_axis=0, concat_axis=0, axis_index_grou...  19 us
    pallas_call x1, Pallas kernels, partial_pieces(): pl.pallas_call(functools.partial(far_kernel, groups=groups, quarter_shell...  6.94 us
    pallas_call x1, Pallas kernels, partial_pieces(): pl.pallas_call(functools.partial(near_kernel, slots=slots, groups=groups)...  6.35 us
    unnamed x15, local copies, waits for them, and re-layouts  5.68 us
  transfers between devices with their start and end apart: 34, of which 19 were waited for; matrix products, arithmetic and copies ran while one was open for 5% of the time, Pallas kernels for 13%

profile of v7, /device:TPU:0, one launch (start us, length us, event | category | flops | bytes accessed | tf_op | source)
XLA Modules:
  0.0 176.8 jit_solution(4205625369910433920)
XLA Ops:
  2.1 6.9 %far_rows.1 = (bf16[288,512]{1,0:T(8,128)(2,1)S(1)}, bf16[8,96,256]{2,1,0:T(8,128)(2,1)S(1)}, bf16[8,96,256]{2,1,0:T(8,128)(2,1)S(1)}, bf16[8,96,256]{2,1,0:T(8,128)(2,1)S(1)}, bf16[8,96,256]{2,1,0:T(8,128)(2,1)S(1)}) custom-call(s32[8,4]{1,0:T(8,128)S(1)} %copy.23.blocks, s32[128]{0:T(128)S(1)} %copy-done.2, bf16[2,4352]{1,0:T(2,128)(2,1)S(1)} %copy-done.4, ...), custom_call_target="tpu_custom_call" | custom-call | flops 1073741824 | bytes 10485760 | tf_op jit(solution)/shard_map/far_rows/pallas_call | solution.py:182
  14.4 6.4 %near_rows.1 = (bf16[16,96,256]{2,1,0:T(8,128)(2,1)S(1)}, bf16[8,96,256]{2,1,0:T(8,128)(2,1)S(1)}, bf16[8,96,256]{2,1,0:T(8,128)(2,1)S(1)}, bf16[8,96,256]{2,1,0...) custom-call(s32[8,4]{1,0:T(8,128)S(1)} %copy.23.blocks, ...), custom_call_target="tpu_custom_call" | custom-call | flops 2147483648 | bytes 8388608 | tf_op jit(solution)/shard_map/near_rows/pallas_call | solution.py:203
  24.3 1.7 collective-permute-start.6
  28.0 3.2 %collective-permute-done.4 = bf16[8,96,256]{2,1,0:T(8,128)(2,1)S(1)} collective-permute-done((bf16[8,96,256]{2,1,0:T(8,128)(2,1)S(1)}, bf16[8,96,256]{2,1,0:T(8,128)(2,1)S(1)}, u32[]{:S(2)}, u32[]{:S(2)}) %collective-permute-start.4) | collective-permute-done | bytes 393248 | tf_op jit(solution)/shard_map/ppermute | solution.py:337
  33.1 6.2 %collective-permute-done.5 = bf16[8,96,256]{2,1,0:T(8,128)(2,1)S(1)} collective-permute-done((bf16[8,96,256]{2,1,0:T(8,128)(2,1)S(1)}, bf16[8,96,256]{2,1,0:T(8,128)(2,1)S(1)}, u32[]{:S(2)}, u32[]{:S(2)}) %collective-permute-start.5) | collective-permute-done | bytes 393248 | tf_op jit(solution)/shard_map/ppermute | solution.py:337
  41.1 1.7 collective-permute-start.16
  42.9 5.2 %collective-permute-done.7 = bf16[8,96,256]{2,1,0:T(8,128)(2,1)S(1)} collective-permute-done((bf16[8,96,256]{2,1,0:T(8,128)(2,1)S(1)}, bf16[8,96,256]{2,1,0:T(8,128)(2,1)S(1)}, u32[]{:S(2)}, u32[]{:S(2)}) %collective-permute-start.7) | collective-permute-done | bytes 393248 | tf_op jit(solution)/shard_map/ppermute | solution.py:337
  49.4 8.1 %all-to-all-start = ((bf16[16,96,256]{2,1,0:T(8,128)(2,1)}), bf16[16,96,256]{2,1,0:T(8,128)(2,1)S(1)}, u32[]{:S(2)}, u32[]{:S(2)}) async-start(bf16[16,96,256]{2,1,0:T(8,128)(2,1)} %pad_maximum_fusion.2), calls=%async_computation | async-start | bytes 1572864 | tf_op jit(solution)/shard_map/all_to_all | solution.py:386
  58.0 5.4 %collective-permute-done.15 = bf16[16,96,256]{2,1,0:T(8,128)(2,1)} collective-permute-done((bf16[16,96,256]{2,1,0:T(8,128)(2,1)S(1)}, bf16[16,96,256]{2,1,0:T(8,128)(2,1)}, u32[]{:S(2)}, u32[]{:S(2)}) %collective-permute-start.15) | collective-permute-done | bytes 786464 | tf_op jit(solution)/shard_map/ppermute | solution.py:337
  63.5 2.6 %add_convert_fusion = bf16[16,96,256]{2,1,0:T(8,128)(2,1)} fusion(bf16[16,96,256]{2,1,0:T(8,128)(2,1)} %collective-permute-done.16, bf16[16,96,256]{2,1,0:T(8,128)(2,1)} %collective-permute-done.15, bf16[16,96,256]{2,1,0:T(8,128)(2,1)S(1)} %get-tuple-element.50), kind=kLoop, calls=%fused_computation.2 | loop fusion | flops 2359296 | bytes 3145728 | tf_op jit(solution)/shard_map/convert_element_type | solution.py:341
  66.2 3.3 %all-to-all-done = bf16[16,96,256]{2,1,0:T(8,128)(2,1)S(1)} async-done(((bf16[16,96,256]{2,1,0:T(8,128)(2,1)}), bf16[16,96,256]{2,1,0:T(8,128)(2,1)S(1)}, u32[]{:S(2)}, u32[]{:S(2)}) %all-to-all-start) | async-done | bytes 786464 | tf_op jit(solution)/shard_map/all_to_all | solution.py:386
  69.4 4.9 %all-to-all-start.2 = ((bf16[16,96,256]{2,1,0:T(8,128)(2,1)}), bf16[16,96,256]{2,1,0:T(8,128)(2,1)S(1)}, u32[]{:S(2)}, u32[]{:S(2)}) async-start(bf16[16,96,256]{2,1,0:T(8,128)(2,1)} %add_convert_fusion), calls=%async_computation.2 | async-start | bytes 1572864 | tf_op jit(solution)/shard_map/all_to_all | solution.py:386
  76.4 2.8 %collective-permute-start.10 = (bf16[256,256]{1,0:T(8,128)(2,1)S(1)}, bf16[256,256]{1,0:T(8,128)(2,1)S(1)}, u32[]{:S(2)}, u32[]{:S(2)}) collective-permute-start(bf16[256,256]{1,0:T(8,128)(2,1)S(1)} %get-tuple-element.59), channel_id=1, source_target_pairs={{0,2},{1,3},{2,0},{3,1},{4,6},{5,7},{6,4},{7,5},{8,10},{9,11},{10,... | collective-permute-start | bytes 393224 | tf_op jit(solution)/shard_map/ppermute | solution.py:337
  81.3 6.5 %all-to-all-done.2 = bf16[16,96,256]{2,1,0:T(8,128)(2,1)S(1)} async-done(((bf16[16,96,256]{2,1,0:T(8,128)(2,1)}), bf16[16,96,256]{2,1,0:T(8,128)(2,1)S(1)}, u32[]{:S(2)}, u32[]{:S(2)}) %all-to-all-start.2) | async-done | bytes 786464 | tf_op jit(solution)/shard_map/all_to_all | solution.py:386
  89.7 5.9 %all-to-all-start.1 = ((bf16[16,96,256]{2,1,0:T(8,128)(2,1)}), bf16[16,96,256]{2,1,0:T(8,128)(2,1)S(1)}, u32[]{:S(2)}, u32[]{:S(2)}) async-start(bf16[16,96,256]{2,1,0:T(8,128)(2,1)} %bitcast.2), calls=%async_computation.1 | async-start | bytes 1572864 | tf_op jit(solution)/shard_map/all_to_all | solution.py:386
  96.5 2.9 %collective-permute-start.19 = (bf16[256,256]{1,0:T(8,128)(2,1)S(1)}, bf16[256,256]{1,0:T(8,128)(2,1)S(1)}, u32[]{:S(2)}, u32[]{:S(2)}) collective-permute-start(bf16[256,256]{1,0:T(8,128)(2,1)S(1)} %get-tuple-element.57), channel_id=1, source_target_pairs={{0,2},{1,3},{2,0},{3,1},{4,6},{5,7},{6,4},{7,5},{8,10},{9,11},{10,... | collective-permute-start | bytes 393224 | tf_op jit(solution)/shard_map/ppermute | solution.py:337
  100.5 1.9 %collective-permute-done.18 = bf16[256,256]{1,0:T(8,128)(2,1)S(1)} collective-permute-done((bf16[256,256]{1,0:T(8,128)(2,1)S(1)}, bf16[256,256]{1,0:T(8,128)(2,1)S(1)}, u32[]{:S(2)}, u32[]{:S(2)}) %collective-permute-start.18) | collective-permute-done | bytes 131104 | tf_op jit(solution)/shard_map/ppermute | solution.py:337
  102.3 3.0 %collective-permute-done.19 = bf16[256,256]{1,0:T(8,128)(2,1)S(1)} collective-permute-done((bf16[256,256]{1,0:T(8,128)(2,1)S(1)}, bf16[256,256]{1,0:T(8,128)(2,1)S(1)}, u32[]{:S(2)}, u32[]{:S(2)}) %collective-permute-start.19) | collective-permute-done | bytes 131104 | tf_op jit(solution)/shard_map/ppermute | solution.py:337
  106.8 2.2 %all-to-all-done.1 = bf16[16,96,256]{2,1,0:T(8,128)(2,1)S(1)} async-done(((bf16[16,96,256]{2,1,0:T(8,128)(2,1)}), bf16[16,96,256]{2,1,0:T(8,128)(2,1)S(1)}, u32[]{:S(2)}, u32[]{:S(2)}) %all-to-all-start.1) | async-done | bytes 786464 | tf_op jit(solution)/shard_map/all_to_all | solution.py:386
  109.0 4.8 %all-to-all-start.3 = ((bf16[16,96,256]{2,1,0:T(8,128)(2,1)}), bf16[16,96,256]{2,1,0:T(8,128)(2,1)S(1)}, u32[]{:S(2)}, u32[]{:S(2)}) async-start(bf16[16,96,256]{2,1,0:T(8,128)(2,1)} %bitcast.5), calls=%async_computation.3 | async-start | bytes 1572864 | tf_op jit(solution)/shard_map/all_to_all | solution.py:386
  113.8 2.5 %collective-permute-start.14 = (bf16[8,96,256]{2,1,0:T(8,128)(2,1)S(1)}, bf16[8,96,256]{2,1,0:T(8,128)(2,1)S(1)}, u32[]{:S(2)}, u32[]{:S(2)}) collective-permute-start(bf16[8,96,256]{2,1,0:T(8,128)(2,1)S(1)} %get-tuple-element.63.refs_1_), channel_id=1, source_target_pairs={{0,3},{1,0},{2,1},{3,2},{4,7},{5,4},{6,5},{7,6},{8,11},{9,8},{10,9... | collective-permute-start | bytes 1179656 | tf_op jit(solution)/shard_map/ppermute | solution.py:337
  116.3 3.2 %collective-permute-start.26 = (bf16[8,96,256]{2,1,0:T(8,128)(2,1)S(1)}, bf16[8,96,256]{2,1,0:T(8,128)(2,1)S(1)}, u32[]{:S(2)}, u32[]{:S(2)}) collective-permute-start(bf16[8,96,256]{2,1,0:T(8,128)(2,1)S(1)} %get-tuple-element.64.refs_0_), channel_id=1, source_target_pairs={{0,3},{1,0},{2,1},{3,2},{4,7},{5,4},{6,5},{7,6},{8,11},{9,8},{10,9... | collective-permute-start | bytes 1179656 | tf_op jit(solution)/shard_map/ppermute | solution.py:337
  119.5 7.1 %all-to-all-done.3 = bf16[16,96,256]{2,1,0:T(8,128)(2,1)S(1)} async-done(((bf16[16,96,256]{2,1,0:T(8,128)(2,1)}), bf16[16,96,256]{2,1,0:T(8,128)(2,1)S(1)}, u32[]{:S(2)}, u32[]{:S(2)}) %all-to-all-start.3) | async-done | bytes 786464 | tf_op jit(solution)/shard_map/all_to_all | solution.py:386
  126.6 2.0 %collective-permute-start.22 = (bf16[8,96,256]{2,1,0:T(8,128)(2,1)S(1)}, bf16[8,96,256]{2,1,0:T(8,128)(2,1)S(1)}, u32[]{:S(2)}, u32[]{:S(2)}) collective-permute-start(bf16[8,96,256]{2,1,0:T(8,128)(2,1)S(1)} %get-tuple-element.62.refs_2_), channel_id=1, source_target_pairs={{0,1},{1,2},{2,3},{3,0},{4,5},{5,6},{6,7},{7,4},{8,9},{9,10},{10,1... | collective-permute-start | bytes 1179656 | tf_op jit(solution)/shard_map/ppermute | solution.py:337
  131.4 3.0 %collective-permute-done.26.refs_0_ = bf16[8,96,256]{2,1,0:T(8,128)(2,1)S(1)} collective-permute-done((bf16[8,96,256]{2,1,0:T(8,128)(2,1)S(1)}, bf16[8,96,256]{2,1,0:T(8,128)(2,1)S(1)}, u32[]{:S(2)}, u32[]{:S(2)}) %collective-permute-start.26) | collective-permute-done | bytes 393248 | tf_op jit(solution)/shard_map/ppermute | solution.py:337
  135.5 3.5 %copy-done.1 = bf16[1088,4096]{1,0:T(8,128)(2,1)S(1)} copy-done((bf16[1088,4096]{1,0:T(8,128)(2,1)S(1)}, bf16[1088,4096]{1,0:T(8,128)(2,1)}, u32[]{:S(2)}) %copy-start.1) | copy-done | bytes 8912920
  139.0 6.4 %add_columns.3.refs_8_ = bf16[2,1088,384]{2,1,0:T(8,128)(2,1)S(1)} custom-call(s32[8,4]{1,0:T(8,128)S(1)} %copy.23.blocks, s32[128]{0:T(128)S(1)} %copy-done.3, bf16[1088,4096]{1,0:T(8,128)(2,1)S(1)} %copy-done.1, bf16[8,96,256]{2,1,0:T(8,128)(2,1)S(1)} %get-tuple-element.64.refs_0_, bf16[8,96,256]{2,1,0:T(8,128)(2,1)S(1)} %get-tuple-element.63.refs_1_, ...), custom_call_target="tpu_custom_call" | custom-call | flops 1711276032 | bytes 12582912 | tf_op jit(solution)/shard_map/add_columns/pallas_call | solution.py:309
  146.5 2.5 %collective-permute-start.21 = (bf16[8,96,256]{2,1,0:T(8,128)(2,1)S(1)}, bf16[8,96,256]{2,1,0:T(8,128)(2,1)S(1)}, u32[]{:S(2)}, u32[]{:S(2)}) collective-permute-start(bf16[8,96,256]{2,1,0:T(8,128)(2,1)S(1)} %collective-permute-done.14.refs_1_), channel_id=1, source_target_pairs={{0,3},{1,0},{2,1},{3,2},{4,7},{5,4},{6,5},{7,6},{8,11},{9,8},{10,9... | collective-permute-start | bytes 1179656 | tf_op jit(solution)/shard_map/ppermute | solution.py:337
  151.2 3.6 %collective-permute-start.25 = (bf16[8,96,256]{2,1,0:T(8,128)(2,1)S(1)}, bf16[8,96,256]{2,1,0:T(8,128)(2,1)S(1)}, u32[]{:S(2)}, u32[]{:S(2)}) collective-permute-start(bf16[8,96,256]{2,1,0:T(8,128)(2,1)S(1)} %collective-permute-done.24.refs_3_), channel_id=1, source_target_pairs={{0,3},{1,0},{2,1},{3,2},{4,7},{5,4},{6,5},{7,6},{8,11},{9,8},{10,9... | collective-permute-start | bytes 1179656 | tf_op jit(solution)/shard_map/ppermute | solution.py:337
  154.8 10.5 %add_columns.4.refs_4_ = bf16[2,1088,384]{2,1,0:T(8,128)(2,1)S(1)} custom-call(s32[8,4]{1,0:T(8,128)S(1)} %copy.23.blocks, s32[128]{0:T(128)S(1)} %copy-done.3, bf16[1088,4096]{1,0:T(8,128)(2,1)S(1)} %copy-done.1, bf16[8,96,256]{2,1,0:T(8,128)(2,1)S(1)} %collective-permute-done.26.refs_0_, bf16[8,96,256]{2,1,0:T(8,128)(2,1)S(1)} %collective-permute-done.14.refs_1_, ...), custom_call_target="tpu_custom_call" | custom-call | flops 3422552064 | bytes 12582912 | tf_op jit(solution)/shard_map/add_columns/pallas_call | solution.py:309
  165.4 3.3 %collective-permute-done.23.refs_2_ = bf16[8,96,256]{2,1,0:T(8,128)(2,1)S(1)} collective-permute-done((bf16[8,96,256]{2,1,0:T(8,128)(2,1)S(1)}, bf16[8,96,256]{2,1,0:T(8,128)(2,1)S(1)}, u32[]{:S(2)}, u32[]{:S(2)}) %collective-permute-start.23) | collective-permute-done | bytes 393248 | tf_op jit(solution)/shard_map/ppermute | solution.py:337
  168.7 7.9 %add_columns.5 = bf16[2,1088,384]{2,1,0:T(8,128)(2,1)} custom-call(s32[8,4]{1,0:T(8,128)S(1)} %copy.23.blocks, s32[128]{0:T(128)S(1)} %copy-done.3, bf16[1088,4096]{1,0:T(8,128)(2,1)S(1)} %copy-done.1, bf16[8,96,256]{2,1,0:T(8,128)(2,1)S(1)} %collective-permute-done.13.refs_0_, bf16[8,96,256]{2,1,0:T(8,128)(2,1)S(1)} %collective-permute-done.21.refs_1_, ...), custom_call_target="tpu_custom_call" | custom-call | flops 1711276032 | bytes 12582912 | tf_op jit(solution)/shard_map/add_columns/pallas_call | solution.py:309
  (85 shorter events, 35.3 us)
Async XLA Ops:
  9.1 13.3 %collective-permute-start = (bf16[8,96,256]{2,1,0:T(8,128)(2,1)S(1)}, bf16[8,96,256]{2,1,0:T(8,128)(2,1)S(1)}, u32[]{:S(2)}, u32[]{:S(2)}) collective-permute-start(bf16[8,96,256]{2,1,0:T(8,128)(2,1)S(1)} %get-tuple-element.35), channel_id=1, source_target_pairs={{0,1},{1,2},{2,3},{3,0},{4,5},{5,6},{6,7},{7,4},{8,9},{9,10},{10,1... | collective-permute-start | bytes 1179656 | tf_op jit(solution)/shard_map/ppermute | solution.py:337
  10.7 12.0 %collective-permute-start.1 = (bf16[8,96,256]{2,1,0:T(8,128)(2,1)S(1)}, bf16[8,96,256]{2,1,0:T(8,128)(2,1)S(1)}, u32[]{:S(2)}, u32[]{:S(2)}) collective-permute-start(bf16[8,96,256]{2,1,0:T(8,128)(2,1)S(1)} %get-tuple-element.36), channel_id=1, source_target_pairs={{0,3},{1,0},{2,1},{3,2},{4,7},{5,4},{6,5},{7,6},{8,11},{9,8},{10,9... | collective-permute-start | bytes 1179656 | tf_op jit(solution)/shard_map/ppermute | solution.py:337
  12.4 18.8 %collective-permute-start.4 = (bf16[8,96,256]{2,1,0:T(8,128)(2,1)S(1)}, bf16[8,96,256]{2,1,0:T(8,128)(2,1)S(1)}, u32[]{:S(2)}, u32[]{:S(2)}) collective-permute-start(bf16[8,96,256]{2,1,0:T(8,128)(2,1)S(1)} %get-tuple-element.43), channel_id=1, source_target_pairs={{0,3},{1,0},{2,1},{3,2},{4,7},{5,4},{6,5},{7,6},{8,11},{9,8},{10,9... | collective-permute-start | bytes 1179656 | tf_op jit(solution)/shard_map/ppermute | solution.py:337
  14.0 18.9 %collective-permute-start.3 = (bf16[8,96,256]{2,1,0:T(8,128)(2,1)S(1)}, bf16[8,96,256]{2,1,0:T(8,128)(2,1)S(1)}, u32[]{:S(2)}, u32[]{:S(2)}) collective-permute-start(bf16[8,96,256]{2,1,0:T(8,128)(2,1)S(1)} %get-tuple-element.39), channel_id=1, source_target_pairs={{0,1},{1,2},{2,3},{3,0},{4,5},{5,6},{6,7},{7,4},{8,9},{9,10},{10,1... | collective-permute-start | bytes 1179656 | tf_op jit(solution)/shard_map/ppermute | solution.py:337
  22.8 16.5 %collective-permute-start.5 = (bf16[8,96,256]{2,1,0:T(8,128)(2,1)S(1)}, bf16[8,96,256]{2,1,0:T(8,128)(2,1)S(1)}, u32[]{:S(2)}, u32[]{:S(2)}) collective-permute-start(bf16[8,96,256]{2,1,0:T(8,128)(2,1)S(1)} %get-tuple-element.44), channel_id=1, source_target_pairs={{0,1},{1,2},{2,3},{3,0},{4,5},{5,6},{6,7},{7,4},{8,9},{9,10},{10,1... | collective-permute-start | bytes 1179656 | tf_op jit(solution)/shard_map/ppermute | solution.py:337
  24.3 15.4 %collective-permute-start.6 = (bf16[8,96,256]{2,1,0:T(8,128)(2,1)S(1)}, bf16[8,96,256]{2,1,0:T(8,128)(2,1)S(1)}, u32[]{:S(2)}, u32[]{:S(2)}) collective-permute-start(bf16[8,96,256]{2,1,0:T(8,128)(2,1)S(1)} %get-tuple-element.45), channel_id=1, source_target_pairs={{0,3},{1,0},{2,1},{3,2},{4,7},{5,4},{6,5},{7,6},{8,11},{9,8},{10,9... | collective-permute-start | bytes 1179656 | tf_op jit(solution)/shard_map/ppermute | solution.py:337
  26.1 21.9 %collective-permute-start.7 = (bf16[8,96,256]{2,1,0:T(8,128)(2,1)S(1)}, bf16[8,96,256]{2,1,0:T(8,128)(2,1)S(1)}, u32[]{:S(2)}, u32[]{:S(2)}) collective-permute-start(bf16[8,96,256]{2,1,0:T(8,128)(2,1)S(1)} %add_convert_fusion.2), channel_id=1, source_target_pairs={{0,3},{1,0},{2,1},{3,2},{4,7},{5,4},{6,5},{7,6},{8,11},{9,8},{10,9... | collective-permute-start | bytes 1179656 | tf_op jit(solution)/shard_map/ppermute | solution.py:337
  31.2 16.9 %collective-permute-start.2 = (bf16[8,96,256]{2,1,0:T(8,128)(2,1)S(1)}, bf16[8,96,256]{2,1,0:T(8,128)(2,1)S(1)}, u32[]{:S(2)}, u32[]{:S(2)}) collective-permute-start(bf16[8,96,256]{2,1,0:T(8,128)(2,1)S(1)} %add_convert_fusion.6), channel_id=1, source_target_pairs={{0,1},{1,2},{2,3},{3,0},{4,5},{5,6},{6,7},{7,4},{8,9},{9,10},{10,1... | collective-permute-start | bytes 1179656 | tf_op jit(solution)/shard_map/ppermute | solution.py:337
  39.6 23.7 %collective-permute-start.15 = (bf16[16,96,256]{2,1,0:T(8,128)(2,1)S(1)}, bf16[16,96,256]{2,1,0:T(8,128)(2,1)}, u32[]{:S(2)}, u32[]{:S(2)}) collective-permute-start(bf16[16,96,256]{2,1,0:T(8,128)(2,1)S(1)} %pad_maximum_fusion), channel_id=1, source_target_pairs={{0,1},{1,2},{2,3},{3,0},{4,5},{5,6},{6,7},{7,4},{8,9},{9,10},{10,1... | collective-permute-start | bytes 2359304 | tf_op jit(solution)/shard_map/ppermute | solution.py:337
  41.1 22.4 %collective-permute-start.16 = (bf16[16,96,256]{2,1,0:T(8,128)(2,1)S(1)}, bf16[16,96,256]{2,1,0:T(8,128)(2,1)}, u32[]{:S(2)}, u32[]{:S(2)}) collective-permute-start(bf16[16,96,256]{2,1,0:T(8,128)(2,1)S(1)} %pad_maximum_fusion.1), channel_id=1, source_target_pairs={{0,3},{1,0},{2,1},{3,2},{4,7},{5,4},{6,5},{7,6},{8,11},{9,8},{10,9... | collective-permute-start | bytes 2359304 | tf_op jit(solution)/shard_map/ppermute | solution.py:337
  49.4 20.0 %all-to-all-start = ((bf16[16,96,256]{2,1,0:T(8,128)(2,1)}), bf16[16,96,256]{2,1,0:T(8,128)(2,1)S(1)}, u32[]{:S(2)}, u32[]{:S(2)}) async-start(bf16[16,96,256]{2,1,0:T(8,128)(2,1)} %pad_maximum_fusion.2), calls=%async_computation | async-start | bytes 1572864 | tf_op jit(solution)/shard_map/all_to_all | solution.py:386
  69.4 18.4 %all-to-all-start.2 = ((bf16[16,96,256]{2,1,0:T(8,128)(2,1)}), bf16[16,96,256]{2,1,0:T(8,128)(2,1)S(1)}, u32[]{:S(2)}, u32[]{:S(2)}) async-start(bf16[16,96,256]{2,1,0:T(8,128)(2,1)} %add_convert_fusion), calls=%async_computation.2 | async-start | bytes 1572864 | tf_op jit(solution)/shard_map/all_to_all | solution.py:386
  76.4 11.9 %collective-permute-start.10 = (bf16[256,256]{1,0:T(8,128)(2,1)S(1)}, bf16[256,256]{1,0:T(8,128)(2,1)S(1)}, u32[]{:S(2)}, u32[]{:S(2)}) collective-permute-start(bf16[256,256]{1,0:T(8,128)(2,1)S(1)} %get-tuple-element.59), channel_id=1, source_target_pairs={{0,2},{1,3},{2,0},{3,1},{4,6},{5,7},{6,4},{7,5},{8,10},{9,11},{10,... | collective-permute-start | bytes 393224 | tf_op jit(solution)/shard_map/ppermute | solution.py:337
  79.2 9.1 %collective-permute-start.11 = (bf16[256,256]{1,0:T(8,128)(2,1)S(1)}, bf16[256,256]{1,0:T(8,128)(2,1)S(1)}, u32[]{:S(2)}, u32[]{:S(2)}) collective-permute-start(bf16[256,256]{1,0:T(8,128)(2,1)S(1)} %get-tuple-element.59), channel_id=1, source_target_pairs={{0,3},{1,0},{2,1},{3,2},{4,7},{5,4},{6,5},{7,6},{8,11},{9,8},{10,9... | collective-permute-start | bytes 393224 | tf_op jit(solution)/shard_map/ppermute | solution.py:337
  80.7 7.6 %collective-permute-start.9 = (bf16[256,256]{1,0:T(8,128)(2,1)S(1)}, bf16[256,256]{1,0:T(8,128)(2,1)S(1)}, u32[]{:S(2)}, u32[]{:S(2)}) collective-permute-start(bf16[256,256]{1,0:T(8,128)(2,1)S(1)} %get-tuple-element.59), channel_id=1, source_target_pairs={{0,1},{1,2},{2,3},{3,0},{4,5},{5,6},{6,7},{7,4},{8,9},{9,10},{10,1... | collective-permute-start | bytes 393224 | tf_op jit(solution)/shard_map/ppermute | solution.py:337
  88.2 7.3 %collective-permute-start.17 = (f32[256,256]{1,0:T(8,128)S(1)}, f32[256,256]{1,0:T(8,128)S(1)}, u32[]{:S(2)}, u32[]{:S(2)}) collective-permute-start(f32[256,256]{1,0:T(8,128)S(1)} %convolution_bitcast_fusion), channel_id=1, source_target_pairs={{0,4},{4,0},{8,12},{12,8},{16,20},{20,16},{24,28},{28,24},{32,36},... | collective-permute-start | bytes 786440 | tf_op jit(solution)/shard_map/ppermute | solution.py:397
  89.7 19.3 %all-to-all-start.1 = ((bf16[16,96,256]{2,1,0:T(8,128)(2,1)}), bf16[16,96,256]{2,1,0:T(8,128)(2,1)S(1)}, u32[]{:S(2)}, u32[]{:S(2)}) async-start(bf16[16,96,256]{2,1,0:T(8,128)(2,1)} %bitcast.2), calls=%async_computation.1 | async-start | bytes 1572864 | tf_op jit(solution)/shard_map/all_to_all | solution.py:386
  95.6 6.8 %collective-permute-start.18 = (bf16[256,256]{1,0:T(8,128)(2,1)S(1)}, bf16[256,256]{1,0:T(8,128)(2,1)S(1)}, u32[]{:S(2)}, u32[]{:S(2)}) collective-permute-start(bf16[256,256]{1,0:T(8,128)(2,1)S(1)} %get-tuple-element.57), channel_id=1, source_target_pairs={{0,1},{1,2},{2,3},{3,0},{4,5},{5,6},{6,7},{7,4},{8,9},{9,10},{10,1... | collective-permute-start | bytes 393224 | tf_op jit(solution)/shard_map/ppermute | solution.py:337
  96.5 8.8 %collective-permute-start.19 = (bf16[256,256]{1,0:T(8,128)(2,1)S(1)}, bf16[256,256]{1,0:T(8,128)(2,1)S(1)}, u32[]{:S(2)}, u32[]{:S(2)}) collective-permute-start(bf16[256,256]{1,0:T(8,128)(2,1)S(1)} %get-tuple-element.57), channel_id=1, source_target_pairs={{0,2},{1,3},{2,0},{3,1},{4,6},{5,7},{6,4},{7,5},{8,10},{9,11},{10,... | collective-permute-start | bytes 393224 | tf_op jit(solution)/shard_map/ppermute | solution.py:337
  109.0 17.6 %all-to-all-start.3 = ((bf16[16,96,256]{2,1,0:T(8,128)(2,1)}), bf16[16,96,256]{2,1,0:T(8,128)(2,1)S(1)}, u32[]{:S(2)}, u32[]{:S(2)}) async-start(bf16[16,96,256]{2,1,0:T(8,128)(2,1)} %bitcast.5), calls=%async_computation.3 | async-start | bytes 1572864 | tf_op jit(solution)/shard_map/all_to_all | solution.py:386
  113.8 14.8 %collective-permute-start.14 = (bf16[8,96,256]{2,1,0:T(8,128)(2,1)S(1)}, bf16[8,96,256]{2,1,0:T(8,128)(2,1)S(1)}, u32[]{:S(2)}, u32[]{:S(2)}) collective-permute-start(bf16[8,96,256]{2,1,0:T(8,128)(2,1)S(1)} %get-tuple-element.63.refs_1_), channel_id=1, source_target_pairs={{0,3},{1,0},{2,1},{3,2},{4,7},{5,4},{6,5},{7,6},{8,11},{9,8},{10,9... | collective-permute-start | bytes 1179656 | tf_op jit(solution)/shard_map/ppermute | solution.py:337
  116.3 13.7 %collective-permute-start.12 = (bf16[8,96,256]{2,1,0:T(8,128)(2,1)S(1)}, bf16[8,96,256]{2,1,0:T(8,128)(2,1)S(1)}, u32[]{:S(2)}, u32[]{:S(2)}) collective-permute-start(bf16[8,96,256]{2,1,0:T(8,128)(2,1)S(1)} %get-tuple-element.64.refs_0_), channel_id=1, source_target_pairs={{0,1},{1,2},{2,3},{3,0},{4,5},{5,6},{6,7},{7,4},{8,9},{9,10},{10,1... | collective-permute-start | bytes 1179656 | tf_op jit(solution)/shard_map/ppermute | solution.py:337
  116.3 18.1 %collective-permute-start.26 = (bf16[8,96,256]{2,1,0:T(8,128)(2,1)S(1)}, bf16[8,96,256]{2,1,0:T(8,128)(2,1)S(1)}, u32[]{:S(2)}, u32[]{:S(2)}) collective-permute-start(bf16[8,96,256]{2,1,0:T(8,128)(2,1)S(1)} %get-tuple-element.64.refs_0_), channel_id=1, source_target_pairs={{0,3},{1,0},{2,1},{3,2},{4,7},{5,4},{6,5},{7,6},{8,11},{9,8},{10,9... | collective-permute-start | bytes 1179656 | tf_op jit(solution)/shard_map/ppermute | solution.py:337
  119.5 25.9 %collective-permute-start.28 = (bf16[8,96,256]{2,1,0:T(8,128)(2,1)S(1)}, bf16[8,96,256]{2,1,0:T(8,128)(2,1)S(1)}, u32[]{:S(2)}, u32[]{:S(2)}) collective-permute-start(bf16[8,96,256]{2,1,0:T(8,128)(2,1)S(1)} %get-tuple-element.63.refs_1_), channel_id=1, source_target_pairs={{0,1},{1,2},{2,3},{3,0},{4,5},{5,6},{6,7},{7,4},{8,9},{9,10},{10,1... | collective-permute-start | bytes 1179656 | tf_op jit(solution)/shard_map/ppermute | solution.py:337
  126.6 19.9 %collective-permute-start.22 = (bf16[8,96,256]{2,1,0:T(8,128)(2,1)S(1)}, bf16[8,96,256]{2,1,0:T(8,128)(2,1)S(1)}, u32[]{:S(2)}, u32[]{:S(2)}) collective-permute-start(bf16[8,96,256]{2,1,0:T(8,128)(2,1)S(1)} %get-tuple-element.62.refs_2_), channel_id=1, source_target_pairs={{0,1},{1,2},{2,3},{3,0},{4,5},{5,6},{6,7},{7,4},{8,9},{9,10},{10,1... | collective-permute-start | bytes 1179656 | tf_op jit(solution)/shard_map/ppermute | solution.py:337
  128.6 20.4 %collective-permute-start.24 = (bf16[8,96,256]{2,1,0:T(8,128)(2,1)S(1)}, bf16[8,96,256]{2,1,0:T(8,128)(2,1)S(1)}, u32[]{:S(2)}, u32[]{:S(2)}) collective-permute-start(bf16[8,96,256]{2,1,0:T(8,128)(2,1)S(1)} %get-tuple-element.61.refs_3_), channel_id=1, source_target_pairs={{0,3},{1,0},{2,1},{3,2},{4,7},{5,4},{6,5},{7,6},{8,11},{9,8},{10,9... | collective-permute-start | bytes 1179656 | tf_op jit(solution)/shard_map/ppermute | solution.py:337
  129.9 21.3 %collective-permute-start.27 = (bf16[8,96,256]{2,1,0:T(8,128)(2,1)S(1)}, bf16[8,96,256]{2,1,0:T(8,128)(2,1)S(1)}, u32[]{:S(2)}, u32[]{:S(2)}) collective-permute-start(bf16[8,96,256]{2,1,0:T(8,128)(2,1)S(1)} %get-tuple-element.62.refs_2_), channel_id=1, source_target_pairs={{0,3},{1,0},{2,1},{3,2},{4,7},{5,4},{6,5},{7,6},{8,11},{9,8},{10,9... | collective-permute-start | bytes 1179656 | tf_op jit(solution)/shard_map/ppermute | solution.py:337
  134.3 20.5 %collective-permute-start.29 = (bf16[8,96,256]{2,1,0:T(8,128)(2,1)S(1)}, bf16[8,96,256]{2,1,0:T(8,128)(2,1)S(1)}, u32[]{:S(2)}, u32[]{:S(2)}) collective-permute-start(bf16[8,96,256]{2,1,0:T(8,128)(2,1)S(1)} %get-tuple-element.61.refs_3_), channel_id=1, source_target_pairs={{0,1},{1,2},{2,3},{3,0},{4,5},{5,6},{6,7},{7,4},{8,9},{9,10},{10,1... | collective-permute-start | bytes 1179656 | tf_op jit(solution)/shard_map/ppermute | solution.py:337
  145.4 19.9 %collective-permute-start.13 = (bf16[8,96,256]{2,1,0:T(8,128)(2,1)S(1)}, bf16[8,96,256]{2,1,0:T(8,128)(2,1)S(1)}, u32[]{:S(2)}, u32[]{:S(2)}) collective-permute-start(bf16[8,96,256]{2,1,0:T(8,128)(2,1)S(1)} %collective-permute-done.12.refs_4_), channel_id=1, source_target_pairs={{0,1},{1,2},{2,3},{3,0},{4,5},{5,6},{6,7},{7,4},{8,9},{9,10},{10,1... | collective-permute-start | bytes 1179656 | tf_op jit(solution)/shard_map/ppermute | solution.py:337
  146.5 18.9 %collective-permute-start.21 = (bf16[8,96,256]{2,1,0:T(8,128)(2,1)S(1)}, bf16[8,96,256]{2,1,0:T(8,128)(2,1)S(1)}, u32[]{:S(2)}, u32[]{:S(2)}) collective-permute-start(bf16[8,96,256]{2,1,0:T(8,128)(2,1)S(1)} %collective-permute-done.14.refs_1_), channel_id=1, source_target_pairs={{0,3},{1,0},{2,1},{3,2},{4,7},{5,4},{6,5},{7,6},{8,11},{9,8},{10,9... | collective-permute-start | bytes 1179656 | tf_op jit(solution)/shard_map/ppermute | solution.py:337
  149.0 19.7 %collective-permute-start.23 = (bf16[8,96,256]{2,1,0:T(8,128)(2,1)S(1)}, bf16[8,96,256]{2,1,0:T(8,128)(2,1)S(1)}, u32[]{:S(2)}, u32[]{:S(2)}) collective-permute-start(bf16[8,96,256]{2,1,0:T(8,128)(2,1)S(1)} %collective-permute-done.22.refs_6_), channel_id=1, source_target_pairs={{0,1},{1,2},{2,3},{3,0},{4,5},{5,6},{6,7},{7,4},{8,9},{9,10},{10,1... | collective-permute-start | bytes 1179656 | tf_op jit(solution)/shard_map/ppermute | solution.py:337
  151.2 17.5 %collective-permute-start.25 = (bf16[8,96,256]{2,1,0:T(8,128)(2,1)S(1)}, bf16[8,96,256]{2,1,0:T(8,128)(2,1)S(1)}, u32[]{:S(2)}, u32[]{:S(2)}) collective-permute-start(bf16[8,96,256]{2,1,0:T(8,128)(2,1)S(1)} %collective-permute-done.24.refs_3_), channel_id=1, source_target_pairs={{0,3},{1,0},{2,1},{3,2},{4,7},{5,4},{6,5},{7,6},{8,11},{9,8},{10,9... | collective-permute-start | bytes 1179656 | tf_op jit(solution)/shard_map/ppermute | solution.py:337
  (9 other events, 51.9 us)

commit v8 on v6

--- a/solution.py
+++ b/solution.py
@@ -284,18 +284,22 @@
     ).astype(BF)
     for copy in keep:
         copy.wait()
-    for k, r in enumerate(turns):
-        for q in range(GRP):
-
-            @pl.when(lax.rem(quarter + r, GRP) == q)
-            def _():
-                for i in range(2):
+    stores = []
+    for i in range(2):
+        for k, r in enumerate(turns):
+            for q in range(GRP):
+
+                @pl.when(lax.rem(quarter + r, GRP) == q)
+                def _():
                     begin = i * width + k * rows
                     target[i, :, q * rows : (q + 1) * rows] = both[:, begin : begin + rows]
 
-    if last:
-        store = pltpu.make_async_copy(held, out, arrived.at[len(given) + 1])
-        store.start()
+        if last:
+            stores.append(
+                pltpu.make_async_copy(held.at[i], out.at[i], arrived.at[len(given) + 1 + i])
+            )
+            stores[-1].start()
+    for store in stores:
         store.wait()
 
 
@@ -321,7 +325,7 @@
             pltpu.VMEM((len(turns), groups, rows, 256), BF),
             pltpu.VMEM((2 * len(turns) * rows, virtuals), BF),
             pltpu.VMEM(shape if last else (2, 16, 128), BF),
-            pltpu.SemaphoreType.DMA((len(parts) + 2,)),
+            pltpu.SemaphoreType.DMA((len(parts) + 3,)),
         ],
         compiler_params=pltpu.CompilerParams(vmem_limit_bytes=24 * MIB),
         cost_estimate=pl.CostEstimate(

time: 175 us -> 175 us (level)
  transfers between devices with their start and end apart: 34 -> 34, of which waited for: 20 -> 19; matrix products, arithmetic and copies ran while one was open for 5% -> 5% of each run, Pallas kernels for 13% -> 14%
where the time goes in v8:
time: 175 us
  starting transfers between devices  66.8 us (38%)
  waiting for transfers between devices  54.4 us (31%)
  Pallas kernels  38.3 us (22%)
  local copies, waits for them, and re-layouts  6.38 us (4%)
  other arithmetic  4.83 us (3%)
  matrix products  3.48 us (2%)
    ppermute x28, starting transfers between devices, shift(): return lax.ppermute(value, 'grp', [(j, (j + by) % GRP) for j in range(GRP)])  43 us
    ppermute x28, waiting for transfers between devices, shift(): return lax.ppermute(value, 'grp', [(j, (j + by) % GRP) for j in range(GRP)])  33.8 us
    pallas_call x3, Pallas kernels, add_columns(): pl.pallas_call(functools.partial(columns_kernel, quarter_shells=nus // sh...  25.1 us
    all_to_all x4, starting transfers between devices, exchange(): lax.all_to_all(value, 'aux', split_axis=0, concat_axis=0, axis_index_grou...  23.6 us
    all_to_all x4, waiting for transfers between devices, exchange(): lax.all_to_all(value, 'aux', split_axis=0, concat_axis=0, axis_index_grou...  19.4 us
    pallas_call x1, Pallas kernels, partial_pieces(): pl.pallas_call(functools.partial(far_kernel, groups=groups, quarter_shell...  6.94 us
    pallas_call x1, Pallas kernels, partial_pieces(): pl.pallas_call(functools.partial(near_kernel, slots=slots, groups=groups)...  6.35 us
    unnamed x15, local copies, waits for them, and re-layouts  5.68 us
  transfers between devices with their start and end apart: 34, of which 19 were waited for; matrix products, arithmetic and copies ran while one was open for 5% of the time, Pallas kernels for 14%

profile of v8, /device:TPU:0, one launch (start us, length us, event | category | flops | bytes accessed | tf_op | source)
XLA Modules:
  0.0 174.7 jit_solution(18143676871610804505)
XLA Ops:
  2.1 6.9 %far_rows.1 = (bf16[288,512]{1,0:T(8,128)(2,1)S(1)}, bf16[8,96,256]{2,1,0:T(8,128)(2,1)S(1)}, bf16[8,96,256]{2,1,0:T(8,128)(2,1)S(1)}, bf16[8,96,256]{2,1,0:T(8,128)(2,1)S(1)}, bf16[8,96,256]{2,1,0:T(8,128)(2,1)S(1)}) custom-call(s32[8,4]{1,0:T(8,128)S(1)} %copy.23.blocks, s32[128]{0:T(128)S(1)} %copy-done.2, bf16[2,4352]{1,0:T(2,128)(2,1)S(1)} %copy-done.4, ...), custom_call_target="tpu_custom_call" | custom-call | flops 1073741824 | bytes 10485760 | tf_op jit(solution)/shard_map/far_rows/pallas_call | solution.py:182
  10.7 1.7 collective-permute-start.1
  14.4 6.4 %near_rows.1 = (bf16[16,96,256]{2,1,0:T(8,128)(2,1)S(1)}, bf16[8,96,256]{2,1,0:T(8,128)(2,1)S(1)}, bf16[8,96,256]{2,1,0:T(8,128)(2,1)S(1)}, bf16[8,96,256]{2,1,0...) custom-call(s32[8,4]{1,0:T(8,128)S(1)} %copy.23.blocks, ...), custom_call_target="tpu_custom_call" | custom-call | flops 2147483648 | bytes 8388608 | tf_op jit(solution)/shard_map/near_rows/pallas_call | solution.py:203
  24.3 1.7 collective-permute-start.6
  26.1 1.7 collective-permute-start.7
  28.0 3.2 %collective-permute-done.4 = bf16[8,96,256]{2,1,0:T(8,128)(2,1)S(1)} collective-permute-done((bf16[8,96,256]{2,1,0:T(8,128)(2,1)S(1)}, bf16[8,96,256]{2,1,0:T(8,128)(2,1)S(1)}, u32[]{:S(2)}, u32[]{:S(2)}) %collective-permute-start.4) | collective-permute-done | bytes 393248 | tf_op jit(solution)/shard_map/ppermute | solution.py:341
  33.1 6.2 %collective-permute-done.5 = bf16[8,96,256]{2,1,0:T(8,128)(2,1)S(1)} collective-permute-done((bf16[8,96,256]{2,1,0:T(8,128)(2,1)S(1)}, bf16[8,96,256]{2,1,0:T(8,128)(2,1)S(1)}, u32[]{:S(2)}, u32[]{:S(2)}) %collective-permute-start.5) | collective-permute-done | bytes 393248 | tf_op jit(solution)/shard_map/ppermute | solution.py:341
  41.1 1.7 collective-permute-start.15
  42.9 5.2 %collective-permute-done.7 = bf16[8,96,256]{2,1,0:T(8,128)(2,1)S(1)} collective-permute-done((bf16[8,96,256]{2,1,0:T(8,128)(2,1)S(1)}, bf16[8,96,256]{2,1,0:T(8,128)(2,1)S(1)}, u32[]{:S(2)}, u32[]{:S(2)}) %collective-permute-start.7) | collective-permute-done | bytes 393248 | tf_op jit(solution)/shard_map/ppermute | solution.py:341
  49.4 8.1 %all-to-all-start = ((bf16[16,96,256]{2,1,0:T(8,128)(2,1)}), bf16[16,96,256]{2,1,0:T(8,128)(2,1)S(1)}, u32[]{:S(2)}, u32[]{:S(2)}) async-start(bf16[16,96,256]{2,1,0:T(8,128)(2,1)} %pad_maximum_fusion.2), calls=%async_computation | async-start | bytes 1572864 | tf_op jit(solution)/shard_map/all_to_all | solution.py:390
  58.0 5.4 %collective-permute-done.14 = bf16[16,96,256]{2,1,0:T(8,128)(2,1)} collective-permute-done((bf16[16,96,256]{2,1,0:T(8,128)(2,1)S(1)}, bf16[16,96,256]{2,1,0:T(8,128)(2,1)}, u32[]{:S(2)}, u32[]{:S(2)}) %collective-permute-start.14) | collective-permute-done | bytes 786464 | tf_op jit(solution)/shard_map/ppermute | solution.py:341
  63.5 2.6 %add_convert_fusion = bf16[16,96,256]{2,1,0:T(8,128)(2,1)} fusion(bf16[16,96,256]{2,1,0:T(8,128)(2,1)} %collective-permute-done.15, bf16[16,96,256]{2,1,0:T(8,128)(2,1)} %collective-permute-done.14, bf16[16,96,256]{2,1,0:T(8,128)(2,1)S(1)} %get-tuple-element.51), kind=kLoop, calls=%fused_computation.2 | loop fusion | flops 2359296 | bytes 3145728 | tf_op jit(solution)/shard_map/convert_element_type | solution.py:345
  66.2 3.3 %all-to-all-done = bf16[16,96,256]{2,1,0:T(8,128)(2,1)S(1)} async-done(((bf16[16,96,256]{2,1,0:T(8,128)(2,1)}), bf16[16,96,256]{2,1,0:T(8,128)(2,1)S(1)}, u32[]{:S(2)}, u32[]{:S(2)}) %all-to-all-start) | async-done | bytes 786464 | tf_op jit(solution)/shard_map/all_to_all | solution.py:390
  69.4 4.9 %all-to-all-start.2 = ((bf16[16,96,256]{2,1,0:T(8,128)(2,1)}), bf16[16,96,256]{2,1,0:T(8,128)(2,1)S(1)}, u32[]{:S(2)}, u32[]{:S(2)}) async-start(bf16[16,96,256]{2,1,0:T(8,128)(2,1)} %add_convert_fusion), calls=%async_computation.2 | async-start | bytes 1572864 | tf_op jit(solution)/shard_map/all_to_all | solution.py:390
  76.4 2.8 %collective-permute-start.10 = (bf16[256,256]{1,0:T(8,128)(2,1)S(1)}, bf16[256,256]{1,0:T(8,128)(2,1)S(1)}, u32[]{:S(2)}, u32[]{:S(2)}) collective-permute-start(bf16[256,256]{1,0:T(8,128)(2,1)S(1)} %get-tuple-element.61), channel_id=1, source_target_pairs={{0,2},{1,3},{2,0},{3,1},{4,6},{5,7},{6,4},{7,5},{8,10},{9,11},{10,... | collective-permute-start | bytes 393224 | tf_op jit(solution)/shard_map/ppermute | solution.py:341
  81.3 6.5 %all-to-all-done.2 = bf16[16,96,256]{2,1,0:T(8,128)(2,1)S(1)} async-done(((bf16[16,96,256]{2,1,0:T(8,128)(2,1)}), bf16[16,96,256]{2,1,0:T(8,128)(2,1)S(1)}, u32[]{:S(2)}, u32[]{:S(2)}) %all-to-all-start.2) | async-done | bytes 786464 | tf_op jit(solution)/shard_map/all_to_all | solution.py:390
  89.7 5.8 %all-to-all-start.1 = ((bf16[16,96,256]{2,1,0:T(8,128)(2,1)}), bf16[16,96,256]{2,1,0:T(8,128)(2,1)S(1)}, u32[]{:S(2)}, u32[]{:S(2)}) async-start(bf16[16,96,256]{2,1,0:T(8,128)(2,1)} %bitcast.2), calls=%async_computation.1 | async-start | bytes 1572864 | tf_op jit(solution)/shard_map/all_to_all | solution.py:390
  96.5 2.9 %collective-permute-start.18 = (bf16[256,256]{1,0:T(8,128)(2,1)S(1)}, bf16[256,256]{1,0:T(8,128)(2,1)S(1)}, u32[]{:S(2)}, u32[]{:S(2)}) collective-permute-start(bf16[256,256]{1,0:T(8,128)(2,1)S(1)} %get-tuple-element.59), channel_id=1, source_target_pairs={{0,2},{1,3},{2,0},{3,1},{4,6},{5,7},{6,4},{7,5},{8,10},{9,11},{10,... | collective-permute-start | bytes 393224 | tf_op jit(solution)/shard_map/ppermute | solution.py:341
  100.5 1.8 %collective-permute-done.17 = bf16[256,256]{1,0:T(8,128)(2,1)S(1)} collective-permute-done((bf16[256,256]{1,0:T(8,128)(2,1)S(1)}, bf16[256,256]{1,0:T(8,128)(2,1)S(1)}, u32[]{:S(2)}, u32[]{:S(2)}) %collective-permute-start.17) | collective-permute-done | bytes 131104 | tf_op jit(solution)/shard_map/ppermute | solution.py:341
  102.3 3.1 %collective-permute-done.18 = bf16[256,256]{1,0:T(8,128)(2,1)S(1)} collective-permute-done((bf16[256,256]{1,0:T(8,128)(2,1)S(1)}, bf16[256,256]{1,0:T(8,128)(2,1)S(1)}, u32[]{:S(2)}, u32[]{:S(2)}) %collective-permute-start.18) | collective-permute-done | bytes 131104 | tf_op jit(solution)/shard_map/ppermute | solution.py:341
  106.8 2.2 %all-to-all-done.1 = bf16[16,96,256]{2,1,0:T(8,128)(2,1)S(1)} async-done(((bf16[16,96,256]{2,1,0:T(8,128)(2,1)}), bf16[16,96,256]{2,1,0:T(8,128)(2,1)S(1)}, u32[]{:S(2)}, u32[]{:S(2)}) %all-to-all-start.1) | async-done | bytes 786464 | tf_op jit(solution)/shard_map/all_to_all | solution.py:390
  109.0 4.8 %all-to-all-start.3 = ((bf16[16,96,256]{2,1,0:T(8,128)(2,1)}), bf16[16,96,256]{2,1,0:T(8,128)(2,1)S(1)}, u32[]{:S(2)}, u32[]{:S(2)}) async-start(bf16[16,96,256]{2,1,0:T(8,128)(2,1)} %bitcast.5), calls=%async_computation.3 | async-start | bytes 1572864 | tf_op jit(solution)/shard_map/all_to_all | solution.py:390
  115.0 2.1 %collective-permute-start.13 = (bf16[8,96,256]{2,1,0:T(8,128)(2,1)S(1)}, bf16[8,96,256]{2,1,0:T(8,128)(2,1)S(1)}, u32[]{:S(2)}, u32[]{:S(2)}) collective-permute-start(bf16[8,96,256]{2,1,0:T(8,128)(2,1)S(1)} %get-tuple-element.65.refs_1_), channel_id=1, source_target_pairs={{0,3},{1,0},{2,1},{3,2},{4,7},{5,4},{6,5},{7,6},{8,11},{9,8},{10,9... | collective-permute-start | bytes 1179656 | tf_op jit(solution)/shard_map/ppermute | solution.py:341
  119.1 7.5 %all-to-all-done.3 = bf16[16,96,256]{2,1,0:T(8,128)(2,1)S(1)} async-done(((bf16[16,96,256]{2,1,0:T(8,128)(2,1)}), bf16[16,96,256]{2,1,0:T(8,128)(2,1)S(1)}, u32[]{:S(2)}, u32[]{:S(2)}) %all-to-all-start.3) | async-done | bytes 786464 | tf_op jit(solution)/shard_map/all_to_all | solution.py:390
  126.6 2.0 %collective-permute-start.22 = (bf16[8,96,256]{2,1,0:T(8,128)(2,1)S(1)}, bf16[8,96,256]{2,1,0:T(8,128)(2,1)S(1)}, u32[]{:S(2)}, u32[]{:S(2)}) collective-permute-start(bf16[8,96,256]{2,1,0:T(8,128)(2,1)S(1)} %get-tuple-element.64.refs_2_), channel_id=1, source_target_pairs={{0,1},{1,2},{2,3},{3,0},{4,5},{5,6},{6,7},{7,4},{8,9},{9,10},{10,1... | collective-permute-start | bytes 1179656 | tf_op jit(solution)/shard_map/ppermute | solution.py:341
  131.4 4.1 %collective-permute-done.26.refs_0_ = bf16[8,96,256]{2,1,0:T(8,128)(2,1)S(1)} collective-permute-done((bf16[8,96,256]{2,1,0:T(8,128)(2,1)S(1)}, bf16[8,96,256]{2,1,0:T(8,128)(2,1)S(1)}, u32[]{:S(2)}, u32[]{:S(2)}) %collective-permute-start.26) | collective-permute-done | bytes 393248 | tf_op jit(solution)/shard_map/ppermute | solution.py:341
  136.3 3.5 %copy-done.1 = bf16[1088,4096]{1,0:T(8,128)(2,1)S(1)} copy-done((bf16[1088,4096]{1,0:T(8,128)(2,1)S(1)}, bf16[1088,4096]{1,0:T(8,128)(2,1)}, u32[]{:S(2)}) %copy-start.1) | copy-done | bytes 8912920
  139.8 6.6 %add_columns.3.refs_8_ = bf16[2,1088,384]{2,1,0:T(8,128)(2,1)S(1)} custom-call(s32[8,4]{1,0:T(8,128)S(1)} %copy.23.blocks, s32[128]{0:T(128)S(1)} %copy-done.3, bf16[1088,4096]{1,0:T(8,128)(2,1)S(1)} %copy-done.1, bf16[8,96,256]{2,1,0:T(8,128)(2,1)S(1)} %get-tuple-element.66.refs_0_, bf16[8,96,256]{2,1,0:T(8,128)(2,1)S(1)} %get-tuple-element.65.refs_1_, ...), custom_call_target="tpu_custom_call" | custom-call | flops 1711276032 | bytes 12582912 | tf_op jit(solution)/shard_map/add_columns/pallas_call | solution.py:313
  146.5 2.0 %collective-permute-start.20 = (bf16[8,96,256]{2,1,0:T(8,128)(2,1)S(1)}, bf16[8,96,256]{2,1,0:T(8,128)(2,1)S(1)}, u32[]{:S(2)}, u32[]{:S(2)}) collective-permute-start(bf16[8,96,256]{2,1,0:T(8,128)(2,1)S(1)} %collective-permute-done.12.refs_4_), channel_id=1, source_target_pairs={{0,1},{1,2},{2,3},{3,0},{4,5},{5,6},{6,7},{7,4},{8,9},{9,10},{10,1... | collective-permute-start | bytes 1179656 | tf_op jit(solution)/shard_map/ppermute | solution.py:341
  152.4 3.3 %collective-permute-start.25 = (bf16[8,96,256]{2,1,0:T(8,128)(2,1)S(1)}, bf16[8,96,256]{2,1,0:T(8,128)(2,1)S(1)}, u32[]{:S(2)}, u32[]{:S(2)}) collective-permute-start(bf16[8,96,256]{2,1,0:T(8,128)(2,1)S(1)} %collective-permute-done.24.refs_3_), channel_id=1, source_target_pairs={{0,3},{1,0},{2,1},{3,2},{4,7},{5,4},{6,5},{7,6},{8,11},{9,8},{10,9... | collective-permute-start | bytes 1179656 | tf_op jit(solution)/shard_map/ppermute | solution.py:341
  155.6 10.6 %add_columns.4.refs_4_ = bf16[2,1088,384]{2,1,0:T(8,128)(2,1)S(1)} custom-call(s32[8,4]{1,0:T(8,128)S(1)} %copy.23.blocks, s32[128]{0:T(128)S(1)} %copy-done.3, bf16[1088,4096]{1,0:T(8,128)(2,1)S(1)} %copy-done.1, bf16[8,96,256]{2,1,0:T(8,128)(2,1)S(1)} %collective-permute-done.26.refs_0_, bf16[8,96,256]{2,1,0:T(8,128)(2,1)S(1)} %collective-permute-done.13.refs_1_, ...), custom_call_target="tpu_custom_call" | custom-call | flops 3422552064 | bytes 12582912 | tf_op jit(solution)/shard_map/add_columns/pallas_call | solution.py:313
  166.7 7.8 %add_columns.5 = bf16[2,1088,384]{2,1,0:T(8,128)(2,1)} custom-call(s32[8,4]{1,0:T(8,128)S(1)} %copy.23.blocks, s32[128]{0:T(128)S(1)} %copy-done.3, bf16[1088,4096]{1,0:T(8,128)(2,1)S(1)} %copy-done.1, bf16[8,96,256]{2,1,0:T(8,128)(2,1)S(1)} %collective-permute-done.20.refs_0_, bf16[8,96,256]{2,1,0:T(8,128)(2,1)S(1)} %collective-permute-done.21.refs_1_, ...), custom_call_target="tpu_custom_call" | custom-call | flops 1711276032 | bytes 12582912 | tf_op jit(solution)/shard_map/add_columns/pallas_call | solution.py:313
  (85 shorter events, 35.8 us)
Async XLA Ops:
  9.1 13.3 %collective-permute-start = (bf16[8,96,256]{2,1,0:T(8,128)(2,1)S(1)}, bf16[8,96,256]{2,1,0:T(8,128)(2,1)S(1)}, u32[]{:S(2)}, u32[]{:S(2)}) collective-permute-start(bf16[8,96,256]{2,1,0:T(8,128)(2,1)S(1)} %get-tuple-element.36), channel_id=1, source_target_pairs={{0,1},{1,2},{2,3},{3,0},{4,5},{5,6},{6,7},{7,4},{8,9},{9,10},{10,1... | collective-permute-start | bytes 1179656 | tf_op jit(solution)/shard_map/ppermute | solution.py:341
  10.7 12.0 %collective-permute-start.1 = (bf16[8,96,256]{2,1,0:T(8,128)(2,1)S(1)}, bf16[8,96,256]{2,1,0:T(8,128)(2,1)S(1)}, u32[]{:S(2)}, u32[]{:S(2)}) collective-permute-start(bf16[8,96,256]{2,1,0:T(8,128)(2,1)S(1)} %get-tuple-element.37), channel_id=1, source_target_pairs={{0,3},{1,0},{2,1},{3,2},{4,7},{5,4},{6,5},{7,6},{8,11},{9,8},{10,9... | collective-permute-start | bytes 1179656 | tf_op jit(solution)/shard_map/ppermute | solution.py:341
  12.4 18.8 %collective-permute-start.4 = (bf16[8,96,256]{2,1,0:T(8,128)(2,1)S(1)}, bf16[8,96,256]{2,1,0:T(8,128)(2,1)S(1)}, u32[]{:S(2)}, u32[]{:S(2)}) collective-permute-start(bf16[8,96,256]{2,1,0:T(8,128)(2,1)S(1)} %get-tuple-element.44), channel_id=1, source_target_pairs={{0,3},{1,0},{2,1},{3,2},{4,7},{5,4},{6,5},{7,6},{8,11},{9,8},{10,9... | collective-permute-start | bytes 1179656 | tf_op jit(solution)/shard_map/ppermute | solution.py:341
  14.0 18.9 %collective-permute-start.3 = (bf16[8,96,256]{2,1,0:T(8,128)(2,1)S(1)}, bf16[8,96,256]{2,1,0:T(8,128)(2,1)S(1)}, u32[]{:S(2)}, u32[]{:S(2)}) collective-permute-start(bf16[8,96,256]{2,1,0:T(8,128)(2,1)S(1)} %get-tuple-element.40), channel_id=1, source_target_pairs={{0,1},{1,2},{2,3},{3,0},{4,5},{5,6},{6,7},{7,4},{8,9},{9,10},{10,1... | collective-permute-start | bytes 1179656 | tf_op jit(solution)/shard_map/ppermute | solution.py:341
  22.8 16.5 %collective-permute-start.5 = (bf16[8,96,256]{2,1,0:T(8,128)(2,1)S(1)}, bf16[8,96,256]{2,1,0:T(8,128)(2,1)S(1)}, u32[]{:S(2)}, u32[]{:S(2)}) collective-permute-start(bf16[8,96,256]{2,1,0:T(8,128)(2,1)S(1)} %get-tuple-element.45), channel_id=1, source_target_pairs={{0,1},{1,2},{2,3},{3,0},{4,5},{5,6},{6,7},{7,4},{8,9},{9,10},{10,1... | collective-permute-start | bytes 1179656 | tf_op jit(solution)/shard_map/ppermute | solution.py:341
  24.3 15.4 %collective-permute-start.6 = (bf16[8,96,256]{2,1,0:T(8,128)(2,1)S(1)}, bf16[8,96,256]{2,1,0:T(8,128)(2,1)S(1)}, u32[]{:S(2)}, u32[]{:S(2)}) collective-permute-start(bf16[8,96,256]{2,1,0:T(8,128)(2,1)S(1)} %get-tuple-element.46), channel_id=1, source_target_pairs={{0,3},{1,0},{2,1},{3,2},{4,7},{5,4},{6,5},{7,6},{8,11},{9,8},{10,9... | collective-permute-start | bytes 1179656 | tf_op jit(solution)/shard_map/ppermute | solution.py:341
  26.1 21.9 %collective-permute-start.7 = (bf16[8,96,256]{2,1,0:T(8,128)(2,1)S(1)}, bf16[8,96,256]{2,1,0:T(8,128)(2,1)S(1)}, u32[]{:S(2)}, u32[]{:S(2)}) collective-permute-start(bf16[8,96,256]{2,1,0:T(8,128)(2,1)S(1)} %add_convert_fusion.2), channel_id=1, source_target_pairs={{0,3},{1,0},{2,1},{3,2},{4,7},{5,4},{6,5},{7,6},{8,11},{9,8},{10,9... | collective-permute-start | bytes 1179656 | tf_op jit(solution)/shard_map/ppermute | solution.py:341
  31.2 16.9 %collective-permute-start.2 = (bf16[8,96,256]{2,1,0:T(8,128)(2,1)S(1)}, bf16[8,96,256]{2,1,0:T(8,128)(2,1)S(1)}, u32[]{:S(2)}, u32[]{:S(2)}) collective-permute-start(bf16[8,96,256]{2,1,0:T(8,128)(2,1)S(1)} %add_convert_fusion.6), channel_id=1, source_target_pairs={{0,1},{1,2},{2,3},{3,0},{4,5},{5,6},{6,7},{7,4},{8,9},{9,10},{10,1... | collective-permute-start | bytes 1179656 | tf_op jit(solution)/shard_map/ppermute | solution.py:341
  39.6 23.7 %collective-permute-start.14 = (bf16[16,96,256]{2,1,0:T(8,128)(2,1)S(1)}, bf16[16,96,256]{2,1,0:T(8,128)(2,1)}, u32[]{:S(2)}, u32[]{:S(2)}) collective-permute-start(bf16[16,96,256]{2,1,0:T(8,128)(2,1)S(1)} %pad_maximum_fusion), channel_id=1, source_target_pairs={{0,1},{1,2},{2,3},{3,0},{4,5},{5,6},{6,7},{7,4},{8,9},{9,10},{10,1... | collective-permute-start | bytes 2359304 | tf_op jit(solution)/shard_map/ppermute | solution.py:341
  41.1 22.4 %collective-permute-start.15 = (bf16[16,96,256]{2,1,0:T(8,128)(2,1)S(1)}, bf16[16,96,256]{2,1,0:T(8,128)(2,1)}, u32[]{:S(2)}, u32[]{:S(2)}) collective-permute-start(bf16[16,96,256]{2,1,0:T(8,128)(2,1)S(1)} %pad_maximum_fusion.1), channel_id=1, source_target_pairs={{0,3},{1,0},{2,1},{3,2},{4,7},{5,4},{6,5},{7,6},{8,11},{9,8},{10,9... | collective-permute-start | bytes 2359304 | tf_op jit(solution)/shard_map/ppermute | solution.py:341
  49.4 20.0 %all-to-all-start = ((bf16[16,96,256]{2,1,0:T(8,128)(2,1)}), bf16[16,96,256]{2,1,0:T(8,128)(2,1)S(1)}, u32[]{:S(2)}, u32[]{:S(2)}) async-start(bf16[16,96,256]{2,1,0:T(8,128)(2,1)} %pad_maximum_fusion.2), calls=%async_computation | async-start | bytes 1572864 | tf_op jit(solution)/shard_map/all_to_all | solution.py:390
  69.4 18.4 %all-to-all-start.2 = ((bf16[16,96,256]{2,1,0:T(8,128)(2,1)}), bf16[16,96,256]{2,1,0:T(8,128)(2,1)S(1)}, u32[]{:S(2)}, u32[]{:S(2)}) async-start(bf16[16,96,256]{2,1,0:T(8,128)(2,1)} %add_convert_fusion), calls=%async_computation.2 | async-start | bytes 1572864 | tf_op jit(solution)/shard_map/all_to_all | solution.py:390
  76.4 11.9 %collective-permute-start.10 = (bf16[256,256]{1,0:T(8,128)(2,1)S(1)}, bf16[256,256]{1,0:T(8,128)(2,1)S(1)}, u32[]{:S(2)}, u32[]{:S(2)}) collective-permute-start(bf16[256,256]{1,0:T(8,128)(2,1)S(1)} %get-tuple-element.61), channel_id=1, source_target_pairs={{0,2},{1,3},{2,0},{3,1},{4,6},{5,7},{6,4},{7,5},{8,10},{9,11},{10,... | collective-permute-start | bytes 393224 | tf_op jit(solution)/shard_map/ppermute | solution.py:341
  79.2 9.1 %collective-permute-start.11 = (bf16[256,256]{1,0:T(8,128)(2,1)S(1)}, bf16[256,256]{1,0:T(8,128)(2,1)S(1)}, u32[]{:S(2)}, u32[]{:S(2)}) collective-permute-start(bf16[256,256]{1,0:T(8,128)(2,1)S(1)} %get-tuple-element.61), channel_id=1, source_target_pairs={{0,3},{1,0},{2,1},{3,2},{4,7},{5,4},{6,5},{7,6},{8,11},{9,8},{10,9... | collective-permute-start | bytes 393224 | tf_op jit(solution)/shard_map/ppermute | solution.py:341
  80.7 7.6 %collective-permute-start.9 = (bf16[256,256]{1,0:T(8,128)(2,1)S(1)}, bf16[256,256]{1,0:T(8,128)(2,1)S(1)}, u32[]{:S(2)}, u32[]{:S(2)}) collective-permute-start(bf16[256,256]{1,0:T(8,128)(2,1)S(1)} %get-tuple-element.61), channel_id=1, source_target_pairs={{0,1},{1,2},{2,3},{3,0},{4,5},{5,6},{6,7},{7,4},{8,9},{9,10},{10,1... | collective-permute-start | bytes 393224 | tf_op jit(solution)/shard_map/ppermute | solution.py:341
  88.2 7.3 %collective-permute-start.16 = (f32[256,256]{1,0:T(8,128)S(1)}, f32[256,256]{1,0:T(8,128)S(1)}, u32[]{:S(2)}, u32[]{:S(2)}) collective-permute-start(f32[256,256]{1,0:T(8,128)S(1)} %convolution_bitcast_fusion), channel_id=1, source_target_pairs={{0,4},{4,0},{8,12},{12,8},{16,20},{20,16},{24,28},{28,24},{32,36},... | collective-permute-start | bytes 786440 | tf_op jit(solution)/shard_map/ppermute | solution.py:401
  89.7 19.3 %all-to-all-start.1 = ((bf16[16,96,256]{2,1,0:T(8,128)(2,1)}), bf16[16,96,256]{2,1,0:T(8,128)(2,1)S(1)}, u32[]{:S(2)}, u32[]{:S(2)}) async-start(bf16[16,96,256]{2,1,0:T(8,128)(2,1)} %bitcast.2), calls=%async_computation.1 | async-start | bytes 1572864 | tf_op jit(solution)/shard_map/all_to_all | solution.py:390
  95.6 6.8 %collective-permute-start.17 = (bf16[256,256]{1,0:T(8,128)(2,1)S(1)}, bf16[256,256]{1,0:T(8,128)(2,1)S(1)}, u32[]{:S(2)}, u32[]{:S(2)}) collective-permute-start(bf16[256,256]{1,0:T(8,128)(2,1)S(1)} %get-tuple-element.59), channel_id=1, source_target_pairs={{0,1},{1,2},{2,3},{3,0},{4,5},{5,6},{6,7},{7,4},{8,9},{9,10},{10,1... | collective-permute-start | bytes 393224 | tf_op jit(solution)/shard_map/ppermute | solution.py:341
  96.5 8.8 %collective-permute-start.18 = (bf16[256,256]{1,0:T(8,128)(2,1)S(1)}, bf16[256,256]{1,0:T(8,128)(2,1)S(1)}, u32[]{:S(2)}, u32[]{:S(2)}) collective-permute-start(bf16[256,256]{1,0:T(8,128)(2,1)S(1)} %get-tuple-element.59), channel_id=1, source_target_pairs={{0,2},{1,3},{2,0},{3,1},{4,6},{5,7},{6,4},{7,5},{8,10},{9,11},{10,... | collective-permute-start | bytes 393224 | tf_op jit(solution)/shard_map/ppermute | solution.py:341
  109.0 17.6 %all-to-all-start.3 = ((bf16[16,96,256]{2,1,0:T(8,128)(2,1)}), bf16[16,96,256]{2,1,0:T(8,128)(2,1)S(1)}, u32[]{:S(2)}, u32[]{:S(2)}) async-start(bf16[16,96,256]{2,1,0:T(8,128)(2,1)} %bitcast.5), calls=%async_computation.3 | async-start | bytes 1572864 | tf_op jit(solution)/shard_map/all_to_all | solution.py:390
  113.8 14.8 %collective-permute-start.12 = (bf16[8,96,256]{2,1,0:T(8,128)(2,1)S(1)}, bf16[8,96,256]{2,1,0:T(8,128)(2,1)S(1)}, u32[]{:S(2)}, u32[]{:S(2)}) collective-permute-start(bf16[8,96,256]{2,1,0:T(8,128)(2,1)S(1)} %get-tuple-element.66.refs_0_), channel_id=1, source_target_pairs={{0,1},{1,2},{2,3},{3,0},{4,5},{5,6},{6,7},{7,4},{8,9},{9,10},{10,1... | collective-permute-start | bytes 1179656 | tf_op jit(solution)/shard_map/ppermute | solution.py:341
  115.0 14.9 %collective-permute-start.13 = (bf16[8,96,256]{2,1,0:T(8,128)(2,1)S(1)}, bf16[8,96,256]{2,1,0:T(8,128)(2,1)S(1)}, u32[]{:S(2)}, u32[]{:S(2)}) collective-permute-start(bf16[8,96,256]{2,1,0:T(8,128)(2,1)S(1)} %get-tuple-element.65.refs_1_), channel_id=1, source_target_pairs={{0,3},{1,0},{2,1},{3,2},{4,7},{5,4},{6,5},{7,6},{8,11},{9,8},{10,9... | collective-permute-start | bytes 1179656 | tf_op jit(solution)/shard_map/ppermute | solution.py:341
  117.1 18.4 %collective-permute-start.26 = (bf16[8,96,256]{2,1,0:T(8,128)(2,1)S(1)}, bf16[8,96,256]{2,1,0:T(8,128)(2,1)S(1)}, u32[]{:S(2)}, u32[]{:S(2)}) collective-permute-start(bf16[8,96,256]{2,1,0:T(8,128)(2,1)S(1)} %get-tuple-element.66.refs_0_), channel_id=1, source_target_pairs={{0,3},{1,0},{2,1},{3,2},{4,7},{5,4},{6,5},{7,6},{8,11},{9,8},{10,9... | collective-permute-start | bytes 1179656 | tf_op jit(solution)/shard_map/ppermute | solution.py:341
  118.3 28.1 %collective-permute-start.28 = (bf16[8,96,256]{2,1,0:T(8,128)(2,1)S(1)}, bf16[8,96,256]{2,1,0:T(8,128)(2,1)S(1)}, u32[]{:S(2)}, u32[]{:S(2)}) collective-permute-start(bf16[8,96,256]{2,1,0:T(8,128)(2,1)S(1)} %get-tuple-element.65.refs_1_), channel_id=1, source_target_pairs={{0,1},{1,2},{2,3},{3,0},{4,5},{5,6},{6,7},{7,4},{8,9},{9,10},{10,1... | collective-permute-start | bytes 1179656 | tf_op jit(solution)/shard_map/ppermute | solution.py:341
  126.6 21.8 %collective-permute-start.22 = (bf16[8,96,256]{2,1,0:T(8,128)(2,1)S(1)}, bf16[8,96,256]{2,1,0:T(8,128)(2,1)S(1)}, u32[]{:S(2)}, u32[]{:S(2)}) collective-permute-start(bf16[8,96,256]{2,1,0:T(8,128)(2,1)S(1)} %get-tuple-element.64.refs_2_), channel_id=1, source_target_pairs={{0,1},{1,2},{2,3},{3,0},{4,5},{5,6},{6,7},{7,4},{8,9},{9,10},{10,1... | collective-permute-start | bytes 1179656 | tf_op jit(solution)/shard_map/ppermute | solution.py:341
  128.6 21.2 %collective-permute-start.24 = (bf16[8,96,256]{2,1,0:T(8,128)(2,1)S(1)}, bf16[8,96,256]{2,1,0:T(8,128)(2,1)S(1)}, u32[]{:S(2)}, u32[]{:S(2)}) collective-permute-start(bf16[8,96,256]{2,1,0:T(8,128)(2,1)S(1)} %get-tuple-element.63.refs_3_), channel_id=1, source_target_pairs={{0,3},{1,0},{2,1},{3,2},{4,7},{5,4},{6,5},{7,6},{8,11},{9,8},{10,9... | collective-permute-start | bytes 1179656 | tf_op jit(solution)/shard_map/ppermute | solution.py:341
  129.9 22.4 %collective-permute-start.27 = (bf16[8,96,256]{2,1,0:T(8,128)(2,1)S(1)}, bf16[8,96,256]{2,1,0:T(8,128)(2,1)S(1)}, u32[]{:S(2)}, u32[]{:S(2)}) collective-permute-start(bf16[8,96,256]{2,1,0:T(8,128)(2,1)S(1)} %get-tuple-element.64.refs_2_), channel_id=1, source_target_pairs={{0,3},{1,0},{2,1},{3,2},{4,7},{5,4},{6,5},{7,6},{8,11},{9,8},{10,9... | collective-permute-start | bytes 1179656 | tf_op jit(solution)/shard_map/ppermute | solution.py:341
  135.5 20.1 %collective-permute-start.29 = (bf16[8,96,256]{2,1,0:T(8,128)(2,1)S(1)}, bf16[8,96,256]{2,1,0:T(8,128)(2,1)S(1)}, u32[]{:S(2)}, u32[]{:S(2)}) collective-permute-start(bf16[8,96,256]{2,1,0:T(8,128)(2,1)S(1)} %get-tuple-element.63.refs_3_), channel_id=1, source_target_pairs={{0,1},{1,2},{2,3},{3,0},{4,5},{5,6},{6,7},{7,4},{8,9},{9,10},{10,1... | collective-permute-start | bytes 1179656 | tf_op jit(solution)/shard_map/ppermute | solution.py:341
  146.5 19.8 %collective-permute-start.20 = (bf16[8,96,256]{2,1,0:T(8,128)(2,1)S(1)}, bf16[8,96,256]{2,1,0:T(8,128)(2,1)S(1)}, u32[]{:S(2)}, u32[]{:S(2)}) collective-permute-start(bf16[8,96,256]{2,1,0:T(8,128)(2,1)S(1)} %collective-permute-done.12.refs_4_), channel_id=1, source_target_pairs={{0,1},{1,2},{2,3},{3,0},{4,5},{5,6},{6,7},{7,4},{8,9},{9,10},{10,1... | collective-permute-start | bytes 1179656 | tf_op jit(solution)/shard_map/ppermute | solution.py:341
  148.5 17.8 %collective-permute-start.21 = (bf16[8,96,256]{2,1,0:T(8,128)(2,1)S(1)}, bf16[8,96,256]{2,1,0:T(8,128)(2,1)S(1)}, u32[]{:S(2)}, u32[]{:S(2)}) collective-permute-start(bf16[8,96,256]{2,1,0:T(8,128)(2,1)S(1)} %collective-permute-done.13.refs_1_), channel_id=1, source_target_pairs={{0,3},{1,0},{2,1},{3,2},{4,7},{5,4},{6,5},{7,6},{8,11},{9,8},{10,9... | collective-permute-start | bytes 1179656 | tf_op jit(solution)/shard_map/ppermute | solution.py:341
  149.8 16.6 %collective-permute-start.23 = (bf16[8,96,256]{2,1,0:T(8,128)(2,1)S(1)}, bf16[8,96,256]{2,1,0:T(8,128)(2,1)S(1)}, u32[]{:S(2)}, u32[]{:S(2)}) collective-permute-start(bf16[8,96,256]{2,1,0:T(8,128)(2,1)S(1)} %collective-permute-done.22.refs_6_), channel_id=1, source_target_pairs={{0,1},{1,2},{2,3},{3,0},{4,5},{5,6},{6,7},{7,4},{8,9},{9,10},{10,1... | collective-permute-start | bytes 1179656 | tf_op jit(solution)/shard_map/ppermute | solution.py:341
  152.4 14.4 %collective-permute-start.25 = (bf16[8,96,256]{2,1,0:T(8,128)(2,1)S(1)}, bf16[8,96,256]{2,1,0:T(8,128)(2,1)S(1)}, u32[]{:S(2)}, u32[]{:S(2)}) collective-permute-start(bf16[8,96,256]{2,1,0:T(8,128)(2,1)S(1)} %collective-permute-done.24.refs_3_), channel_id=1, source_target_pairs={{0,3},{1,0},{2,1},{3,2},{4,7},{5,4},{6,5},{7,6},{8,11},{9,8},{10,9... | collective-permute-start | bytes 1179656 | tf_op jit(solution)/shard_map/ppermute | solution.py:341
  (9 other events, 51.9 us)
